TPU v7x, 32 devices: a whole 2x2x4 slice. The times are simulated.
32 devices in a mesh: grp: 2 (over x), ctx: 4 (over y, core), fsdp: 4 (over z).
Axes of the slice: x: 2, y: 2, z: 4, core: 2. Of those that a mesh axis runs over, the one named last changes fastest.
Arguments:
- tokens: bfloat16 [8, 1024, 2048], P(('grp', 'fsdp'), 'ctx'), may hold values from -6 to 6
- places: int32 [8, 1024], P(('grp', 'fsdp')), may hold values from 0 to 1023, as said below
- segments: int32 [8, 1024], P(('grp', 'fsdp')), may hold values from 0 to 3, as said below
- routes: int32 [8, 1024, 8], P(('grp', 'fsdp'), 'ctx'), may hold values from 0 to 15, all different within a row; in each aligned block of 256 rows (0 to 255, 256 to 511, ..., all dimensions but the last counted through in order) at most 160 rows name the same one
- w_query: bfloat16 [2048, 4096], P(('ctx', 'fsdp')), may hold values from -0.125 to 0.125
- w_key: bfloat16 [2048, 512], P(('ctx', 'fsdp')), may hold values from -0.125 to 0.125
- w_value: bfloat16 [2048, 512], P(('ctx', 'fsdp')), may hold values from -0.125 to 0.125
- w_out: bfloat16 [4096, 2048], P(('ctx', 'fsdp')), may hold values from -0.25 to 0.25
- w_router: bfloat16 [2048, 16], P(('ctx', 'fsdp')), may hold values from -0.0625 to 0.0625
- w_gate: bfloat16 [16, 2048, 768], P(None, ('ctx', 'fsdp')), may hold values from -0.125 to 0.125
- w_up: bfloat16 [16, 2048, 768], P(None, ('ctx', 'fsdp')), may hold values from -0.125 to 0.125
- w_down: bfloat16 [16, 768, 2048], P(None, ('ctx', 'fsdp')), may hold values from -0.4375 to 0.4375
- gain_attn: float32 [2048], replicated, may hold values from 0.25 to 1.75
- gain_ffn: float32 [2048], replicated, may hold values from 0.25 to 1.75
- gain_query: float32 [128], replicated, may hold values from 0.25 to 1.75
- gain_key: float32 [128], replicated, may hold values from 0.25 to 1.75
- cotangent: bfloat16 [8, 1024, 2048], P(('grp', 'fsdp'), 'ctx'), may hold values from -6 to 6
Outputs:
- output: bfloat16 [8, 1024, 2048], P(('grp', 'fsdp'), 'ctx')
- grad_tokens: float32 [8, 1024, 2048], P(('grp', 'fsdp'), 'ctx')
- grad_query: float32 [2048, 4096], P(('ctx', 'fsdp'))
- grad_key: float32 [2048, 512], P(('ctx', 'fsdp'))
- grad_value: float32 [2048, 512], P(('ctx', 'fsdp'))
- grad_out: float32 [4096, 2048], P(('ctx', 'fsdp'))
- grad_router: float32 [2048, 16], P(('ctx', 'fsdp'))
- grad_gate: float32 [16, 2048, 768], P(None, ('ctx', 'fsdp'))
- grad_up: float32 [16, 2048, 768], P(None, ('ctx', 'fsdp'))
- grad_down: float32 [16, 768, 2048], P(None, ('ctx', 'fsdp'))
- grad_gain_attn: float32 [2048], replicated
- grad_gain_ffn: float32 [2048], replicated
- grad_gain_query: float32 [128], replicated
- grad_gain_key: float32 [128], replicated
Inputs may be any that keep to these rules, and one draw needn't show every extreme that they name: Each sequence of 1024 tokens is cut into 8 blocks of 128 positions; the c-th 256 stored tokens hold two whole blocks b and 7 - b, each in rising order; places of one sequence are a permutation of 0 to 1023. `segments`: document numbers never fall with the position given by places; each sequence has 4 documents, each of 200 positions or more. `routes`: among the 256 tokens of one device, no expert is named by more than 160 tokens.
All inputs are finite; a program needn't handle non-finite values.
Results may differ from a plain program's by a relative error of at most 0.023.
Values may be sent and summed in bfloat16 or wider, within the bound.
A program may use at most 448 MiB of HBM per device.

v0:
```python
import math

import jax
import jax.numpy as jnp
from jax import lax
from jax.sharding import PartitionSpec as P

EXP_BLOCK = 4
CAP = 160


epsilon = 1e-06


def normed(values, gain):
    return values * lax.rsqrt(jnp.mean(values * values, axis=-1, keepdims=True) + epsilon) * gain


def angles(place, width):
    steps = jnp.arange(width // 2).astype(jnp.float32)
    inverse = jnp.exp(steps * (-2.0 * math.log(1000000.0) / width))
    return place.astype(jnp.float32)[:, None] * inverse[None, :]


def rotate(values, angle):
    half = values.shape[-1] // 2
    cosine = jnp.cos(angle)[:, None, :]
    sine = jnp.sin(angle)[:, None, :]
    first = values[..., :half]
    second = values[..., half:]
    return jnp.concatenate(
        [first * cosine - second * sine, second * cosine + first * sine], axis=-1
    )


def head_prep(q_lin, k_lin, gain_query, gain_key, angle):
    count = q_lin.shape[0]
    width = gain_query.shape[0]
    query = rotate(normed(q_lin.reshape(count, -1, width), gain_query), angle)
    keyed = rotate(normed(k_lin.reshape(count, -1, width), gain_key), angle)
    return (query, keyed)


def expert_ahead(rows_in, full_gate, full_up, full_down):
    act_gate = jnp.einsum("bcd,bdf->bcf", rows_in, full_gate, preferred_element_type=jnp.float32)
    act_up = jnp.einsum("bcd,bdf->bcf", rows_in, full_up, preferred_element_type=jnp.float32)
    hidden = (jax.nn.silu(act_gate) * act_up).astype(jnp.bfloat16)
    made = jnp.einsum("bcf,bfd->bcd", hidden, full_down, preferred_element_type=jnp.float32).astype(
        jnp.bfloat16
    )
    return (act_gate, act_up, made)


def expert_behind(rows_in, act_gate, act_up, d_made, full_gate, full_up, full_down):
    sigmoid = jax.nn.sigmoid(act_gate)
    silu_gate = act_gate * sigmoid
    hidden = (silu_gate * act_up).astype(jnp.bfloat16)
    d_hidden = jnp.einsum("bcd,bfd->bcf", d_made, full_down, preferred_element_type=jnp.float32)
    d_gate_low = (d_hidden * act_up * (sigmoid * (1.0 + act_gate * (1.0 - sigmoid)))).astype(
        jnp.bfloat16
    )
    d_up_low = (d_hidden * silu_gate).astype(jnp.bfloat16)
    part_down = jnp.einsum("bcf,bcd->bfd", hidden, d_made, preferred_element_type=jnp.float32)
    part_gate = jnp.einsum("bcd,bcf->bdf", rows_in, d_gate_low, preferred_element_type=jnp.float32)
    part_up = jnp.einsum("bcd,bcf->bdf", rows_in, d_up_low, preferred_element_type=jnp.float32)
    d_rows = jnp.einsum(
        "bcf,bdf->bcd", d_gate_low, full_gate, preferred_element_type=jnp.float32
    ) + jnp.einsum("bcf,bdf->bcd", d_up_low, full_up, preferred_element_type=jnp.float32)
    return (d_rows.astype(jnp.bfloat16), part_gate, part_up, part_down)


def per_device(
    tokens,
    places,
    segments,
    routes,
    w_query,
    w_key,
    w_value,
    w_out,
    w_router,
    w_gate,
    w_up,
    w_down,
    gain_attn,
    gain_ffn,
    gain_query,
    gain_key,
    cotangent,
):
    count = tokens.shape[1]
    width = gain_query.shape[0]
    heads = w_query.shape[1] // width
    kv_heads = w_key.shape[1] // width
    group = heads // kv_heads
    experts = w_gate.shape[0]
    blocks = experts // EXP_BLOCK
    model_width = tokens.shape[2]
    hidden_width = w_gate.shape[2]
    scale = 1.0 / math.sqrt(width)
    route_ids = routes[0]
    first_row = lax.axis_index("ctx") * count
    key_place = places[0]
    key_segment = segments[0]
    own_place = lax.dynamic_slice_in_dim(key_place, first_row, count)
    own_segment = lax.dynamic_slice_in_dim(key_segment, first_row, count)
    allowed = (own_segment[:, None] == key_segment[None, :]) & (
        key_place[None, :] <= own_place[:, None]
    )
    angle = angles(own_place, width)
    resid = tokens[0].astype(jnp.float32)
    norm_one, back_one = jax.vjp(normed, resid, gain_attn)
    normed_one = norm_one.astype(jnp.bfloat16)
    full_query, full_key, full_value, full_out, full_router = (
        lax.all_gather(w_query, ("ctx", "fsdp"), axis=0, tiled=True),
        lax.all_gather(w_key, ("ctx", "fsdp"), axis=0, tiled=True),
        lax.all_gather(w_value, ("ctx", "fsdp"), axis=0, tiled=True),
        lax.all_gather(w_out, ("ctx", "fsdp"), axis=0, tiled=True),
        lax.all_gather(w_router, ("ctx", "fsdp"), axis=0, tiled=True),
    )
    q_lin = jnp.dot(normed_one, full_query, preferred_element_type=jnp.float32)
    k_lin = jnp.dot(normed_one, full_key, preferred_element_type=jnp.float32)
    v_lin = jnp.dot(normed_one, full_value, preferred_element_type=jnp.float32)
    (query, keyed), back_heads = jax.vjp(
        lambda first, second, third, fourth: head_prep(first, second, third, fourth, angle),
        q_lin,
        k_lin,
        gain_query,
        gain_key,
    )
    query_low = query.astype(jnp.bfloat16).reshape(count, kv_heads, group, width)
    keyed_low = keyed.astype(jnp.bfloat16)
    value_low = v_lin.astype(jnp.bfloat16).reshape(count, kv_heads, width)
    keys_all, values_all = (
        lax.all_gather(keyed_low, "ctx", axis=0, tiled=True),
        lax.all_gather(value_low, "ctx", axis=0, tiled=True),
    )
    scores = (
        jnp.einsum("ikgd,jkd->kgij", query_low, keys_all, preferred_element_type=jnp.float32)
        * scale
    )
    masked = jnp.where(allowed, scores, -1e30)
    row_max = jnp.max(masked, axis=-1, keepdims=True)
    expd = jnp.exp(masked - row_max)
    row_total = jnp.sum(expd, axis=-1, keepdims=True)
    log_total = row_max + jnp.log(row_total)
    probs_low = (expd / row_total).astype(jnp.bfloat16)
    mixed = jnp.einsum("kgij,jkd->ikgd", probs_low, values_all, preferred_element_type=jnp.float32)
    mixed_low = mixed.reshape(count, heads * width).astype(jnp.bfloat16)
    resid_one = resid + jnp.dot(mixed_low, full_out, preferred_element_type=jnp.float32)
    norm_two, back_two = jax.vjp(normed, resid_one, gain_ffn)
    normed_two = norm_two.astype(jnp.bfloat16)
    logits = jnp.dot(normed_two, full_router, preferred_element_type=jnp.float32)
    gates, back_gates = jax.vjp(
        lambda scored: jax.nn.softmax(jnp.take_along_axis(scored, route_ids, axis=1), axis=-1),
        logits,
    )
    labels = jnp.arange(experts, dtype=jnp.int32)
    onehot = route_ids[:, :, None] == labels[None, None, :]
    assign = jnp.sum(onehot.astype(jnp.int32), axis=1)
    rank = jnp.cumsum(assign, axis=0) - 1
    slot_ids = jnp.arange(CAP, dtype=jnp.int32)
    hit = (assign[:, :, None] == 1) & (rank[:, :, None] == slot_ids[None, None, :])
    token_ids = jnp.arange(count, dtype=jnp.int32)
    slot_token = jnp.sum(jnp.where(hit, token_ids[:, None, None], 0), axis=0)
    slot_flat = slot_token.reshape(-1)
    route_rank = jnp.take_along_axis(rank, route_ids, axis=1)
    flat_index = (route_ids * CAP + route_rank).reshape(-1)
    slot_inputs = jnp.take(normed_two, slot_flat, axis=0)
    grad_rows = cotangent[0].astype(jnp.float32)
    gate_token = jnp.sum(jnp.where(onehot, gates[:, :, None], 0.0), axis=1)
    gate_slot = jnp.sum(jnp.where(hit, gate_token[:, :, None], 0.0), axis=0)
    d_expert = (jnp.take(grad_rows, slot_flat, axis=0) * gate_slot.reshape(-1)[:, None]).astype(
        jnp.bfloat16
    )
    gate_blocks = w_gate.reshape(blocks, EXP_BLOCK, -1, hidden_width)
    up_blocks = w_up.reshape(blocks, EXP_BLOCK, -1, hidden_width)
    down_blocks = w_down.reshape(blocks, EXP_BLOCK, -1, model_width)
    expert_rows = slot_inputs.reshape(blocks, EXP_BLOCK, CAP, model_width)
    d_blocks = d_expert.reshape(blocks, EXP_BLOCK, CAP, model_width)

    def forward_block(carry, pieces):
        piece_gate, piece_up, piece_down, rows_in = pieces
        full_gate, full_up, full_down = (
            lax.all_gather(piece_gate, ("ctx", "fsdp"), axis=1, tiled=True),
            lax.all_gather(piece_up, ("ctx", "fsdp"), axis=1, tiled=True),
            lax.all_gather(piece_down, ("ctx", "fsdp"), axis=1, tiled=True),
        )
        return (carry, expert_ahead(rows_in, full_gate, full_up, full_down))

    unused, (acts_gate, acts_up, expert_out) = lax.scan(
        forward_block, jnp.float32(0.0), (gate_blocks, up_blocks, down_blocks, expert_rows)
    )

    def backward_block(carry, pieces):
        piece_gate, piece_up, piece_down, rows_in, act_gate, act_up, d_made = pieces
        full_gate, full_up, full_down = (
            lax.all_gather(piece_gate, ("ctx", "fsdp"), axis=1, tiled=True),
            lax.all_gather(piece_up, ("ctx", "fsdp"), axis=1, tiled=True),
            lax.all_gather(piece_down, ("ctx", "fsdp"), axis=1, tiled=True),
        )
        d_rows, part_gate, part_up, part_down = expert_behind(
            rows_in, act_gate, act_up, d_made, full_gate, full_up, full_down
        )
        shares = (
            lax.psum_scatter(
                part_gate.astype(jnp.bfloat16), ("ctx", "fsdp"), scatter_dimension=1, tiled=True
            ).astype(jnp.float32),
            lax.psum_scatter(
                part_up.astype(jnp.bfloat16), ("ctx", "fsdp"), scatter_dimension=1, tiled=True
            ).astype(jnp.float32),
            lax.psum_scatter(
                part_down.astype(jnp.bfloat16), ("ctx", "fsdp"), scatter_dimension=1, tiled=True
            ).astype(jnp.float32),
        )
        return (carry, (d_rows, shares))

    unused, (d_rows_blocks, (block_gate, block_up, block_down)) = lax.scan(
        backward_block,
        jnp.float32(0.0),
        (gate_blocks, up_blocks, down_blocks, expert_rows, acts_gate, acts_up, d_blocks),
    )
    made_slots = expert_out.reshape(experts * CAP, model_width)
    d_rows_all = d_rows_blocks.reshape(experts * CAP, model_width)
    share_gate = block_gate.reshape(experts, -1, hidden_width)
    share_up = block_up.reshape(experts, -1, hidden_width)
    share_down = block_down.reshape(experts, -1, model_width)
    picked = (
        jnp.take(made_slots, flat_index, axis=0)
        .astype(jnp.float32)
        .reshape(count, route_ids.shape[1], -1)
    )
    resid_two = resid_one + jnp.sum(gates[:, :, None] * picked, axis=1)
    output = resid_two.astype(jnp.bfloat16)[None]
    d_gates = jnp.sum(picked * grad_rows[:, None, :], axis=-1)
    d_normed_two = jax.ops.segment_sum(
        d_rows_all.astype(jnp.float32), slot_flat, num_segments=count
    )
    d_logits = back_gates(d_gates)[0].astype(jnp.bfloat16)
    part_router = jnp.einsum("td,te->de", normed_two, d_logits, preferred_element_type=jnp.float32)
    d_normed_two = d_normed_two + jnp.einsum(
        "te,de->td", d_logits, full_router, preferred_element_type=jnp.float32
    )
    d_resid_one, d_gain_ffn = back_two(d_normed_two)
    d_resid_one = d_resid_one + grad_rows
    full_query, full_key, full_value, full_out, full_router = (
        lax.all_gather(w_query, ("ctx", "fsdp"), axis=0, tiled=True),
        lax.all_gather(w_key, ("ctx", "fsdp"), axis=0, tiled=True),
        lax.all_gather(w_value, ("ctx", "fsdp"), axis=0, tiled=True),
        lax.all_gather(w_out, ("ctx", "fsdp"), axis=0, tiled=True),
        lax.all_gather(w_router, ("ctx", "fsdp"), axis=0, tiled=True),
    )
    d_branch = d_resid_one.astype(jnp.bfloat16)
    part_out = jnp.einsum("ip,id->pd", mixed_low, d_branch, preferred_element_type=jnp.float32)
    d_mixed = (
        jnp.einsum("id,pd->ip", d_branch, full_out, preferred_element_type=jnp.float32)
        .astype(jnp.bfloat16)
        .reshape(count, kv_heads, group, width)
    )
    again_scores = (
        jnp.einsum("ikgd,jkd->kgij", query_low, keys_all, preferred_element_type=jnp.float32)
        * scale
    )
    probs_full = jnp.where(allowed, jnp.exp(again_scores - log_total), 0.0)
    probs_again = probs_full.astype(jnp.bfloat16)
    d_probs = jnp.einsum("ikgd,jkd->kgij", d_mixed, values_all, preferred_element_type=jnp.float32)
    row_dot = jnp.sum(probs_full * d_probs, axis=-1, keepdims=True)
    d_scores = (probs_full * (d_probs - row_dot)).astype(jnp.bfloat16)
    d_query = (
        jnp.einsum("kgij,jkd->ikgd", d_scores, keys_all, preferred_element_type=jnp.float32) * scale
    )
    d_keys_all = (
        jnp.einsum("kgij,ikgd->jkd", d_scores, query_low, preferred_element_type=jnp.float32)
        * scale
    )
    d_values_all = jnp.einsum(
        "kgij,ikgd->jkd", probs_again, d_mixed, preferred_element_type=jnp.float32
    )
    d_keyed, d_value = (
        lax.psum_scatter(
            d_keys_all.astype(jnp.bfloat16), "ctx", scatter_dimension=0, tiled=True
        ).astype(jnp.float32),
        lax.psum_scatter(
            d_values_all.astype(jnp.bfloat16), "ctx", scatter_dimension=0, tiled=True
        ).astype(jnp.float32),
    )
    d_query_round = d_query.reshape(count, heads, width).astype(jnp.bfloat16).astype(jnp.float32)
    d_keyed_round = d_keyed.astype(jnp.bfloat16).astype(jnp.float32)
    d_value_low = d_value.astype(jnp.bfloat16).reshape(count, kv_heads * width)
    d_q_lin, d_k_lin, d_gain_query, d_gain_key = back_heads((d_query_round, d_keyed_round))
    d_q_low = d_q_lin.astype(jnp.bfloat16)
    d_k_low = d_k_lin.astype(jnp.bfloat16)
    part_query = jnp.einsum("ic,ip->cp", normed_one, d_q_low, preferred_element_type=jnp.float32)
    part_key = jnp.einsum("ic,ip->cp", normed_one, d_k_low, preferred_element_type=jnp.float32)
    part_value = jnp.einsum(
        "ic,ip->cp", normed_one, d_value_low, preferred_element_type=jnp.float32
    )
    d_normed_one = jnp.einsum("ip,cp->ic", d_q_low, full_query, preferred_element_type=jnp.float32)
    d_normed_one = d_normed_one + jnp.einsum(
        "ip,cp->ic", d_k_low, full_key, preferred_element_type=jnp.float32
    )
    d_normed_one = d_normed_one + jnp.einsum(
        "ip,cp->ic", d_value_low, full_value, preferred_element_type=jnp.float32
    )
    d_resid, d_gain_attn = back_one(d_normed_one)
    grad_tokens = (d_resid + d_resid_one)[None]
    attn_shares = (
        lax.psum_scatter(
            part_query.astype(jnp.bfloat16), ("ctx", "fsdp"), scatter_dimension=0, tiled=True
        ).astype(jnp.float32),
        lax.psum_scatter(
            part_key.astype(jnp.bfloat16), ("ctx", "fsdp"), scatter_dimension=0, tiled=True
        ).astype(jnp.float32),
        lax.psum_scatter(
            part_value.astype(jnp.bfloat16), ("ctx", "fsdp"), scatter_dimension=0, tiled=True
        ).astype(jnp.float32),
        lax.psum_scatter(
            part_out.astype(jnp.bfloat16), ("ctx", "fsdp"), scatter_dimension=0, tiled=True
        ).astype(jnp.float32),
        lax.psum_scatter(
            part_router.astype(jnp.bfloat16), ("ctx", "fsdp"), scatter_dimension=0, tiled=True
        ).astype(jnp.float32),
    )
    summed = (
        lax.psum(attn_shares[0].astype(jnp.bfloat16), "grp").astype(jnp.float32),
        lax.psum(attn_shares[1].astype(jnp.bfloat16), "grp").astype(jnp.float32),
        lax.psum(attn_shares[2].astype(jnp.bfloat16), "grp").astype(jnp.float32),
        lax.psum(attn_shares[3].astype(jnp.bfloat16), "grp").astype(jnp.float32),
        lax.psum(attn_shares[4].astype(jnp.bfloat16), "grp").astype(jnp.float32),
        lax.psum(share_gate.astype(jnp.bfloat16), "grp").astype(jnp.float32),
        lax.psum(share_up.astype(jnp.bfloat16), "grp").astype(jnp.float32),
        lax.psum(share_down.astype(jnp.bfloat16), "grp").astype(jnp.float32),
    )
    gain_attn_sum, gain_ffn_sum, gain_query_sum, gain_key_sum = lax.psum(
        (d_gain_attn, d_gain_ffn, d_gain_query, d_gain_key), ("grp", "ctx", "fsdp")
    )
    return (
        output,
        grad_tokens,
        summed[0],
        summed[1],
        summed[2],
        summed[3],
        summed[4],
        summed[5],
        summed[6],
        summed[7],
        gain_attn_sum,
        gain_ffn_sum,
        gain_query_sum,
        gain_key_sum,
    )


def solution(mesh):
    in_specs = (
        P(("grp", "fsdp"), "ctx", None),
        P(("grp", "fsdp"), None),
        P(("grp", "fsdp"), None),
        P(("grp", "fsdp"), "ctx", None),
        P(("ctx", "fsdp"), None),
        P(("ctx", "fsdp"), None),
        P(("ctx", "fsdp"), None),
        P(("ctx", "fsdp"), None),
        P(("ctx", "fsdp"), None),
        P(None, ("ctx", "fsdp"), None),
        P(None, ("ctx", "fsdp"), None),
        P(None, ("ctx", "fsdp"), None),
        P(),
        P(),
        P(),
        P(),
        P(("grp", "fsdp"), "ctx", None),
    )
    out_specs = (
        P(("grp", "fsdp"), "ctx", None),
        P(("grp", "fsdp"), "ctx", None),
        P(("ctx", "fsdp"), None),
        P(("ctx", "fsdp"), None),
        P(("ctx", "fsdp"), None),
        P(("ctx", "fsdp"), None),
        P(("ctx", "fsdp"), None),
        P(None, ("ctx", "fsdp"), None),
        P(None, ("ctx", "fsdp"), None),
        P(None, ("ctx", "fsdp"), None),
        P(),
        P(),
        P(),
        P(),
    )
    return jax.shard_map(
        per_device, mesh=mesh, in_specs=in_specs, out_specs=out_specs, check_vma=False
    )
```

profile of v0, /device:TPU:0, one launch (start us, length us, event | category | flops | bytes accessed | tf_op | source)
XLA Modules:
  0.0 5725.1 jit_solution(9030230621862295770)
XLA Ops:
  443.9 1260.2 %while.30 = (s32[]{:T(128)}, f32[4,4,160,768]{3,2,1,0:T(8,128)}, f32[4,4,160,768]{3,2,1,0:T(8,128)}, bf16[4,4,160,2048]{3,2,1,0:T(8,128)(2,1)}, bf16[4,4,160,204...) while((s32[]{:T(128)}, f32[4,4,160,768]{3,2,1,0:T(8,128)}, ...), condition=%wide.region_13.14_spmd, body=%wide.region_12.13_spmd.sunk | while | flops 6044057600 | bytes 182454512 | solution.py:191
  450.5 96.0 %all-gather.45.cloned.1.call-done = bf16[1,4,2048,768]{3,2,1,0:T(8,128)(2,1)} async-done(((bf16[1,4,128,768]{3,2,1,0:T(8,128)(2,1)}), bf16[1,4,2048,768]{3,2,1,0:T(8,128)(2,1)}) %all-gather.45.cloned.1.call-update) | async-done | bytes 12582928 | tf_op jit(solution)/shard_map/while/body/eval_jaxpr/all_gather | solution.py:186
  765.8 95.7 %all-gather.45.cloned.1.call-done = bf16[1,4,2048,768]{3,2,1,0:T(8,128)(2,1)} async-done(((bf16[1,4,128,768]{3,2,1,0:T(8,128)(2,1)}), bf16[1,4,2048,768]{3,2,1,0:T(8,128)(2,1)}) %all-gather.45.cloned.1.call-update) | async-done | bytes 12582928 | tf_op jit(solution)/shard_map/while/body/eval_jaxpr/all_gather | solution.py:186
  1080.8 96.0 %all-gather.45.cloned.1.call-done = bf16[1,4,2048,768]{3,2,1,0:T(8,128)(2,1)} async-done(((bf16[1,4,128,768]{3,2,1,0:T(8,128)(2,1)}), bf16[1,4,2048,768]{3,2,1,0:T(8,128)(2,1)}) %all-gather.45.cloned.1.call-update) | async-done | bytes 12582928 | tf_op jit(solution)/shard_map/while/body/eval_jaxpr/all_gather | solution.py:186
  1775.6 2894.5 %while.31 = (s32[]{:T(128)}, bf16[4,4,160,2048]{3,2,1,0:T(8,128)(2,1)}, bf16[4,4,128,768]{3,2,1,0:T(8,128)(2,1)}, bf16[4,4,128,768]{3,2,1,0:T(8,128)(2,1)}, bf16...) while((s32[]{:T(128)}, ...), condition=%wide.region_24.25_spmd, body=%wide.region_20.24_spmd.sunk | while | flops 12111609856 | bytes 365300128 | solution.py:218
  1912.1 104.2 %reduce-scatter.31.cloned.1.call-done = bf16[4,48,2048]{2,1,0:T(8,128)(2,1)} async-done(((bf16[4,768,2048]{2,1,0:T(8,128)(2,1)}), bf16[4,48,2048]{2,1,0:T(8,128)(2,1)}) %reduce-scatter.31.cloned.1.call-update) | async-done | bytes 786448 | tf_op jit(solution)/shard_map/while/body/eval_jaxpr/reduce_scatter | solution.py:212
  2018.4 101.0 %all-gather.51.cloned.1.call-done = bf16[1,4,2048,768]{3,2,1,0:T(8,128)(2,1)} async-done(((bf16[1,4,128,768]{3,2,1,0:T(8,128)(2,1)}), bf16[1,4,2048,768]{3,2,1,0:T(8,128)(2,1)}) %all-gather.51.cloned.1.call-update) | async-done | bytes 12582928 | tf_op jit(solution)/shard_map/while/body/eval_jaxpr/all_gather | solution.py:199
  2232.8 125.6 %reduce-scatter.27.cloned.1.call-done = bf16[4,128,768]{2,1,0:T(8,128)(2,1)} async-done(((bf16[4,2048,768]{2,1,0:T(8,128)(2,1)}), bf16[4,128,768]{2,1,0:T(8,128)(2,1)}) %reduce-scatter.27.cloned.1.call-update) | async-done | bytes 786448 | tf_op jit(solution)/shard_map/while/body/eval_jaxpr/reduce_scatter | solution.py:206
  2360.5 136.2 %reduce-scatter.29.cloned.1.call-done = bf16[4,128,768]{2,1,0:T(8,128)(2,1)} async-done(((bf16[4,2048,768]{2,1,0:T(8,128)(2,1)}), bf16[4,128,768]{2,1,0:T(8,128)(2,1)}) %reduce-scatter.29.cloned.1.call-update) | async-done | bytes 786448 | tf_op jit(solution)/shard_map/while/body/eval_jaxpr/reduce_scatter | solution.py:209
  2635.8 104.2 %reduce-scatter.31.cloned.1.call-done = bf16[4,48,2048]{2,1,0:T(8,128)(2,1)} async-done(((bf16[4,768,2048]{2,1,0:T(8,128)(2,1)}), bf16[4,48,2048]{2,1,0:T(8,128)(2,1)}) %reduce-scatter.31.cloned.1.call-update) | async-done | bytes 786448 | tf_op jit(solution)/shard_map/while/body/eval_jaxpr/reduce_scatter | solution.py:212
  2742.0 100.9 %all-gather.51.cloned.1.call-done = bf16[1,4,2048,768]{3,2,1,0:T(8,128)(2,1)} async-done(((bf16[1,4,128,768]{3,2,1,0:T(8,128)(2,1)}), bf16[1,4,2048,768]{3,2,1,0:T(8,128)(2,1)}) %all-gather.51.cloned.1.call-update) | async-done | bytes 12582928 | tf_op jit(solution)/shard_map/while/body/eval_jaxpr/all_gather | solution.py:199
  2956.5 125.5 %reduce-scatter.27.cloned.1.call-done = bf16[4,128,768]{2,1,0:T(8,128)(2,1)} async-done(((bf16[4,2048,768]{2,1,0:T(8,128)(2,1)}), bf16[4,128,768]{2,1,0:T(8,128)(2,1)}) %reduce-scatter.27.cloned.1.call-update) | async-done | bytes 786448 | tf_op jit(solution)/shard_map/while/body/eval_jaxpr/reduce_scatter | solution.py:206
  3084.1 136.2 %reduce-scatter.29.cloned.1.call-done = bf16[4,128,768]{2,1,0:T(8,128)(2,1)} async-done(((bf16[4,2048,768]{2,1,0:T(8,128)(2,1)}), bf16[4,128,768]{2,1,0:T(8,128)(2,1)}) %reduce-scatter.29.cloned.1.call-update) | async-done | bytes 786448 | tf_op jit(solution)/shard_map/while/body/eval_jaxpr/reduce_scatter | solution.py:209
  3359.3 104.4 %reduce-scatter.31.cloned.1.call-done = bf16[4,48,2048]{2,1,0:T(8,128)(2,1)} async-done(((bf16[4,768,2048]{2,1,0:T(8,128)(2,1)}), bf16[4,48,2048]{2,1,0:T(8,128)(2,1)}) %reduce-scatter.31.cloned.1.call-update) | async-done | bytes 786448 | tf_op jit(solution)/shard_map/while/body/eval_jaxpr/reduce_scatter | solution.py:212
  3465.8 100.9 %all-gather.51.cloned.1.call-done = bf16[1,4,2048,768]{3,2,1,0:T(8,128)(2,1)} async-done(((bf16[1,4,128,768]{3,2,1,0:T(8,128)(2,1)}), bf16[1,4,2048,768]{3,2,1,0:T(8,128)(2,1)}) %all-gather.51.cloned.1.call-update) | async-done | bytes 12582928 | tf_op jit(solution)/shard_map/while/body/eval_jaxpr/all_gather | solution.py:199
  3680.0 125.7 %reduce-scatter.27.cloned.1.call-done = bf16[4,128,768]{2,1,0:T(8,128)(2,1)} async-done(((bf16[4,2048,768]{2,1,0:T(8,128)(2,1)}), bf16[4,128,768]{2,1,0:T(8,128)(2,1)}) %reduce-scatter.27.cloned.1.call-update) | async-done | bytes 786448 | tf_op jit(solution)/shard_map/while/body/eval_jaxpr/reduce_scatter | solution.py:206
  3807.8 136.2 %reduce-scatter.29.cloned.1.call-done = bf16[4,128,768]{2,1,0:T(8,128)(2,1)} async-done(((bf16[4,2048,768]{2,1,0:T(8,128)(2,1)}), bf16[4,128,768]{2,1,0:T(8,128)(2,1)}) %reduce-scatter.29.cloned.1.call-update) | async-done | bytes 786448 | tf_op jit(solution)/shard_map/while/body/eval_jaxpr/reduce_scatter | solution.py:209
  4082.8 104.5 %reduce-scatter.31.cloned.1.call-done = bf16[4,48,2048]{2,1,0:T(8,128)(2,1)} async-done(((bf16[4,768,2048]{2,1,0:T(8,128)(2,1)}), bf16[4,48,2048]{2,1,0:T(8,128)(2,1)}) %reduce-scatter.31.cloned.1.call-update) | async-done | bytes 786448 | tf_op jit(solution)/shard_map/while/body/eval_jaxpr/reduce_scatter | solution.py:212
  4189.4 100.9 %all-gather.51.cloned.1.call-done = bf16[1,4,2048,768]{3,2,1,0:T(8,128)(2,1)} async-done(((bf16[1,4,128,768]{3,2,1,0:T(8,128)(2,1)}), bf16[1,4,2048,768]{3,2,1,0:T(8,128)(2,1)}) %all-gather.51.cloned.1.call-update) | async-done | bytes 12582928 | tf_op jit(solution)/shard_map/while/body/eval_jaxpr/all_gather | solution.py:199
  4403.7 125.6 %reduce-scatter.27.cloned.1.call-done = bf16[4,128,768]{2,1,0:T(8,128)(2,1)} async-done(((bf16[4,2048,768]{2,1,0:T(8,128)(2,1)}), bf16[4,128,768]{2,1,0:T(8,128)(2,1)}) %reduce-scatter.27.cloned.1.call-update) | async-done | bytes 786448 | tf_op jit(solution)/shard_map/while/body/eval_jaxpr/reduce_scatter | solution.py:206
  4531.4 136.5 %reduce-scatter.29.cloned.1.call-done = bf16[4,128,768]{2,1,0:T(8,128)(2,1)} async-done(((bf16[4,2048,768]{2,1,0:T(8,128)(2,1)}), bf16[4,128,768]{2,1,0:T(8,128)(2,1)}) %reduce-scatter.29.cloned.1.call-update) | async-done | bytes 786448 | tf_op jit(solution)/shard_map/while/body/eval_jaxpr/reduce_scatter | solution.py:209
  5000.6 181.7 %reduce-scatter.17.cloned.1.call-done = bf16[128,4096]{1,0:T(8,128)(2,1)} async-done(((bf16[2048,4096]{1,0:T(8,128)(2,1)}), bf16[128,4096]{1,0:T(8,128)(2,1)}) %reduce-scatter.17.cloned.1.call-update) | async-done | bytes 1048592 | tf_op jit(solution)/shard_map/reduce_scatter | solution.py:308
  5182.3 181.5 %reduce-scatter.23.cloned.1.call-done = bf16[256,2048]{1,0:T(8,128)(2,1)} async-done(((bf16[4096,2048]{1,0:T(8,128)(2,1)}), bf16[256,2048]{1,0:T(8,128)(2,1)}) %reduce-scatter.23.cloned.1.call-update) | async-done | bytes 1048592 | tf_op jit(solution)/shard_map/reduce_scatter | solution.py:317
  5479.9 221.5 %all-reduce.8.cloned.1.call-done = (bf16[128,4096]{1,0:T(8,128)(2,1)}, bf16[128,512]{1,0:T(8,128)(2,1)}, bf16[128,512]{1,0:T(8,128)(2,1)}, bf16[256,2048]{1,0:T(...) async-done(((bf16[128,4096]{1,0:T(8,128)(2,1)}, bf16[128,512]{1,0:T(8,128)(2,1)}, ...) | async-done | bytes 11796496 | tf_op jit(solution)/shard_map/psum | solution.py:325
  (514 shorter events, 2967.6 us)
Async XLA Ops:
  448.3 302.0 %all-gather.47.cloned.1.call-start = ((), (), s32[]{:S(2)}) async-start(), calls=%async_computation.26 | async-start | bytes 13369344 | tf_op jit(solution)/shard_map/while/body/eval_jaxpr/all_gather | solution.py:187
  763.7 301.6 %all-gather.47.cloned.1.call-start = ((), (), s32[]{:S(2)}) async-start(), calls=%async_computation.26 | async-start | bytes 13369344 | tf_op jit(solution)/shard_map/while/body/eval_jaxpr/all_gather | solution.py:187
  1078.6 301.7 %all-gather.47.cloned.1.call-start = ((), (), s32[]{:S(2)}) async-start(), calls=%async_computation.26 | async-start | bytes 13369344 | tf_op jit(solution)/shard_map/while/body/eval_jaxpr/all_gather | solution.py:187
  1393.6 301.4 %all-gather.47.cloned.1.call-start = ((), (), s32[]{:S(2)}) async-start(), calls=%async_computation.26 | async-start | bytes 13369344 | tf_op jit(solution)/shard_map/while/body/eval_jaxpr/all_gather | solution.py:187
  1789.5 329.9 %all-gather.51.cloned.1.call-start = ((), (), s32[]{:S(2)}) async-start(), calls=%async_computation.28 | async-start | bytes 13369344 | tf_op jit(solution)/shard_map/while/body/eval_jaxpr/all_gather | solution.py:199
  1791.6 429.4 %all-gather.53.cloned.1.call-start = ((), (), s32[]{:S(2)}) async-start(), calls=%async_computation.29 | async-start | bytes 13369344 | tf_op jit(solution)/shard_map/while/body/eval_jaxpr/all_gather | solution.py:198
  1793.8 564.6 %reduce-scatter.27.cloned.1.call-start = ((), (), s32[]{:S(2)}) async-start(), calls=%async_computation.30 | async-start | bytes 13369344 | tf_op jit(solution)/shard_map/while/body/eval_jaxpr/reduce_scatter | solution.py:206
  1901.8 594.8 %reduce-scatter.29.cloned.1.call-start = ((), (), s32[]{:S(2)}) async-start(), calls=%async_computation.31 | async-start | bytes 13369344 | tf_op jit(solution)/shard_map/while/body/eval_jaxpr/reduce_scatter | solution.py:209
  2512.3 330.7 %all-gather.51.cloned.1.call-start = ((), (), s32[]{:S(2)}) async-start(), calls=%async_computation.28 | async-start | bytes 13369344 | tf_op jit(solution)/shard_map/while/body/eval_jaxpr/all_gather | solution.py:199
  2514.5 430.1 %all-gather.53.cloned.1.call-start = ((), (), s32[]{:S(2)}) async-start(), calls=%async_computation.29 | async-start | bytes 13369344 | tf_op jit(solution)/shard_map/while/body/eval_jaxpr/all_gather | solution.py:198
  2516.6 565.4 %reduce-scatter.27.cloned.1.call-start = ((), (), s32[]{:S(2)}) async-start(), calls=%async_computation.30 | async-start | bytes 13369344 | tf_op jit(solution)/shard_map/while/body/eval_jaxpr/reduce_scatter | solution.py:206
  2625.5 594.7 %reduce-scatter.29.cloned.1.call-start = ((), (), s32[]{:S(2)}) async-start(), calls=%async_computation.31 | async-start | bytes 13369344 | tf_op jit(solution)/shard_map/while/body/eval_jaxpr/reduce_scatter | solution.py:209
  3235.9 330.8 %all-gather.51.cloned.1.call-start = ((), (), s32[]{:S(2)}) async-start(), calls=%async_computation.28 | async-start | bytes 13369344 | tf_op jit(solution)/shard_map/while/body/eval_jaxpr/all_gather | solution.py:199
  3238.0 430.3 %all-gather.53.cloned.1.call-start = ((), (), s32[]{:S(2)}) async-start(), calls=%async_computation.29 | async-start | bytes 13369344 | tf_op jit(solution)/shard_map/while/body/eval_jaxpr/all_gather | solution.py:198
  3240.2 565.5 %reduce-scatter.27.cloned.1.call-start = ((), (), s32[]{:S(2)}) async-start(), calls=%async_computation.30 | async-start | bytes 13369344 | tf_op jit(solution)/shard_map/while/body/eval_jaxpr/reduce_scatter | solution.py:206
  3349.1 594.8 %reduce-scatter.29.cloned.1.call-start = ((), (), s32[]{:S(2)}) async-start(), calls=%async_computation.31 | async-start | bytes 13369344 | tf_op jit(solution)/shard_map/while/body/eval_jaxpr/reduce_scatter | solution.py:209
  3959.6 330.6 %all-gather.51.cloned.1.call-start = ((), (), s32[]{:S(2)}) async-start(), calls=%async_computation.28 | async-start | bytes 13369344 | tf_op jit(solution)/shard_map/while/body/eval_jaxpr/all_gather | solution.py:199
  3961.8 430.1 %all-gather.53.cloned.1.call-start = ((), (), s32[]{:S(2)}) async-start(), calls=%async_computation.29 | async-start | bytes 13369344 | tf_op jit(solution)/shard_map/while/body/eval_jaxpr/all_gather | solution.py:198
  3963.9 565.4 %reduce-scatter.27.cloned.1.call-start = ((), (), s32[]{:S(2)}) async-start(), calls=%async_computation.30 | async-start | bytes 13369344 | tf_op jit(solution)/shard_map/while/body/eval_jaxpr/reduce_scatter | solution.py:206
  4072.5 595.3 %reduce-scatter.29.cloned.1.call-start = ((), (), s32[]{:S(2)}) async-start(), calls=%async_computation.31 | async-start | bytes 13369344 | tf_op jit(solution)/shard_map/while/body/eval_jaxpr/reduce_scatter | solution.py:209
  4875.1 307.2 %reduce-scatter.17.cloned.1.call-start = ((), (), s32[]{:S(2)}) async-start(), calls=%async_computation.18 | async-start | bytes 17825792 | tf_op jit(solution)/shard_map/reduce_scatter | solution.py:308
  4900.4 463.4 %reduce-scatter.23.cloned.1.call-start = ((), (), s32[]{:S(2)}) async-start(), calls=%async_computation.21 | async-start | bytes 17825792 | tf_op jit(solution)/shard_map/reduce_scatter | solution.py:317
  4913.4 509.2 %reduce-scatter.25.cloned.1.call-start = ((), (), s32[]{:S(2)}) async-start(), calls=%async_computation.22 | async-start | bytes 557056
  4915.9 785.6 %all-reduce.8.cloned.1.call-start = ((), (), s32[]{:S(2)}) async-start(), calls=%async_computation.23 | async-start | bytes 23592960 | tf_op jit(solution)/shard_map/psum | solution.py:325
  (111 other events, 7782.4 us)
Sparse Core Ops, SparseCore 0:
  99.0 125.7 all-gather.38
  262.9 126.8 all-gather.40
  1883.4 132.7 reduce-scatter.30
  2019.4 99.8 all-gather.50
  2225.6 132.7 reduce-scatter.26
  2362.9 133.7 reduce-scatter.28
  2502.8 99.9 all-gather.48
  2607.2 132.7 reduce-scatter.30
  2743.0 99.9 all-gather.50
  2949.2 132.7 reduce-scatter.26
  3086.4 133.7 reduce-scatter.28
  3226.3 99.8 all-gather.48
  3330.9 132.7 reduce-scatter.30
  3466.7 99.8 all-gather.50
  3672.9 132.7 reduce-scatter.26
  3810.1 133.7 reduce-scatter.28
  3949.7 99.8 all-gather.48
  4054.3 132.9 reduce-scatter.30
  4190.3 99.9 all-gather.50
  4396.5 132.7 reduce-scatter.26
  4533.9 133.8 reduce-scatter.28
  5004.6 177.6 reduce-scatter.16
  5186.2 177.5 reduce-scatter.22
  5426.5 274.8 all-reduce.7
  (26 shorter events, 2022.7 us)
where the time goes:
time: 5730 us
  waiting for transfers between devices  4660 us (81%)
  matrix products  549 us (10%)
  local copies, waits for them, and re-layouts  209 us (4%)
  other arithmetic  208 us (4%)
  blocking collectives  77.7 us (1%)
    reduce_scatter x4, waiting for transfers between devices, backward_block(): lax.psum_scatter(part_up.astype(jnp.bfloat16), ('ctx', 'fsdp'), scatter_d...  545 us
    reduce_scatter x4, waiting for transfers between devices, backward_block(): lax.psum_scatter(part_gate.astype(jnp.bfloat16), ('ctx', 'fsdp'), scatter...  502 us
    reduce_scatter x4, waiting for transfers between devices, backward_block(): lax.psum_scatter(part_down.astype(jnp.bfloat16), ('ctx', 'fsdp'), scatter...  417 us
    all_gather x4, waiting for transfers between devices, backward_block(): lax.all_gather(piece_up, ('ctx', 'fsdp'), axis=1, tiled=True)  404 us
    all_gather x4, waiting for transfers between devices, forward_block(): lax.all_gather(piece_up, ('ctx', 'fsdp'), axis=1, tiled=True)  383 us
    all_gather x4, waiting for transfers between devices, forward_block(): lax.all_gather(piece_gate, ('ctx', 'fsdp'), axis=1, tiled=True)  373 us
    all_gather x4, waiting for transfers between devices, forward_block(): lax.all_gather(piece_down, ('ctx', 'fsdp'), axis=1, tiled=True)  368 us
    all_gather x4, waiting for transfers between devices, backward_block(): lax.all_gather(piece_gate, ('ctx', 'fsdp'), axis=1, tiled=True)  362 us
  transfers between devices with their start and end apart: 50, of which 48 were waited for; matrix products, arithmetic and copies ran while one was open for 11% of the time, Pallas kernels for 0%

commit v1 on v0

v1 whole, which is shorter than its diff:
```python
import math

import jax
import jax.numpy as jnp
from jax import lax
from jax.sharding import Mesh
from jax.sharding import PartitionSpec as P

epsilon = 1e-06
low = jnp.bfloat16
wide = jnp.float32
SWAP = [(0, 1), (1, 0)]
ROW_TILE = 16


def normed(values, gain):
    return values * lax.rsqrt(jnp.mean(values * values, axis=-1, keepdims=True) + epsilon) * gain


def angles(place, width):
    steps = jnp.arange(width // 2).astype(jnp.float32)
    inverse = jnp.exp(steps * (-2.0 * math.log(1000000.0) / width))
    return place.astype(jnp.float32)[:, None] * inverse[None, :]


def rotate(values, angle):
    half = values.shape[-1] // 2
    cosine = jnp.cos(angle)[:, None, :]
    sine = jnp.sin(angle)[:, None, :]
    first = values[..., :half]
    second = values[..., half:]
    return jnp.concatenate(
        [first * cosine - second * sine, second * cosine + first * sine], axis=-1
    )


def head_prep(q_lin, k_lin, gain_query, gain_key, angle):
    count = q_lin.shape[0]
    width = gain_query.shape[0]
    query = rotate(normed(q_lin.reshape(count, -1, width), gain_query), angle)
    keyed = rotate(normed(k_lin.reshape(count, -1, width), gain_key), angle)
    return (query, keyed)


def dot(left, right):
    return jnp.dot(left, right, preferred_element_type=jnp.float32)


def dot_nt(left, right):
    return lax.dot_general(left, right, (((1,), (1,)), ((), ())), preferred_element_type=jnp.float32)


def dot_tn(left, right):
    return lax.dot_general(left, right, (((0,), (0,)), ((), ())), preferred_element_type=jnp.float32)


def flat_index(axes):
    index = 0
    for axis in axes:
        index = index * 2 + lax.axis_index(axis)
    return index


def gather_rows(rows, order):
    for axis in order:
        rows = jnp.concatenate([rows, lax.ppermute(rows, axis, SWAP)], axis=0)
    return rows


def scatter_rows(rows, order, sent):
    for axis in reversed(order):
        half = rows.shape[0] // 2
        arrived = lax.ppermute(rows[half:].astype(sent), axis, SWAP)
        rows = rows[:half].astype(wide) + arrived.astype(wide)
    return rows


def all_to_all(axes, pick):
    amount = 1 << len(axes)
    here = flat_index(axes)
    own = pick(here)
    held = jnp.zeros((amount,) + own.shape, own.dtype)
    held = lax.dynamic_update_index_in_dim(held, own, here, 0)
    for step in range(1, amount):
        other = jnp.bitwise_xor(here, step)
        pairs = [(place, place ^ step) for place in range(amount)]
        arrived = lax.ppermute(pick(other), axes, pairs)
        held = lax.dynamic_update_index_in_dim(held, arrived, other, 0)
    return held


def take(stack, index):
    return lax.dynamic_index_in_dim(stack, index, 0, keepdims=False)


def gather_blocks(block, axes, at):
    if not axes:
        return block
    if len(axes) > 1:
        return lax.all_gather(block, axes, axis=at, tiled=True)
    other = lax.ppermute(block, axes[0], SWAP)
    first = lax.axis_index(axes[0]) == 0
    return jnp.concatenate(
        [jnp.where(first, block, other), jnp.where(first, other, block)], axis=at
    )


def own_first(stack, axes):
    if len(axes) != 1:
        return stack
    first = lax.axis_index(axes[0]) == 0
    return jnp.where(first, stack, jnp.flip(stack, 0))


def gather_halves(block, axes):
    if not axes:
        return block[None]
    if len(axes) > 1:
        return lax.all_gather(block, axes, axis=0, tiled=False)
    return jnp.stack([block, lax.ppermute(block, axes[0], SWAP)])


def scatter_halves(stack, axes):
    if not axes:
        return stack[0].astype(low)
    if len(axes) > 1:
        return lax.psum_scatter(stack.astype(low), axes, scatter_dimension=0, tiled=False)
    arrived = lax.ppermute(stack[1].astype(low), axes[0], SWAP)
    return (stack[0].astype(wide) + arrived.astype(wide)).astype(low)


def scatter_blocks(stack, axes):
    if not axes:
        return stack[0].astype(low)
    if len(axes) > 1:
        return lax.psum_scatter(stack.astype(low), axes, scatter_dimension=0, tiled=False)
    here = lax.axis_index(axes[0])
    arrived = lax.ppermute(take(stack, 1 - here).astype(low), axes[0], SWAP)
    return (take(stack, here).astype(wide) + arrived.astype(wide)).astype(low)


def sum_all(value, axes):
    for axis in axes:
        value = value + lax.ppermute(value, axis, SWAP)
    return value


def per_device(
    g_axes,
    c_axes,
    f_axes,
    tokens,
    places,
    segments,
    routes,
    w_query,
    w_key,
    w_value,
    w_out,
    w_router,
    w_gate,
    w_up,
    w_down,
    gain_attn,
    gain_ffn,
    gain_query,
    gain_key,
    cotangent,
):
    groups, parts_c, parts_f = 1 << len(g_axes), 1 << len(c_axes), 1 << len(f_axes)
    count = tokens.shape[1]
    width = gain_query.shape[0]
    model_width = tokens.shape[2]
    heads = w_query.shape[1] // width // parts_c
    kv_heads = w_key.shape[1] // width // parts_c
    group = heads // kv_heads
    experts = w_gate.shape[0]
    hidden_width = w_gate.shape[2]
    scale = 1.0 / math.sqrt(width)
    rows_d = w_query.shape[0]
    rows_f = w_down.shape[1]
    pair_count = experts.bit_length() - 1 - len(g_axes) - len(c_axes)
    assert 0 <= pair_count <= len(f_axes)
    far_axes = f_axes[: len(f_axes) - pair_count]
    near_axes = f_axes[len(f_axes) - pair_count :]
    parts_far, parts_near = 1 << len(far_axes), 1 << len(near_axes)
    team_axes = c_axes + near_axes
    team = parts_c * parts_near
    all_axes = g_axes + c_axes + f_axes
    g_here = flat_index(g_axes)
    c_here = flat_index(c_axes)
    expert_here = flat_index(g_axes + team_axes)

    resid = tokens[0].astype(jnp.float32)
    norm_one, back_one = jax.vjp(normed, resid, gain_attn)
    normed_one = norm_one.astype(low)
    rows_one = (
        normed_one.reshape(count, parts_c, parts_f, rows_d)
        .transpose(0, 2, 1, 3)
        .reshape(count, model_width)
    )
    all_one = gather_rows(rows_one, c_axes)

    q_cols, k_cols = heads * width, kv_heads * width
    qkv_cols = q_cols + 2 * k_cols
    own_qkv = jnp.concatenate(
        [
            w_query.reshape(rows_d, parts_c, q_cols),
            w_key.reshape(rows_d, parts_c, k_cols),
            w_value.reshape(rows_d, parts_c, k_cols),
        ],
        axis=2,
    )
    own_qkv = own_qkv.reshape(rows_d, parts_c, groups, qkv_cols // groups).transpose(2, 1, 0, 3)
    mine_qkv = take(own_qkv, g_here)
    got_qkv = all_to_all(c_axes, lambda other: take(mine_qkv, other))
    got_qkv = lax.all_gather(
        got_qkv.reshape(parts_c * rows_d, qkv_cols // groups), f_axes, axis=0, tiled=True
    )
    w_qkv = gather_blocks(got_qkv, g_axes, 1)
    out_cols = model_width // groups
    mine_out = take(w_out.reshape(-1, groups, out_cols).transpose(1, 0, 2), g_here)
    got_out = lax.all_gather(mine_out, f_axes, axis=0, tiled=True)
    w_mix = gather_blocks(got_out, g_axes, 1)
    full_router = lax.all_gather(w_router, c_axes + f_axes, axis=0, tiled=True)

    def fetch(pieces):
        got = all_to_all(team_axes, lambda other: take(pieces, g_here * team + other))
        return gather_halves(got, far_axes)

    full_gate = fetch(w_gate).reshape(model_width, hidden_width)
    full_up = fetch(w_up).reshape(model_width, hidden_width)
    got_down = own_first(fetch(w_down), far_axes)
    full_down = (
        got_down.reshape(parts_far, parts_c, parts_near * rows_f, model_width)
        .transpose(1, 0, 2, 3)
        .reshape(hidden_width, model_width)
    )

    turn = g_axes + c_axes[:-1] + near_axes
    orders = [turn[step:] + turn[:step] + c_axes[-1:] for step in range(3)]
    third = (count // 3) // ROW_TILE * ROW_TILE
    cuts = [0, count - 2 * third, count - third, count]
    spans = list(zip(cuts[:-1], cuts[1:], orders))
    grads_low = [gather_rows(cotangent[0, lo:hi], order) for lo, hi, order in spans]

    masks = jnp.array(
        [
            sum(
                ((position >> step) & 1) << (len(c_axes) - 1 - step)
                for step in range(len(c_axes))
            )
            for position in range(parts_c)
        ],
        jnp.int32,
    )
    block_ids = jnp.bitwise_xor(masks, c_here)
    place = jnp.take(places[0].reshape(parts_c, count), block_ids, axis=0).reshape(-1)
    segment = jnp.take(segments[0].reshape(parts_c, count), block_ids, axis=0).reshape(-1)
    length = place.shape[0]
    allowed = (segment[:, None] == segment[None, :]) & (place[None, :] <= place[:, None])
    angle = angles(place, width)
    lin = dot(all_one, w_qkv)
    q_lin, k_lin, v_lin = (
        lin[:, :q_cols],
        lin[:, q_cols : q_cols + k_cols],
        lin[:, q_cols + k_cols :],
    )
    (query, keyed), back_heads = jax.vjp(
        lambda first, second, third, fourth: head_prep(first, second, third, fourth, angle),
        q_lin,
        k_lin,
        gain_query,
        gain_key,
    )
    query_low = query.astype(low).reshape(length, kv_heads, group, width)
    keyed_low = keyed.astype(low)
    value_low = v_lin.astype(low).reshape(length, kv_heads, width)
    scores = (
        jnp.einsum("ikgd,jkd->kgij", query_low, keyed_low, preferred_element_type=jnp.float32)
        * scale
    )
    masked = jnp.where(allowed, scores, -1e30)
    row_max = jnp.max(masked, axis=-1, keepdims=True)
    expd = jnp.exp(masked - row_max)
    row_total = jnp.sum(expd, axis=-1, keepdims=True)
    log_total = row_max + jnp.log(row_total)
    probs_low = (expd / row_total).astype(low)
    mixed = jnp.einsum("kgij,jkd->ikgd", probs_low, value_low, preferred_element_type=jnp.float32)
    mixed_low = mixed.reshape(length, q_cols).astype(low)
    resid_one = resid + scatter_rows(dot(mixed_low, w_mix), c_axes, low)

    norm_two, back_two = jax.vjp(normed, resid_one, gain_ffn)
    normed_two = norm_two.astype(low)
    logits = dot(normed_two, full_router)
    labels = jnp.arange(experts, dtype=jnp.int32)
    chosen = jnp.any(routes[0][:, :, None] == labels[None, None, :], axis=1)
    logits = jnp.where(chosen, logits, -1e30)
    powers = jnp.where(chosen, jnp.exp(logits - jnp.max(logits, axis=-1, keepdims=True)), 0.0)
    gates = powers / jnp.sum(powers, axis=-1, keepdims=True)

    rows_two = normed_two.reshape(count, parts_c, parts_far, parts_near * rows_d)
    rows_two = own_first(rows_two.transpose(2, 0, 1, 3), far_axes)
    rows_two = rows_two.transpose(1, 0, 2, 3).reshape(count, model_width)
    column = labels == expert_here
    made_parts, back_parts, d_gate_parts = [], [], []
    part_gate = part_up = part_down = 0.0
    for (lo, hi, order), grad_rows in zip(spans, grads_low):
        rows = gather_rows(rows_two[lo:hi], order)
        gate = jnp.sum(
            jnp.where(column, gather_rows(gates[lo:hi], order), 0.0), axis=1, keepdims=True
        )
        act_gate = dot(rows, full_gate)
        act_up = dot(rows, full_up)
        d_plain = dot_nt(grad_rows, full_down)
        sigmoid = jax.nn.sigmoid(act_gate)
        silu_gate = act_gate * sigmoid
        hidden = silu_gate * act_up
        d_gate = jnp.sum(hidden * d_plain, axis=1, keepdims=True)
        d_hidden = d_plain * gate
        hidden_low = (hidden * gate).astype(low)
        d_gate_low = (d_hidden * act_up * (sigmoid * (1.0 + act_gate * (1.0 - sigmoid)))).astype(low)
        d_up_low = (d_hidden * silu_gate).astype(low)
        d_rows = dot_nt(d_gate_low, full_gate) + dot_nt(d_up_low, full_up)
        back_parts.append(scatter_rows(d_rows, order, low))
        d_gate_parts.append(scatter_rows(jnp.where(column, d_gate, 0.0), order, wide))
        part_down = part_down + dot_tn(hidden_low, grad_rows)
        part_gate = part_gate + dot_tn(rows, d_gate_low)
        part_up = part_up + dot_tn(rows, d_up_low)
        made_parts.append(scatter_rows(dot(hidden_low, full_down), order, low))
    output = (resid_one + jnp.concatenate(made_parts, axis=0)).astype(low)[None]
    d_gates = jnp.concatenate(d_gate_parts, axis=0)
    d_rows_two = jnp.concatenate(back_parts, axis=0)

    def owners(stack):
        kept = scatter_halves(stack, far_axes)
        got = all_to_all(team_axes, lambda other: take(kept, other))
        return gather_blocks(got, g_axes, 0).astype(jnp.float32)

    part_down = (
        part_down.reshape(parts_c, parts_far, parts_near, rows_f, model_width)
        .transpose(1, 0, 2, 3, 4)
        .reshape(parts_far, team, rows_f, model_width)
    )
    grad_down = owners(own_first(part_down, far_axes))
    grad_gate = owners(part_gate.reshape(parts_far, team, rows_d, hidden_width))
    grad_up = owners(part_up.reshape(parts_far, team, rows_d, hidden_width))

    d_rows_two = d_rows_two.reshape(count, parts_far, parts_c, parts_near * rows_d)
    d_rows_two = own_first(d_rows_two.transpose(1, 0, 2, 3), far_axes)
    d_rows_two = d_rows_two.transpose(1, 2, 0, 3).reshape(count, model_width)
    d_logits = (gates * (d_gates - jnp.sum(gates * d_gates, axis=-1, keepdims=True))).astype(low)
    part_router = dot_tn(normed_two, d_logits)
    d_normed_two = d_rows_two + dot_nt(d_logits, full_router)
    d_resid_one, d_gain_ffn = back_two(d_normed_two)
    d_resid_one = d_resid_one + cotangent[0].astype(jnp.float32)
    share_router = lax.psum_scatter(
        part_router.astype(low), c_axes + f_axes, scatter_dimension=0, tiled=True
    )
    grad_router = sum_all(share_router.astype(jnp.float32), g_axes)

    d_branch = gather_rows(d_resid_one.astype(low), c_axes)
    d_mixed = dot_nt(d_branch, w_mix).astype(low).reshape(length, kv_heads, group, width)
    part_out = dot_tn(mixed_low, d_branch)
    again_scores = (
        jnp.einsum("ikgd,jkd->kgij", query_low, keyed_low, preferred_element_type=jnp.float32)
        * scale
    )
    probs_full = jnp.where(allowed, jnp.exp(again_scores - log_total), 0.0)
    probs_again = probs_full.astype(low)
    d_probs = jnp.einsum("ikgd,jkd->kgij", d_mixed, value_low, preferred_element_type=jnp.float32)
    row_dot = jnp.sum(probs_full * d_probs, axis=-1, keepdims=True)
    d_scores = (probs_full * (d_probs - row_dot)).astype(low)
    d_query = (
        jnp.einsum("kgij,jkd->ikgd", d_scores, keyed_low, preferred_element_type=jnp.float32)
        * scale
    )
    d_keyed = (
        jnp.einsum("kgij,ikgd->jkd", d_scores, query_low, preferred_element_type=jnp.float32)
        * scale
    )
    d_value = jnp.einsum("kgij,ikgd->jkd", probs_again, d_mixed, preferred_element_type=jnp.float32)
    d_query_round = d_query.reshape(length, heads, width).astype(low).astype(jnp.float32)
    d_keyed_round = d_keyed.astype(low).astype(jnp.float32)
    d_q_lin, d_k_lin, d_gain_query, d_gain_key = back_heads((d_query_round, d_keyed_round))
    d_lin = jnp.concatenate(
        [d_q_lin.astype(low), d_k_lin.astype(low), d_value.astype(low).reshape(length, k_cols)],
        axis=1,
    )
    part_qkv = dot_tn(all_one, d_lin)
    d_one = scatter_rows(dot_nt(d_lin, w_qkv), c_axes, low)
    d_one = (
        d_one.reshape(count, parts_f, parts_c, rows_d)
        .transpose(0, 2, 1, 3)
        .reshape(count, model_width)
    )
    d_resid, d_gain_attn = back_one(d_one)
    grad_tokens = (d_resid + d_resid_one)[None]

    share_out = scatter_blocks(
        part_out.reshape(-1, groups, out_cols).transpose(1, 0, 2), g_axes
    )
    share_out = lax.psum_scatter(share_out, f_axes, scatter_dimension=0, tiled=True)
    grad_out = gather_blocks(share_out, g_axes, 1).astype(jnp.float32)
    share_qkv = scatter_blocks(
        part_qkv.reshape(model_width, groups, qkv_cols // groups).transpose(1, 0, 2), g_axes
    )
    share_qkv = lax.psum_scatter(share_qkv, f_axes, scatter_dimension=0, tiled=True)
    share_qkv = share_qkv.reshape(parts_c, rows_d, qkv_cols // groups)
    share_qkv = all_to_all(c_axes, lambda other: take(share_qkv, other))
    grad_qkv = gather_blocks(share_qkv, g_axes, 2).astype(jnp.float32).transpose(1, 0, 2)
    grad_query = grad_qkv[:, :, :q_cols].reshape(rows_d, -1)
    grad_key = grad_qkv[:, :, q_cols : q_cols + k_cols].reshape(rows_d, -1)
    grad_value = grad_qkv[:, :, q_cols + k_cols :].reshape(rows_d, -1)

    gains = sum_all(
        jnp.concatenate([d_gain_attn, d_gain_ffn, d_gain_query, d_gain_key]), all_axes
    )
    return (
        output,
        grad_tokens,
        grad_query,
        grad_key,
        grad_value,
        grad_out,
        grad_router,
        grad_gate,
        grad_up,
        grad_down,
        gains[:model_width],
        gains[model_width : 2 * model_width],
        gains[2 * model_width : 2 * model_width + width],
        gains[2 * model_width + width :],
    )


def solution(mesh):
    def binary(letter, size):
        return tuple(letter + str(step) for step in range(size.bit_length() - 1))

    g_axes = binary("g", mesh.shape["grp"])
    c_axes = binary("c", mesh.shape["ctx"])
    f_axes = binary("f", mesh.shape["fsdp"])
    names = g_axes + c_axes + f_axes
    fine = Mesh(mesh.devices.reshape((2,) * len(names)), names)
    rows = P(g_axes + f_axes, c_axes, None)
    line = P(g_axes + f_axes, None)
    split = P(c_axes + f_axes, None)
    expert = P(None, c_axes + f_axes, None)
    whole = P()
    in_specs = (
        (rows, line, line, rows)
        + (split,) * 5
        + (expert,) * 3
        + (whole,) * 4
        + (rows,)
    )
    out_specs = (rows, rows) + (split,) * 5 + (expert,) * 3 + (whole,) * 4

    def device_part(*arrays):
        return per_device(g_axes, c_axes, f_axes, *arrays)

    return jax.shard_map(
        device_part, mesh=fine, in_specs=in_specs, out_specs=out_specs, check_vma=False
    )
```

time: 5730 us -> 1810 us (0.32)
  waiting for transfers between devices: 4660 us -> 799 us
  matrix products: 549 us -> 375 us
  starting transfers between devices: 2.48 us -> 114 us
    all_gather x30 -> x2, waiting for transfers between devices: 2440 us -> 0.01 us  [the longest x1 0.01 us: per_device(): got_out = lax.all_gather(mine_out, f_axes, axis=0, tiled=True)]
    reduce_scatter x18 -> x2, waiting for transfers between devices: 1950 us -> 4.29 us  [the longest x1 4.29 us: per_device(): lax.psum_scatter(share_out, f_axes, scatter_dimension=0, tiled=True)]
    ppermute x0 -> x149, waiting for transfers between devices: none -> 795 us  [the longest x48 211 us: all_to_all(): arrived = lax.ppermute(pick(other), axes, pairs)]
    psum x1 -> x0, waiting for transfers between devices: 222 us -> none  [per_device(): lax.psum(attn_shares[0].astype(jnp.bfloat16), 'grp').astype(jnp.float32)]
    dot_general x55 -> x40, matrix products: 528 us -> 347 us  [the longest x12 101 us: dot_nt(): lax.dot_general(left, right, (((1,), (1,)), ((), ())), preferred_element_...]
    ppermute x0 -> x149, starting transfers between devices: none -> 114 us  [the longest x48 32.5 us: all_to_all(): arrived = lax.ppermute(pick(other), axes, pairs)]
    gather x12 -> x2, local copies, waits for them, and re-layouts: 79.2 us -> 1.12 us  [the longest x1 0.56 us: per_device(): jnp.take(places[0].reshape(parts_c, count), block_ids, axis=0).reshape(-1)]
    unnamed x176 -> x431, local copies, waits for them, and re-layouts: 12.1 us -> 71.8 us
  transfers between devices with their start and end apart: 50 -> 154, of which waited for: 48 -> 82; matrix products, arithmetic and copies ran while one was open for 11% -> 44% of each run, Pallas kernels for 0% -> 0%
where the time goes in v1:
time: 1810 us; the launch traced here: 1800 us
  waiting for transfers between devices  799 us (44%)
  matrix products  375 us (21%)
  other arithmetic  232 us (13%)
  local copies, waits for them, and re-layouts  227 us (13%)
  starting transfers between devices  114 us (6%)
  blocking collectives  35 us (2%)
    ppermute x48, waiting for transfers between devices, all_to_all(): arrived = lax.ppermute(pick(other), axes, pairs)  211 us
    ppermute x40, waiting for transfers between devices, scatter_rows(): arrived = lax.ppermute(rows[half:].astype(sent), axis, SWAP)  138 us
    ppermute x3, waiting for transfers between devices, scatter_halves(): arrived = lax.ppermute(stack[1].astype(low), axes[0], SWAP)  130 us
    ppermute x40, waiting for transfers between devices, gather_rows(): rows = jnp.concatenate([rows, lax.ppermute(rows, axis, SWAP)], axis=0)  129 us
    dot_general x12, matrix products, dot_nt(): lax.dot_general(left, right, (((1,), (1,)), ((), ())), preferred_element_...  101 us
    dot_general x12, matrix products, dot_tn(): lax.dot_general(left, right, (((0,), (0,)), ((), ())), preferred_element_...  94 us
    ppermute x7, waiting for transfers between devices, gather_blocks(): other = lax.ppermute(block, axes[0], SWAP)  88.1 us
    dot_general x12, matrix products, dot(): return jnp.dot(left, right, preferred_element_type=jnp.float32)  79.7 us
  transfers between devices with their start and end apart: 154, of which 82 were waited for; matrix products, arithmetic and copies ran while one was open for 44% of the time, Pallas kernels for 0%

profile of v1, /device:TPU:0, one launch (start us, length us, event | category | flops | bytes accessed | tf_op | source)
XLA Modules:
  0.0 1799.3 jit_solution(11514312358188084944)
XLA Ops:
  52.1 35.0 %all_gather.11 = bf16[2048,16]{0,1:T(8,128)(2,1)} all-gather(bf16[128,16]{0,1:T(8,128)(2,1)S(1)} %copy-done.163), channel_id=1, replica_groups=mesh['g0'=2,'c0'=2,'c1'=2,'f0'=2,'f1'=2] {'c0','c1','f0','f1'}, dimensions={0}, use_global_device_ids=true | all-gather | bytes 69632 | tf_op jit(solution)/shard_map/all_gather | solution.py:225
  108.4 20.1 %collective-permute-done.35 = bf16[48,2048]{1,0:T(8,128)(2,1)S(1)} collective-permute-done((bf16[48,2048]{1,0:T(8,128)(2,1)}, bf16[48,2048]{1,0:T(8,128)(2,1)S(1)}, u32[]{:S(2)}, u32[]{:S(2)}) %collective-permute-start.35) | collective-permute-done | bytes 196640 | tf_op jit(solution)/shard_map/ppermute | solution.py:87
  138.5 15.4 collective-permute-done.37
  287.7 25.1 %collective-permute-done.6 = bf16[1024,1024]{1,0:T(8,128)(2,1)} collective-permute-done((bf16[1024,1024]{1,0:T(8,128)(2,1)}, bf16[1024,1024]{1,0:T(8,128)(2,1)}, u32[]{:S(2)}, u32[]{:S(2)}) %collective-permute-start.6) | collective-permute-done | bytes 2097184 | tf_op jit(solution)/shard_map/ppermute | solution.py:101
  316.9 50.0 %collective-permute-done.5 = bf16[2048,640]{1,0:T(8,128)(2,1)S(1)} collective-permute-done((bf16[2048,640]{1,0:T(8,128)(2,1)}, bf16[2048,640]{1,0:T(8,128)(2,1)S(1)}, u32[]{:S(2)}, u32[]{:S(2)}) %collective-permute-start.5) | collective-permute-done | bytes 2621472 | tf_op jit(solution)/shard_map/ppermute | solution.py:101
  396.4 14.3 fusion.5
  410.8 14.2 fusion.6
  425.0 17.3 fusion.39
  449.6 26.5 %collective-permute-done.40 = bf16[8,48,2048]{2,1,0:T(8,128)(2,1)} collective-permute-done((bf16[8,48,2048]{2,1,0:T(8,128)(2,1)}, bf16[8,48,2048]{2,1,0:T(8,128)(2,1)}, u32[]{:S(2)}, u32[]{:S(2)}) %collective-permute-start.40) | collective-permute-done | bytes 1572896 | tf_op jit(solution)/shard_map/ppermute | solution.py:120
  494.3 16.9 collective-permute-done.71
  520.7 19.3 %collective-permute-done.8 = bf16[256,2048]{1,0:T(8,128)(2,1)S(1)} collective-permute-done((bf16[256,2048]{1,0:T(8,128)(2,1)S(1)}, bf16[256,2048]{1,0:T(8,128)(2,1)S(1)}, u32[]{:S(2)}, u32[]{:S(2)}) %collective-permute-start.8) | collective-permute-done | bytes 1048608 | tf_op jit(solution)/shard_map/ppermute | solution.py:73
  580.2 25.2 %collective-permute-done.59 = bf16[320,2048]{1,0:T(8,128)(2,1)S(1)} collective-permute-done((bf16[320,2048]{1,0:T(8,128)(2,1)S(1)}, bf16[320,2048]{1,0:T(8,128)(2,1)S(1)}, u32[]{:S(2)}, u32[]{:S(2)}) %collective-permute-start.59) | collective-permute-done | bytes 1310752 | tf_op jit(solution)/shard_map/ppermute | solution.py:66
  620.5 16.7 collective-permute-done.47
  987.5 67.8 %collective-permute-done.135 = bf16[8,48,2048]{2,1,0:T(8,128)(2,1)} collective-permute-done((bf16[8,48,2048]{2,1,0:T(8,128)(2,1)}, bf16[8,48,2048]{2,1,0:T(8,128)(2,1)}, u32[]{:S(2)}, u32[]{:S(2)}) %collective-permute-start.135) | collective-permute-done | bytes 1572896 | tf_op jit(solution)/shard_map/ppermute | solution.py:128
  1057.7 31.3 %collective-permute-done.117 = bf16[8,128,768]{2,1,0:T(8,128)(2,1)} collective-permute-done((bf16[8,128,768]{2,1,0:T(8,128)(2,1)}, bf16[8,128,768]{2,1,0:T(8,128)(2,1)}, u32[]{:S(2)}, u32[]{:S(2)}) %collective-permute-start.117) | collective-permute-done | bytes 1572896 | tf_op jit(solution)/shard_map/ppermute | solution.py:128
  1091.1 31.2 %collective-permute-done.126 = bf16[8,128,768]{2,1,0:T(8,128)(2,1)} collective-permute-done((bf16[8,128,768]{2,1,0:T(8,128)(2,1)}, bf16[8,128,768]{2,1,0:T(8,128)(2,1)}, u32[]{:S(2)}, u32[]{:S(2)}) %collective-permute-start.126) | collective-permute-done | bytes 1572896 | tf_op jit(solution)/shard_map/ppermute | solution.py:128
  1249.9 21.7 %collective-permute-done.90 = bf16[320,2048]{1,0:T(8,128)(2,1)S(1)} collective-permute-done((bf16[320,2048]{1,0:T(8,128)(2,1)}, bf16[320,2048]{1,0:T(8,128)(2,1)S(1)}, u32[]{:S(2)}, u32[]{:S(2)}) %collective-permute-start.90) | collective-permute-done | bytes 1310752 | tf_op jit(solution)/shard_map/ppermute | solution.py:73
  1290.4 18.4 %collective-permute-done.74 = bf16[384,2048]{1,0:T(8,128)(2,1)S(1)} collective-permute-done((bf16[384,2048]{1,0:T(8,128)(2,1)S(1)}, bf16[384,2048]{1,0:T(8,128)(2,1)S(1)}, u32[]{:S(2)}, u32[]{:S(2)}) %collective-permute-start.74) | collective-permute-done | bytes 1572896 | tf_op jit(solution)/shard_map/ppermute | solution.py:73
  1328.7 16.1 collective-permute-done.75
  1430.1 15.8 fusion.54
  1445.8 28.3 %fusion = (f32[8,1024]{1,0:T(8,128)S(1)}, f32[1024,1024,8]{1,0,2:T(8,128)}) fusion(f32[1024,1024,8]{1,0,2:T(8,128)} %get-tuple-element.239, f32[8,1024]{1,0:T(8,128)S(1)} %copy-done.100, pred[1024,1024]{0,1:T(8,128)(4,1)S(1)} %copy-done.5, bf16[1024,8,128]{0,2,1:T(8,128)(2,1)} %bitcast.570, f32[1024,1280]{1,0:T(8,128)} %copy-done.24), kind=kOutput, calls=%fused_computation.4 | convolution fusion | flops 2189418496 | bytes 70582272 | tf_op jit(solution)/shard_map/ikgd,jkd->kgij/dot_general | solution.py:371
  1474.1 28.7 %fusion.9 = bf16[8,1024,1024]{1,2,0:T(8,128)(2,1)} fusion(f32[1024,1024,8]{1,0,2:T(8,128)} %get-tuple-element.250, f32[1024,1024,8]{1,0,2:T(8,128)} %get-tuple-element.239, f32[8,1024]{1,0:T(8,128)S(1)} %get-tuple-element.249, f32[8,1024]{1,0:T(8,128)S(1)} %copy-done.100, pred[1024,1024]{0,1:T(8,128)(4,1)S(1)} %copy-done.5), kind=kLoop, calls=%fused_computation.17 | loop fusion | flops 50331648 | bytes 85000192 | tf_op jit(solution)/shard_map/reshape.28
  1582.8 35.1 %collective-permute-done.109 = bf16[2048,640]{0,1:T(8,128)(2,1)S(1)} collective-permute-done((bf16[2048,640]{0,1:T(8,128)(2,1)S(1)}, bf16[2048,640]{0,1:T(8,128)(2,1)S(1)}, u32[]{:S(2)}, u32[]{:S(2)}) %collective-permute-start.109) | collective-permute-done | bytes 2621472 | tf_op jit(solution)/shard_map/ppermute | solution.py:138
  1678.1 32.0 %collective-permute-done.114 = bf16[1024,1024]{1,0:T(8,128)(2,1)S(1)} collective-permute-done((bf16[1024,1024]{1,0:T(8,128)(2,1)S(1)}, bf16[1024,1024]{1,0:T(8,128)(2,1)S(1)}, u32[]{:S(2)}, u32[]{:S(2)}) %collective-permute-start.114) | collective-permute-done | bytes 2097184 | tf_op jit(solution)/shard_map/ppermute | solution.py:138
  (1100 shorter events, 1159.4 us)
Async XLA Ops:
  7.2 247.3 %all-gather.6.cloned.1.call-start = ((), (), s32[]{:S(2)}) async-start(), calls=%async_computation.6 | async-start | bytes 2621440 | tf_op jit(solution)/shard_map/all_gather | solution.py:223
  8.3 251.2 %collective-permute-start.69 = (bf16[96,2048]{1,0:T(8,128)(2,1)S(1)}, bf16[96,2048]{1,0:T(8,128)(2,1)S(1)}, u32[]{:S(2)}, u32[]{:S(2)}) collective-permute-start(bf16[96,2048]{1,0:T(8,128)(2,1)S(1)} %slice_bitcast_fusion.3), channel_id=1, source_target_pairs={{0,16},{16,0},{1,17},{17,1},{2,18},{18,2},{3,19},{19,3},{4,20},{20... | collective-permute-start | bytes 1179656 | tf_op jit(solution)/shard_map/ppermute | solution.py:66
  13.2 232.5 %collective-permute-start.77 = (bf16[80,2048]{1,0:T(8,128)(2,1)}, bf16[80,2048]{1,0:T(8,128)(2,1)}, u32[]{:S(2)}, u32[]{:S(2)}) collective-permute-start(bf16[80,2048]{1,0:T(8,128)(2,1)} %get-tuple-element.214), channel_id=1, source_target_pairs={{0,8},{8,0},{1,9},{9,1},{2,10},{10,2},{3,11},{11,3},{4,12},{12,4},... | collective-permute-start | bytes 983048 | tf_op jit(solution)/shard_map/ppermute | solution.py:66
  14.7 233.3 %collective-permute-start.85 = (bf16[80,2048]{1,0:T(8,128)(2,1)S(1)}, bf16[80,2048]{1,0:T(8,128)(2,1)}, u32[]{:S(2)}, u32[]{:S(2)}) collective-permute-start(bf16[80,2048]{1,0:T(8,128)(2,1)S(1)} %get-tuple-element.215), channel_id=1, source_target_pairs={{0,1},{1,0},{2,3},{3,2},{4,5},{5,4},{6,7},{7,6},{8,9},{9,8},{10,11... | collective-permute-start | bytes 983048 | tf_op jit(solution)/shard_map/ppermute | solution.py:66
  24.4 235.1 %all-gather.4.cloned.1.call-start = ((), (), s32[]{:S(2)}) async-start(), calls=%async_computation.3 | async-start | bytes 3276800 | tf_op jit(solution)/shard_map/all_gather | solution.py:217
  98.8 868.7 %reduce-scatter.10.cloned.1.call-start = ((), (), s32[]{:S(2)}) async-start(), calls=%async_computation.7 | async-start | bytes 557056
  273.4 206.7 %collective-permute-start.20 = (bf16[8,128,768]{2,1,0:T(8,128)(2,1)}, bf16[8,128,768]{2,1,0:T(8,128)(2,1)}, u32[]{:S(2)}, u32[]{:S(2)}) collective-permute-start(bf16[8,128,768]{2,1,0:T(8,128)(2,1)} %bitcast_dynamic-update-slice_fusion.35), channel_id=1, source_target_pairs={{0,2},{2,0},{1,3},{3,1},{4,6},{6,4},{5,7},{7,5},{8,10},{10,8},{9,1... | collective-permute-start | bytes 4718600 | tf_op jit(solution)/shard_map/ppermute | solution.py:120
  285.5 202.0 %collective-permute-start.28 = (bf16[8,128,768]{2,1,0:T(8,128)(2,1)}, bf16[8,128,768]{2,1,0:T(8,128)(2,1)}, u32[]{:S(2)}, u32[]{:S(2)}) collective-permute-start(bf16[8,128,768]{2,1,0:T(8,128)(2,1)} %bitcast_dynamic-update-slice_fusion.28), channel_id=1, source_target_pairs={{0,2},{2,0},{1,3},{3,1},{4,6},{6,4},{5,7},{7,5},{8,10},{10,8},{9,1... | collective-permute-start | bytes 4718600 | tf_op jit(solution)/shard_map/ppermute | solution.py:120
  312.8 163.2 %collective-permute-start.40 = (bf16[8,48,2048]{2,1,0:T(8,128)(2,1)}, bf16[8,48,2048]{2,1,0:T(8,128)(2,1)}, u32[]{:S(2)}, u32[]{:S(2)}) collective-permute-start(bf16[8,48,2048]{2,1,0:T(8,128)(2,1)} %bitcast_dynamic-update-slice_fusion.21), channel_id=1, source_target_pairs={{0,2},{2,0},{1,3},{3,1},{4,6},{6,4},{5,7},{7,5},{8,10},{10,8},{9,1... | collective-permute-start | bytes 4718600 | tf_op jit(solution)/shard_map/ppermute | solution.py:120
  761.5 988.6 %reduce-scatter.6.cloned.1.call-start = ((), (), s32[]{:S(2)}) async-start(), calls=%async_computation.4 | async-start | bytes 3276800 | tf_op jit(solution)/shard_map/reduce_scatter | solution.py:408
  823.2 558.8 %collective-permute-start.65 = (bf16[640,2048]{1,0:T(8,128)(2,1)}, bf16[640,2048]{1,0:T(8,128)(2,1)}, u32[]{:S(2)}, u32[]{:S(2)}) collective-permute-start(bf16[640,2048]{1,0:T(8,128)(2,1)} %slice.717), channel_id=1, source_target_pairs={{0,4},{4,0},{1,5},{5,1},{2,6},{6,2},{3,7},{7,3},{8,12},{12,8},{9,1... | collective-permute-start | bytes 7864328 | tf_op jit(solution)/shard_map/ppermute | solution.py:73
  916.3 139.1 %collective-permute-start.135 = (bf16[8,48,2048]{2,1,0:T(8,128)(2,1)}, bf16[8,48,2048]{2,1,0:T(8,128)(2,1)}, u32[]{:S(2)}, u32[]{:S(2)}) collective-permute-start(bf16[8,48,2048]{2,1,0:T(8,128)(2,1)} %fusion.45), channel_id=1, source_target_pairs={{0,2},{2,0},{1,3},{3,1},{4,6},{6,4},{5,7},{7,5},{8,10},{10,8},{9,1... | collective-permute-start | bytes 4718600 | tf_op jit(solution)/shard_map/ppermute | solution.py:128
  953.6 135.5 %collective-permute-start.117 = (bf16[8,128,768]{2,1,0:T(8,128)(2,1)}, bf16[8,128,768]{2,1,0:T(8,128)(2,1)}, u32[]{:S(2)}, u32[]{:S(2)}) collective-permute-start(bf16[8,128,768]{2,1,0:T(8,128)(2,1)} %bitcast.144), channel_id=1, source_target_pairs={{0,2},{2,0},{1,3},{3,1},{4,6},{6,4},{5,7},{7,5},{8,10},{10,8},{9,1... | collective-permute-start | bytes 4718600 | tf_op jit(solution)/shard_map/ppermute | solution.py:128
  954.7 167.6 %collective-permute-start.126 = (bf16[8,128,768]{2,1,0:T(8,128)(2,1)}, bf16[8,128,768]{2,1,0:T(8,128)(2,1)}, u32[]{:S(2)}, u32[]{:S(2)}) collective-permute-start(bf16[8,128,768]{2,1,0:T(8,128)(2,1)} %bitcast.160), channel_id=1, source_target_pairs={{0,2},{2,0},{1,3},{3,1},{4,6},{6,4},{5,7},{7,5},{8,10},{10,8},{9,1... | collective-permute-start | bytes 4718600 | tf_op jit(solution)/shard_map/ppermute | solution.py:128
  986.9 244.2 %collective-permute-start.89 = (bf16[640,2048]{1,0:T(8,128)(2,1)S(1)}, bf16[640,2048]{1,0:T(8,128)(2,1)S(1)}, u32[]{:S(2)}, u32[]{:S(2)}) collective-permute-start(bf16[640,2048]{1,0:T(8,128)(2,1)S(1)} %copy-done.77), channel_id=1, source_target_pairs={{0,4},{4,0},{1,5},{5,1},{2,6},{6,2},{3,7},{7,3},{8,12},{12,8},{9,1... | collective-permute-start | bytes 7864328 | tf_op jit(solution)/shard_map/ppermute | solution.py:73
  1055.3 183.3 %collective-permute-start.81 = (bf16[640,2048]{1,0:T(8,128)(2,1)S(1)}, bf16[640,2048]{1,0:T(8,128)(2,1)S(1)}, u32[]{:S(2)}, u32[]{:S(2)}) collective-permute-start(bf16[640,2048]{1,0:T(8,128)(2,1)S(1)} %copy-done.76), channel_id=1, source_target_pairs={{0,4},{4,0},{1,5},{5,1},{2,6},{6,2},{3,7},{7,3},{8,12},{12,8},{9,1... | collective-permute-start | bytes 7864328 | tf_op jit(solution)/shard_map/ppermute | solution.py:73
  1089.0 155.2 %collective-permute-start.73 = (bf16[768,2048]{1,0:T(8,128)(2,1)S(1)}, bf16[768,2048]{1,0:T(8,128)(2,1)S(1)}, u32[]{:S(2)}, u32[]{:S(2)}) collective-permute-start(bf16[768,2048]{1,0:T(8,128)(2,1)S(1)} %slice.713), channel_id=1, source_target_pairs={{0,4},{4,0},{1,5},{5,1},{2,6},{6,2},{3,7},{7,3},{8,12},{12,8},{9,1... | collective-permute-start | bytes 9437192 | tf_op jit(solution)/shard_map/ppermute | solution.py:73
  1231.0 174.0 %collective-permute-start.53 = (bf16[640,2048]{1,0:T(8,128)(2,1)}, bf16[640,2048]{1,0:T(8,128)(2,1)}, u32[]{:S(2)}, u32[]{:S(2)}) collective-permute-start(bf16[640,2048]{1,0:T(8,128)(2,1)} %slice.718), channel_id=1, source_target_pairs={{0,4},{4,0},{1,5},{5,1},{2,6},{6,2},{3,7},{7,3},{8,12},{12,8},{9,1... | collective-permute-start | bytes 7864328 | tf_op jit(solution)/shard_map/ppermute | solution.py:73
  1382.1 176.0 %collective-permute-start.125 = (bf16[8,128,768]{2,1,0:T(8,128)(2,1)}, bf16[8,128,768]{2,1,0:T(8,128)(2,1)}, u32[]{:S(2)}, u32[]{:S(2)}) collective-permute-start(bf16[8,128,768]{2,1,0:T(8,128)(2,1)} %bitcast_dynamic-update-slice_fusion.14), channel_id=1, source_target_pairs={{0,16},{16,0},{1,17},{17,1},{2,18},{18,2},{3,19},{19,3},{4,20},{20... | collective-permute-start | bytes 4718600 | tf_op jit(solution)/shard_map/ppermute | solution.py:101
  1402.0 159.1 %collective-permute-start.134 = (bf16[8,128,768]{2,1,0:T(8,128)(2,1)}, bf16[8,128,768]{2,1,0:T(8,128)(2,1)}, u32[]{:S(2)}, u32[]{:S(2)}) collective-permute-start(bf16[8,128,768]{2,1,0:T(8,128)(2,1)} %bitcast_dynamic-update-slice_fusion.7), channel_id=1, source_target_pairs={{0,16},{16,0},{1,17},{17,1},{2,18},{18,2},{3,19},{19,3},{4,20},{20... | collective-permute-start | bytes 4718600 | tf_op jit(solution)/shard_map/ppermute | solution.py:101
  1412.1 161.5 %collective-permute-start.66 = (bf16[320,2048]{1,0:T(8,128)(2,1)}, bf16[320,2048]{1,0:T(8,128)(2,1)}, u32[]{:S(2)}, u32[]{:S(2)}) collective-permute-start(bf16[320,2048]{1,0:T(8,128)(2,1)} %slice.727), channel_id=1, source_target_pairs={{0,8},{8,0},{1,9},{9,1},{2,10},{10,2},{3,11},{11,3},{4,12},{12,4},... | collective-permute-start | bytes 3932168 | tf_op jit(solution)/shard_map/ppermute | solution.py:73
  1418.3 159.5 %collective-permute-start.54 = (bf16[320,2048]{1,0:T(8,128)(2,1)}, bf16[320,2048]{1,0:T(8,128)(2,1)}, u32[]{:S(2)}, u32[]{:S(2)}) collective-permute-start(bf16[320,2048]{1,0:T(8,128)(2,1)} %slice.728), channel_id=1, source_target_pairs={{0,16},{16,0},{1,17},{17,1},{2,18},{18,2},{3,19},{19,3},{4,20},{20... | collective-permute-start | bytes 3932168 | tf_op jit(solution)/shard_map/ppermute | solution.py:73
  1421.3 246.2 %collective-permute-start.42 = (bf16[384,2048]{1,0:T(8,128)(2,1)}, bf16[384,2048]{1,0:T(8,128)(2,1)}, u32[]{:S(2)}, u32[]{:S(2)}) collective-permute-start(bf16[384,2048]{1,0:T(8,128)(2,1)} %slice.724), channel_id=1, source_target_pairs={{0,1},{1,0},{2,3},{3,2},{4,5},{5,4},{6,7},{7,6},{8,9},{9,8},{10,11... | collective-permute-start | bytes 4718600 | tf_op jit(solution)/shard_map/ppermute | solution.py:73
  1620.4 136.2 %reduce-scatter.8.cloned.1.call-start = ((), (), s32[]{:S(2)}) async-start(), calls=%async_computation.5 | async-start | bytes 2621440 | tf_op jit(solution)/shard_map/reduce_scatter | solution.py:403
  (330 other events, 7608.7 us)
Sparse Core Ops, SparseCore 0:
  24.5 46.2 all-gather.5
  98.9 61.3 all-gather.3
  761.6 54.5 reduce-scatter.9
  1620.6 57.5 reduce-scatter.5
  1712.6 43.9 reduce-scatter.7

commit v2 on v1

v2 whole, which is shorter than its diff:
```python
import functools
import math

import jax
import jax.numpy as jnp
from jax import lax
from jax.experimental import pallas as pl
from jax.experimental.pallas import tpu as pltpu
from jax.sharding import Mesh
from jax.sharding import PartitionSpec as P

epsilon = 1e-06
low = jnp.bfloat16
wide = jnp.float32
SWAP = [(0, 1), (1, 0)]
ROW_TILE = 16
MIB = 1 << 20
WAIT_LAST = 8
BRIEF = pl.CostEstimate(flops=0, bytes_accessed=MIB, transcendentals=0)


def normed(values, gain):
    return values * lax.rsqrt(jnp.mean(values * values, axis=-1, keepdims=True) + epsilon) * gain


def angles(place, width):
    steps = jnp.arange(width // 2).astype(jnp.float32)
    inverse = jnp.exp(steps * (-2.0 * math.log(1000000.0) / width))
    return place.astype(jnp.float32)[:, None] * inverse[None, :]


def dot(left, right):
    return jnp.dot(left, right, preferred_element_type=jnp.float32)


def dot_nt(left, right):
    return lax.dot_general(left, right, (((1,), (1,)), ((), ())), preferred_element_type=jnp.float32)


def dot_tn(left, right):
    return lax.dot_general(left, right, (((0,), (0,)), ((), ())), preferred_element_type=jnp.float32)


def after(value, *anchors):
    return lax.optimization_barrier((value,) + anchors)[0]


def flat_index(axes):
    index = 0
    for axis in axes:
        index = index * 2 + lax.axis_index(axis)
    return index


def take(stack, index):
    return lax.dynamic_index_in_dim(stack, index, 0, keepdims=False)


def take_at(stack, index, at):
    return lax.dynamic_index_in_dim(stack, index, at, keepdims=False)


def exchange(axes, pick):
    amount = 1 << len(axes)
    here = flat_index(axes)
    arrived = [pick(here)]
    for step in range(1, amount):
        pairs = [(place, place ^ step) for place in range(amount)]
        arrived.append(lax.ppermute(pick(jnp.bitwise_xor(here, step)), axes, pairs))
    return arrived


def laid_out(blocks, here, at):
    if len(blocks) == 1:
        return jnp.expand_dims(blocks[0], at)
    if len(blocks) == 2:
        first = here == 0
        return jnp.stack(
            [jnp.where(first, blocks[0], blocks[1]), jnp.where(first, blocks[1], blocks[0])], axis=at
        )
    one = blocks[0]
    held = jnp.zeros(one.shape[:at] + (len(blocks),) + one.shape[at:], one.dtype)
    for step, block in enumerate(blocks):
        held = lax.dynamic_update_index_in_dim(held, block, jnp.bitwise_xor(here, step), at)
    return held


def sems(amount):
    return pltpu.SemaphoreType.DMA((amount,))


def toward(flips):
    return {axis: 1 - lax.axis_index(axis) for axis in flips}


def remote(src, dst, send, recv, flips):
    return pltpu.make_async_remote_copy(
        src_ref=src,
        dst_ref=dst,
        send_sem=send,
        recv_sem=recv,
        device_id=toward(flips),
        device_id_type=pl.DeviceIdType.MESH,
    )


class Direct:
    def __init__(self, axes, operand, block, pick, rounds=0):
        self.axes, self.block, self.pick, self.rounds = axes, block, pick, rounds
        self.amount = 1 << len(axes)
        self.operands = [operand]
        self.results = [jax.ShapeDtypeStruct((self.amount,) + block, operand.dtype)]
        self.scratch = [
            sems(self.amount),
            sems(self.amount),
            sems(2),
            pltpu.VMEM(block, operand.dtype),
        ]
        self.steps = [
            tuple(axis for bit, axis in enumerate(reversed(axes)) if step >> bit & 1)
            for step in range(self.amount)
        ]
        self.flips = self.steps[1:]

    def begin(self, operands, target, send, recv):
        copies = []
        for step in range(1, self.amount):
            other = 0
            for axis in self.axes:
                place = lax.axis_index(axis)
                other = other * 2 + (1 - place if axis in self.steps[step] else place)
            copy = remote(
                operands[0].at[self.pick(other)],
                target,
                send.at[step],
                recv.at[step],
                self.steps[step],
            )
            copy.start()
            copies.append(copy)
        return copies

    def keep(self, operands, target, local, held):
        load = pltpu.make_async_copy(
            operands[0].at[self.pick(flat_index(self.axes))], held, local.at[0]
        )
        load.start()
        load.wait()
        store = pltpu.make_async_copy(held, target, local.at[1])
        store.start()
        store.wait()

    def run(self, operands, results, scratch):
        send, recv, local, held = scratch
        for _ in range(self.rounds):
            yield
        target = results[0].at[flat_index(self.axes)]
        copies = self.begin(operands, target, send, recv)
        self.keep(operands, target, local, held)
        for _ in range(WAIT_LAST):
            yield
        for copy in copies:
            copy.wait()


class Spread(Direct):
    def __init__(self, axes, others, operand, block):
        super().__init__(axes, operand, block, lambda place: place)
        self.others = others
        self.results = [
            jax.ShapeDtypeStruct((self.amount,) + (2,) * len(others) + block, operand.dtype)
        ]
        self.scratch += [sems(max(1, len(others))), sems(max(1, len(others)))]
        self.flips = self.flips + [(axis,) for axis in others]

    def run(self, operands, results, scratch):
        send, recv, local, held, next_send, next_recv = scratch
        here = flat_index(self.axes)
        place = {axis: lax.axis_index(axis) for axis in self.others}
        spot = tuple(place[axis] for axis in self.others)
        copies = self.begin(operands, results[0].at[(here,) + spot], send, recv)
        self.keep(operands, results[0].at[(here,) + spot], local, held)
        yield
        for copy in copies:
            copy.wait_recv()
        for stage, axis in enumerate(self.others):
            region = tuple(
                slice(None) if other in self.others[:stage] else place[other]
                for other in self.others
            )
            region = results[0].at[(slice(None),) + region]
            copy = remote(region, region, next_send.at[stage], next_recv.at[stage], (axis,))
            copy.start()
            yield
            copy.wait()
        for copy in copies:
            copy.wait_send()


class Gather:
    def __init__(self, axes, operand, parts):
        self.axes, self.parts = axes, parts
        self.operands = [operand]
        self.results = [
            jax.ShapeDtypeStruct((2,) * len(axes) + operand.shape, operand.dtype)
        ]
        amount = len(parts) * len(axes)
        self.scratch = [sems(amount), sems(amount), sems(2), pltpu.VMEM(operand.shape, operand.dtype)]
        self.flips = [(axis,) for axis in axes]

    def run(self, operands, results, scratch):
        send, recv, local, held = scratch
        place = {axis: lax.axis_index(axis) for axis in self.axes}
        load = pltpu.make_async_copy(operands[0], held, local.at[0])
        load.start()
        load.wait()
        spot = tuple(place[axis] for axis in self.axes)
        store = pltpu.make_async_copy(held, results[0].at[spot], local.at[1])
        store.start()
        store.wait()
        copies = {}

        def start(number, stage):
            lo, hi, order = self.parts[number]
            region = tuple(
                slice(None) if axis in order[:stage] else place[axis] for axis in self.axes
            )
            region = results[0].at[region + (pl.ds(lo, hi - lo),)]
            slot = number * len(self.axes) + stage
            copies[number, stage] = remote(
                region, region, send.at[slot], recv.at[slot], (order[stage],)
            )
            copies[number, stage].start()

        for number in range(len(self.parts)):
            start(number, 0)
        yield
        for stage in range(1, len(self.axes)):
            for number in range(len(self.parts)):
                copies[number, stage - 1].wait_recv()
                start(number, stage)
            yield
        for number in range(len(self.parts)):
            copies[number, len(self.axes) - 1].wait_recv()
        for copy in copies.values():
            copy.wait_send()


class Reduce:
    def __init__(self, axes, operand, parts, owners=()):
        self.axes, self.parts, self.owners = axes, parts, owners
        count, columns = operand.shape[-2:]
        self.operands = [operand]
        self.results = [jax.ShapeDtypeStruct((count, columns), low if owners else wide)]
        self.scratch = []
        for lo, hi, order in parts:
            for stage in range(len(axes)):
                left = len(axes) - 1 - stage
                self.scratch.append(pltpu.VMEM((2,) * left + (hi - lo, columns), low))
            self.scratch.append(pltpu.VMEM((2,) * (len(axes) - 1) + (hi - lo, columns), low))
        self.scratch.append(pltpu.VMEM((count, columns), wide))
        amount = len(parts) * len(axes)
        self.flips = [(axis,) for axis in axes]
        self.last = None
        if owners:
            block = (count >> len(owners), columns)
            shape = jax.ShapeDtypeStruct((1 << len(owners),) + block, low)
            self.last = Direct(owners, shape, block, lambda place: place)
            self.results = self.last.results
            self.flips = self.flips + self.last.flips
            self.scratch += [pltpu.VMEM(shape.shape, low)] + self.last.scratch
        self.scratch += [sems(amount), sems(amount), sems(len(parts) + 1)]

    def run(self, operands, results, scratch):
        stages = len(self.axes)
        send, recv, local = scratch[-3:]
        total = scratch[len(self.parts) * (stages + 1)]
        place = {axis: lax.axis_index(axis) for axis in self.axes}
        copies, loads = {}, []

        def buffers(number):
            base = number * (stages + 1)
            return scratch[base : base + stages], scratch[base + stages]

        def start(number, stage):
            lo, hi, order = self.parts[number]
            slots, held = buffers(number)
            slot = number * stages + stage
            axis = order[stage]
            if stage == 0:
                spot = tuple(
                    1 - place[other] if other == axis else slice(None) for other in self.axes
                )
                source = operands[0].at[spot + (pl.ds(lo, hi - lo),)]
            else:
                rest = [other for other in self.axes if other != order[0]]
                spot = tuple(
                    place[other]
                    if other in order[:stage]
                    else 1 - place[other]
                    if other == axis
                    else slice(None)
                    for other in rest
                )
                source = held.at[spot]
            copies[number, stage] = remote(
                source, slots[stage], send.at[slot], recv.at[slot], (axis,)
            )
            copies[number, stage].start()

        for number, (lo, hi, order) in enumerate(self.parts):
            start(number, 0)
            spot = tuple(
                place[other] if other == order[0] else slice(None) for other in self.axes
            )
            load = pltpu.make_async_copy(
                operands[0].at[spot + (pl.ds(lo, hi - lo),)], buffers(number)[1], local.at[number]
            )
            load.start()
            loads.append(load)
        yield
        for stage in range(stages):
            for number, (lo, hi, order) in enumerate(self.parts):
                slots, held = buffers(number)
                if stage == 0:
                    loads[number].wait()
                copies[number, stage].wait_recv()
                rest = [other for other in self.axes if other != order[0]]
                gone = order[: stage + 1]
                free = [other for other in rest if other not in gone]
                for code in range(1 << len(free)):
                    bits = {axis: code >> bit & 1 for bit, axis in enumerate(free)}
                    spot = tuple(bits[axis] if axis in bits else place[axis] for axis in rest)
                    slot_spot = tuple(bits[axis] for axis in free)
                    last = stage == stages - 1

                    def add(step, carry, spot=spot, slot_spot=slot_spot, last=last):
                        rows = pl.ds(pl.multiple_of(step * ROW_TILE, ROW_TILE), ROW_TILE)
                        value = held[spot + (rows,)].astype(wide)
                        value = value + slots[stage][slot_spot + (rows,)].astype(wide)
                        if last:
                            at = pl.multiple_of(step * ROW_TILE + lo, ROW_TILE)
                            total[pl.ds(at, ROW_TILE)] = value
                        else:
                            held[spot + (rows,)] = value.astype(low)
                        return carry

                    lax.fori_loop(0, (hi - lo) // ROW_TILE, add, 0)
                if stage + 1 < stages:
                    start(number, stage + 1)
            yield
        if self.last is None:
            store = pltpu.make_async_copy(total, results[0], local.at[len(self.parts)])
            store.start()
            store.wait()
        else:
            ready, *others = scratch[len(self.parts) * (stages + 1) + 1 : -3]
            ready[...] = total[...].astype(low).reshape(ready.shape)
            yield from self.last.run([ready], results, others)
        for copy in copies.values():
            copy.wait_send()


def flow_kernel(flows, *refs):
    refs = list(refs)

    def cut(amount):
        part = refs[:amount]
        del refs[:amount]
        return part

    operands = [cut(len(flow.operands)) for flow in flows]
    results = [cut(len(flow.results)) for flow in flows]
    scratch = [cut(len(flow.scratch)) for flow in flows]
    partners = []
    for flow in flows:
        partners += [flips for flips in flow.flips if flips not in partners]
    barrier = pltpu.get_barrier_semaphore()
    for flips in partners:
        pl.semaphore_signal(
            barrier, inc=1, device_id=toward(flips), device_id_type=pl.DeviceIdType.MESH
        )
    pl.semaphore_wait(barrier, len(partners))
    running = [flow.run(*parts) for flow, *parts in zip(flows, operands, results, scratch)]
    while running:
        running = [run for run in running if next(run, run) is not run]


def transfer(number, flows):
    arrays = [array for flow in flows for array in flow.operands]
    shapes = [shape for flow in flows for shape in flow.results]
    anywhere = pl.BlockSpec(memory_space=pl.ANY)
    return pl.pallas_call(
        functools.partial(flow_kernel, flows),
        out_shape=shapes,
        in_specs=[anywhere] * len(arrays),
        out_specs=[anywhere] * len(shapes),
        scratch_shapes=[one for flow in flows for one in flow.scratch],
        compiler_params=pltpu.CompilerParams(
            collective_id=number, has_side_effects=True, vmem_limit_bytes=52 * MIB
        ),
        cost_estimate=BRIEF,
    )(*arrays)


def gather_blocks(block, axes, at):
    if not axes:
        return block
    if len(axes) > 1:
        return lax.all_gather(block, axes, axis=at, tiled=True)
    other = lax.ppermute(block, axes[0], SWAP)
    first = lax.axis_index(axes[0]) == 0
    return jnp.concatenate(
        [jnp.where(first, block, other), jnp.where(first, other, block)], axis=at
    )


def sum_all(value, axes):
    for axis in axes:
        value = value + lax.ppermute(value, axis, SWAP)
    return value


def tile_of(rows, most):
    steps = -(-rows // most)
    while rows % steps or (rows // steps) % ROW_TILE:
        steps += 1
    return rows // steps


def whole_block(shape):
    return pl.BlockSpec(shape, lambda *ids: (0,) * len(shape), pipeline_mode=pl.Buffered(1))


def expert_kernel(
    rows_ref,
    grad_ref,
    gate_ref,
    in_ref,
    down_ref,
    hidden_ref,
    d_act_ref,
    d_up_ref,
    d_gate_ref,
    made_ref,
    back_ref,
):
    hidden_width = down_ref.shape[0]
    gate = gate_ref[...]
    acts = dot(rows_ref[...], in_ref[...])
    d_plain = dot_nt(grad_ref[...], down_ref[...])
    act_gate, act_up = acts[:, :hidden_width], acts[:, hidden_width:]
    sigmoid = 1.0 / (1.0 + jnp.exp(-act_gate))
    silu_gate = act_gate * sigmoid
    hidden = silu_gate * act_up
    d_gate_ref[...] = jnp.sum(hidden * d_plain, axis=1, keepdims=True)
    d_hidden = d_plain * gate
    hidden_low = (hidden * gate).astype(low)
    d_act_gate = d_hidden * act_up * (sigmoid * (1.0 + act_gate * (1.0 - sigmoid)))
    d_in = jnp.concatenate([d_act_gate.astype(low), (d_hidden * silu_gate).astype(low)], axis=1)
    hidden_ref[...] = hidden_low
    d_act_ref[...] = d_in[:, :hidden_width]
    d_up_ref[...] = d_in[:, hidden_width:]
    back_ref[...] = dot_nt(d_in, in_ref[...]).astype(low)
    made_ref[...] = dot(hidden_low, down_ref[...]).astype(low)


def expert_rows(rows, grad_rows, gate, full_in, full_down):
    amount, model_width = rows.shape
    hidden_width = full_down.shape[0]
    tile = tile_of(amount, 256)

    def by_rows(columns):
        return pl.BlockSpec((tile, columns), lambda step: (step, 0))

    outs = [
        (hidden_width, low),
        (hidden_width, low),
        (hidden_width, low),
        (1, wide),
        (model_width, low),
        (model_width, low),
    ]
    return pl.pallas_call(
        expert_kernel,
        grid=(amount // tile,),
        in_specs=[
            by_rows(model_width),
            by_rows(model_width),
            by_rows(1),
            whole_block(full_in.shape),
            whole_block(full_down.shape),
        ],
        out_specs=[by_rows(columns) for columns, _ in outs],
        out_shape=[jax.ShapeDtypeStruct((amount, columns), kind) for columns, kind in outs],
        compiler_params=pltpu.CompilerParams(vmem_limit_bytes=52 * MIB),
        cost_estimate=BRIEF,
    )(rows, grad_rows, gate, full_in, full_down)


def weight_kernel(amount, *refs):
    total = dot_tn(refs[0][...], refs[amount][...])
    for step in range(1, amount):
        total = total + dot_tn(refs[step][...], refs[amount + step][...])
    refs[-1][...] = total.astype(low)


def weight_grad(lefts, rights, tile=256):
    amount = len(lefts)
    columns, out_columns = lefts[0].shape[1], rights[0].shape[1]
    rows = sum(left.shape[0] for left in lefts)
    return pl.pallas_call(
        functools.partial(weight_kernel, amount),
        grid=(columns // tile,),
        in_specs=[pl.BlockSpec((left.shape[0], tile), lambda step: (0, step)) for left in lefts]
        + [whole_block(right.shape) for right in rights],
        out_specs=pl.BlockSpec((tile, out_columns), lambda step: (step, 0)),
        out_shape=jax.ShapeDtypeStruct((columns, out_columns), low),
        compiler_params=pltpu.CompilerParams(vmem_limit_bytes=52 * MIB),
        cost_estimate=BRIEF,
    )(*lefts, *rights)


def turned(values, cosine, sine):
    return values * cosine + pltpu.roll(values, values.shape[1] // 2, 1) * sine


def turned_back(grads, cosine, sine):
    return grads * cosine + pltpu.roll(grads * sine, grads.shape[1] // 2, 1)


def head_scale(values):
    return lax.rsqrt(jnp.mean(values * values, axis=1, keepdims=True) + epsilon)


def prep_kernel(
    heads, rows_ref, w_ref, cosine_ref, sine_ref, gain_q, gain_k, lin_ref, query_ref, keyed_ref, value_ref
):
    width = gain_q.shape[1]
    cosine, sine = cosine_ref[...], sine_ref[...]
    lin = dot(rows_ref[...], w_ref[...])
    lin_ref[...] = lin[:, : (heads + 1) * width]
    for head in range(heads + 1):
        span = slice(head * width, (head + 1) * width)
        values = lin[:, span]
        gain = gain_q[...] if head < heads else gain_k[...]
        made = turned(values * head_scale(values) * gain, cosine, sine).astype(low)
        if head < heads:
            query_ref[:, span] = made
        else:
            keyed_ref[...] = made
    value_ref[...] = lin[:, (heads + 1) * width :].astype(low)


def unprep_kernel(
    heads,
    scale,
    d_query_ref,
    d_keyed_ref,
    d_value_ref,
    lin_ref,
    w_ref,
    cosine_ref,
    sine_ref,
    gain_q,
    gain_k,
    d_lin_ref,
    d_one_ref,
    d_gain_q,
    d_gain_k,
):
    width = gain_q.shape[1]
    cosine, sine = cosine_ref[...], sine_ref[...]

    @pl.when(pl.program_id(0) == 0)
    def _():
        d_gain_q[...] = jnp.zeros_like(d_gain_q)
        d_gain_k[...] = jnp.zeros_like(d_gain_k)

    for head in range(heads + 1):
        span = slice(head * width, (head + 1) * width)
        values = lin_ref[:, span]
        if head < heads:
            grads, gain, d_gain = d_query_ref[:, span].astype(wide), gain_q[...], d_gain_q
        else:
            grads, gain, d_gain = d_keyed_ref[...] * scale, gain_k[...], d_gain_k
        grads = turned_back(grads, cosine, sine)
        factor = head_scale(values)
        plain = values * factor
        d_gain[...] += jnp.sum(grads * plain, axis=0, keepdims=True)
        grads = grads * gain
        mean = jnp.mean(grads * plain, axis=1, keepdims=True)
        d_lin_ref[:, span] = (factor * (grads - plain * mean)).astype(low)
    d_lin_ref[:, (heads + 1) * width :] = d_value_ref[...].astype(low)
    d_one_ref[...] = dot_nt(d_lin_ref[...], w_ref[...]).astype(low)


def row_call(kernel, rows, tiled, fixed, outs, sums):
    tile = tile_of(rows, 256)

    def by_rows(columns):
        return pl.BlockSpec((tile, columns), lambda step: (step, 0))

    return pl.pallas_call(
        kernel,
        grid=(rows // tile,),
        in_specs=[
            whole_block(array.shape) if number in fixed else by_rows(array.shape[1])
            for number, array in enumerate(tiled)
        ],
        out_specs=[by_rows(columns) for columns, _ in outs]
        + [pl.BlockSpec((1, columns), lambda step: (0, 0)) for columns in sums],
        out_shape=[jax.ShapeDtypeStruct((rows, columns), kind) for columns, kind in outs]
        + [jax.ShapeDtypeStruct((1, columns), wide) for columns in sums],
        compiler_params=pltpu.CompilerParams(vmem_limit_bytes=48 * MIB),
        cost_estimate=BRIEF,
    )(*tiled)


def mask_tile(bias, k_place, k_segment, q_place, q_segment):
    allowed = (k_segment[...] == q_segment[0]) & (k_place[...] <= q_place[0])
    bias[...] = jnp.where(allowed, 0.0, -1e30)


def ahead_kernel(
    scale, k_place, k_segment, q_place, q_segment, q_ref, k_ref, vt_ref, mixed_ref, total_ref, bias
):
    @pl.when(pl.program_id(2) == 0)
    def _():
        mask_tile(bias, k_place.at[0], k_segment.at[0], q_place, q_segment)

    scores = dot_nt(k_ref[0], q_ref[0]) * scale + bias[...]
    row_max = jnp.max(scores, axis=0, keepdims=True)
    expd = jnp.exp(scores - row_max)
    row_total = jnp.sum(expd, axis=0, keepdims=True)
    mixed = dot(vt_ref[0], expd.astype(low)) / row_total
    mixed_ref[0] = mixed.T.astype(low)
    total_ref[0, 0] = row_max + jnp.log(row_total)


def behind_kernel(
    scale,
    k_place,
    k_segment,
    q_place,
    q_segment,
    q_ref,
    d_mixed_ref,
    k_ref,
    v_ref,
    kt_ref,
    total_ref,
    d_q_ref,
    d_k_ref,
    d_v_ref,
    bias,
):
    @pl.when(pl.program_id(2) == 0)
    def _():
        mask_tile(bias, k_place.at[0], k_segment.at[0], q_place, q_segment)

    @pl.when((pl.program_id(1) == 0) & (pl.program_id(2) == 0))
    def _():
        d_k_ref[...] = jnp.zeros_like(d_k_ref)
        d_v_ref[...] = jnp.zeros_like(d_v_ref)

    query, d_mixed = q_ref[0], d_mixed_ref[0]
    probs = jnp.exp(dot_nt(k_ref[0], query) * scale + bias[...] - total_ref[0, 0])
    d_probs = dot_nt(v_ref[0], d_mixed)
    row_dot = jnp.sum(probs * d_probs, axis=0, keepdims=True)
    d_scores = (probs * (d_probs - row_dot)).astype(low)
    d_v_ref[0] += dot(probs.astype(low), d_mixed)
    d_k_ref[0] += dot(d_scores, query)
    d_q_ref[0] = (dot(kt_ref[0], d_scores) * scale).T.astype(low)


def attention_call(kernel, marks, arrays, kinds, outs, width, scale, work):
    place, segment = marks
    seqs, length = place.shape
    tile = min(256, length)
    heads = arrays[0].shape[2] // width
    specs = {
        "query": pl.BlockSpec((1, tile, width), lambda s, i, h: (s, i, h)),
        "keys": pl.BlockSpec((1, length, width), lambda s, i, h: (s, 0, 0)),
        "flat": pl.BlockSpec((1, width, length), lambda s, i, h: (s, 0, 0)),
        "total": pl.BlockSpec((1, 1, 1, tile), lambda s, i, h: (s, h, 0, i)),
    }
    column = pl.BlockSpec((1, length, 1), lambda s, i, h: (s, 0, 0))
    row = pl.BlockSpec((1, 1, tile), lambda s, i, h: (s, 0, i))
    return pl.pallas_call(
        functools.partial(kernel, scale),
        grid=(seqs, length // tile, heads),
        in_specs=[column, column, row, row] + [specs[kind] for kind in kinds],
        out_specs=[specs[kind] for kind, _ in outs],
        out_shape=[shape for _, shape in outs],
        scratch_shapes=[pltpu.VMEM((length, tile), wide)],
        compiler_params=pltpu.CompilerParams(vmem_limit_bytes=48 * MIB),
        cost_estimate=BRIEF,
    )(place[:, :, None], segment[:, :, None], place[:, None, :], segment[:, None, :], *arrays)


def per_device(
    g_axes,
    c_axes,
    f_axes,
    tokens,
    places,
    segments,
    routes,
    w_query,
    w_key,
    w_value,
    w_out,
    w_router,
    w_gate,
    w_up,
    w_down,
    gain_attn,
    gain_ffn,
    gain_query,
    gain_key,
    cotangent,
):
    groups, parts_c, parts_f = 1 << len(g_axes), 1 << len(c_axes), 1 << len(f_axes)
    count = tokens.shape[1]
    width = gain_query.shape[0]
    model_width = tokens.shape[2]
    kv_heads = w_key.shape[1] // width // parts_c
    assert kv_heads == 1
    heads = w_query.shape[1] // width // parts_c // groups
    experts = w_gate.shape[0]
    hidden_width = w_gate.shape[2]
    scale = 1.0 / math.sqrt(width)
    rows_d = w_query.shape[0]
    rows_o = w_out.shape[0]
    rows_f = w_down.shape[1]
    pair_count = experts.bit_length() - 1 - len(g_axes) - len(c_axes)
    assert 0 <= pair_count <= len(f_axes)
    far_axes = f_axes[: len(f_axes) - pair_count]
    near_axes = f_axes[len(f_axes) - pair_count :]
    parts_near = 1 << len(near_axes)
    team_axes = c_axes + near_axes
    team = parts_c * parts_near
    own_axes = c_axes + f_axes
    plane_axes = g_axes + c_axes
    cluster_axes = g_axes + team_axes
    all_axes = g_axes + c_axes + f_axes
    g_here = flat_index(g_axes)
    core = c_axes[-1:]
    plane_shape = (2,) * len(plane_axes) + (count, model_width)
    cluster_shape = (2,) * len(cluster_axes) + (count, model_width)
    turn = g_axes + c_axes[:-1]
    half = count // 2
    plane_parts = [(0, half, turn), (half, count, turn[1:] + turn[:1])]
    turn = turn + near_axes
    third = (count // 3) // ROW_TILE * ROW_TILE
    cuts = [0, count - 2 * third, count - third, count]
    cluster_parts = [
        (cuts[step], cuts[step + 1], turn[step:] + turn[:step]) for step in range(len(cuts) - 1)
    ]
    def core_last(parts):
        return [(lo, hi, order + core) for lo, hi, order in parts]

    def core_first(parts):
        return [(lo, hi, core + order) for lo, hi, order in parts]

    q_cols = heads * width
    qkv_cols = q_cols + 2 * width
    even = rows_o % (groups * width) == 0
    if even:
        own_query = w_query.reshape(rows_d, parts_c, parts_f, groups, q_cols // parts_f)
        own_query = own_query.transpose(3, 1, 0, 2, 4)
    else:
        own_query = w_query.reshape(rows_d, parts_c, groups, q_cols).transpose(2, 1, 0, 3)
    own_query = take(own_query.reshape(groups, parts_c, rows_d, q_cols), g_here)
    mine_qkv = jnp.concatenate(
        [
            own_query,
            w_key.reshape(rows_d, parts_c, width).transpose(1, 0, 2),
            w_value.reshape(rows_d, parts_c, width).transpose(1, 0, 2),
        ],
        axis=2,
    )
    own_in = jnp.concatenate([w_gate, w_up], axis=2)
    wide_router = jnp.pad(w_router, ((0, 0), (0, width - experts)))
    resid = tokens[0].astype(jnp.float32)
    norm_one, back_one = jax.vjp(normed, resid, gain_attn)

    def own_experts(place):
        return flat_index(g_axes) * parts_c + place

    def by_team(pieces):
        return pieces.reshape((groups * parts_c, parts_near) + pieces.shape[1:])

    mine_out = take(w_out.reshape(groups, -1, model_width), g_here) if even else w_out
    all_grads = lax.all_gather(cotangent[0], cluster_axes, axis=0, tiled=True)
    w_qkv, all_one, full_router, marks, w_mix, got_in, got_down = transfer(
        1,
        [
            Spread(c_axes, f_axes, mine_qkv, (rows_d, qkv_cols)),
            Gather(plane_axes, norm_one.astype(low), core_last(plane_parts)),
            Direct(own_axes, wide_router[None], wide_router.shape, lambda place: 0),
            Direct(
                g_axes,
                jnp.stack([places[0], segments[0]])[None],
                (2,) + places.shape[1:],
                lambda place: 0,
            ),
            Gather(f_axes, mine_out, [(0, mine_out.shape[0], f_axes)]),
            Direct(c_axes, by_team(own_in), (parts_near,) + own_in.shape[1:], own_experts, 2),
            Direct(c_axes, by_team(w_down), (parts_near,) + w_down.shape[1:], own_experts, 2),
        ],
    )
    w_qkv = w_qkv.reshape(model_width, qkv_cols)
    all_one = all_one.reshape(-1, model_width)
    full_router = full_router.reshape(model_width, width)[:, :experts]

    w_mix = w_mix.reshape(-1, model_width)
    if not even:
        w_mix = take(w_mix.reshape(groups, q_cols, model_width), g_here)
    f_here = flat_index(f_axes)
    near_here = flat_index(near_axes)

    def whole_expert(got):
        arrived = exchange(f_axes, lambda other: take_at(got, other % parts_near, 1))
        return laid_out(arrived, f_here, 1)

    full_in = whole_expert(got_in).reshape(model_width, 2 * hidden_width)
    full_down = whole_expert(got_down).reshape(hidden_width, model_width)

    place, segment = marks[:, 0], marks[:, 1]
    length = place.shape[1]
    angle = angles(place.reshape(-1), width)
    cosine, sine = jnp.cos(angle), jnp.sin(angle)
    cosine = jnp.concatenate([cosine, cosine], axis=1)
    sine = jnp.concatenate([-sine, sine], axis=1)
    tables = (cosine, sine, gain_query[None], gain_key[None])
    rows = groups * length
    lin, query_low, keyed_low, value_low = row_call(
        functools.partial(prep_kernel, heads),
        rows,
        (all_one, w_qkv) + tables,
        (1, 4, 5),
        [(q_cols + width, wide), (q_cols, low), (width, low), (width, low)],
        [],
    )
    query_low = query_low.reshape(groups, length, q_cols)
    keyed_low = keyed_low.reshape(groups, length, width)
    value_low = value_low.reshape(groups, length, width)
    total_shape = jax.ShapeDtypeStruct((groups, heads, 1, length), wide)
    mixed_low, log_total = attention_call(
        ahead_kernel,
        (place, segment),
        (query_low, keyed_low, value_low.transpose(0, 2, 1)),
        ("query", "keys", "flat"),
        [("query", jax.ShapeDtypeStruct(query_low.shape, low)), ("total", total_shape)],
        width,
        scale,
        4,
    )
    mixed_rows = mixed_low.reshape(groups * length, q_cols)
    branch = dot(mixed_rows, w_mix).astype(low).reshape(plane_shape)
    (branch,) = transfer(2, [Reduce(plane_axes, branch, core_first(plane_parts))])
    resid_one = resid + branch

    norm_two, back_two = jax.vjp(normed, resid_one, gain_ffn)
    normed_two = norm_two.astype(low)
    logits = dot(normed_two, full_router)
    labels = jnp.arange(experts, dtype=jnp.int32)
    chosen = jnp.any(routes[0][:, :, None] == labels[None, None, :], axis=1)
    logits = jnp.where(chosen, logits, -1e30)
    powers = jnp.where(chosen, jnp.exp(logits - jnp.max(logits, axis=-1, keepdims=True)), 0.0)
    gates = powers / jnp.sum(powers, axis=-1, keepdims=True)

    all_two, all_gates = transfer(
        3,
        [
            Gather(cluster_axes, normed_two, core_last(cluster_parts)),
            Gather(cluster_axes, gates.T, [(0, experts, turn + core)]),
        ],
    )
    all_two = all_two.reshape(-1, model_width)
    gate = lax.dynamic_index_in_dim(
        all_gates.reshape(-1, experts, count), flat_index(cluster_axes), 1, keepdims=False
    )
    hiddens, d_acts, d_ups, d_gate, made, back = expert_rows(
        all_two, all_grads, gate.reshape(-1, 1), full_in, full_down
    )
    d_rows_two, d_gates = transfer(
        4,
        [
            Reduce(cluster_axes, back.reshape(cluster_shape), core_first(cluster_parts)),
            Direct(
                cluster_axes, d_gate.reshape(experts, 1, count), (1, count), lambda place: place
            ),
        ],
    )

    def over_fsdp(part, rows):
        stack = part.reshape(parts_c, parts_f, rows, -1)
        arrived = exchange(f_axes, lambda other: take_at(stack, other, 1))
        sums = []
        for near in range(parts_near):
            total = arrived[near].astype(wide)
            for step in range(near + parts_near, parts_f, parts_near):
                total = total + arrived[step].astype(wide)
            sums.append(total.astype(low))
        return laid_out(sums, near_here, 1)

    part_down = weight_grad([after(hiddens, d_rows_two)], [all_grads])
    part_gate = weight_grad([all_two], [after(d_acts, part_down)])
    part_up = weight_grad([all_two], [after(d_ups, part_gate)])
    share_down = over_fsdp(part_down, rows_f)
    share_gate = over_fsdp(part_gate, rows_d)
    share_up = over_fsdp(part_up, rows_d)
    d_gates = d_gates.reshape(experts, count).T

    d_logits = (gates * (d_gates - jnp.sum(gates * d_gates, axis=-1, keepdims=True))).astype(low)
    part_router = dot_tn(normed_two, d_logits)
    d_normed_two = d_rows_two + dot_nt(d_logits, full_router)
    d_resid_one, d_gain_ffn = back_two(d_normed_two)
    d_resid_one = d_resid_one + cotangent[0].astype(jnp.float32)
    wide_part = jnp.pad(part_router.astype(low), ((0, 0), (0, width - experts)))
    share_router = lax.psum_scatter(wide_part, own_axes, scatter_dimension=0, tiled=True)
    grad_router = sum_all(share_router[:, :experts].astype(jnp.float32), g_axes)

    made_shape = (2,) * len(plane_axes) + (parts_near * count, model_width)
    made_parts = [(lo * parts_near, hi * parts_near, order) for lo, hi, order in plane_parts]
    d_branch, made = transfer(
        5,
        [
            Gather(plane_axes, d_resid_one.astype(low), core_last(plane_parts)),
            Reduce(plane_axes, made.reshape(made_shape), core_first(made_parts)),
        ],
    )
    d_branch = d_branch.reshape(-1, model_width)
    d_mixed = dot_nt(d_branch, w_mix).astype(low).reshape(query_low.shape)
    shapes = [
        jax.ShapeDtypeStruct(query_low.shape, low),
        jax.ShapeDtypeStruct(keyed_low.shape, wide),
        jax.ShapeDtypeStruct(keyed_low.shape, wide),
    ]
    d_query, d_keyed, d_value = attention_call(
        behind_kernel,
        (place, segment),
        (query_low, d_mixed, keyed_low, value_low, keyed_low.transpose(0, 2, 1), log_total),
        ("query", "query", "keys", "keys", "flat", "total"),
        list(zip(("query", "keys", "keys"), shapes)),
        width,
        scale,
        10,
    )
    def to_owner(share):
        return Direct(c_axes, share, share.shape[1:], lambda place: place)

    share_down, share_gate = transfer(
        6, [to_owner(after(share_down, d_query)), to_owner(after(share_gate, d_query))]
    )
    share_down = gather_blocks(share_down.reshape((1, -1) + share_down.shape[2:]), g_axes, 0)
    share_gate = gather_blocks(share_gate.reshape((1, -1) + share_gate.shape[2:]), g_axes, 0)
    d_lin, d_one, d_gain_query, d_gain_key = row_call(
        functools.partial(unprep_kernel, heads, scale),
        rows,
        (
            d_query.reshape(rows, q_cols),
            d_keyed.reshape(rows, width),
            d_value.reshape(rows, width),
            lin,
            w_qkv,
        )
        + tables,
        (4, 7, 8),
        [(qkv_cols, low), (model_width, low)],
        [width, width],
    )
    d_one = d_one.reshape(plane_shape)
    part_out = weight_grad([mixed_rows], [d_branch])
    part_qkv = weight_grad([all_one], [d_lin])

    def by_f(part):
        stack = part.reshape(parts_c, parts_f, rows_d, -1).transpose(1, 0, 2, 3)
        return stack.reshape((2,) * len(f_axes) + (parts_c * rows_d, -1))

    flows = [
        Reduce(
            f_axes,
            after(by_f(part_qkv), share_down),
            [(0, parts_c * rows_d, f_axes[::-1])],
            c_axes,
        ),
        Reduce(plane_axes, d_one, core_first(plane_parts)),
        to_owner(share_up),
    ]
    if near_axes:
        near_shape = (2,) * len(near_axes) + (count, model_width)
        near_flow = Reduce(
            near_axes, made.astype(low).reshape(near_shape), [(0, count, near_axes)]
        )
        flows.append(near_flow)
    if even:
        rows = q_cols // parts_f
        stack = part_out.reshape((2,) * len(f_axes) + (rows, model_width))
        flows.append(Reduce(f_axes, stack, [(0, rows, f_axes[::-1])]))
    share_qkv, d_one, share_up, *rest = transfer(7, flows)
    if near_axes:
        made = rest.pop(0)
    output = (resid_one + made).astype(low)[None]
    d_resid, d_gain_attn = back_one(d_one)
    grad_tokens = (d_resid + d_resid_one)[None]
    share_up = gather_blocks(share_up.reshape((1, -1) + share_up.shape[2:]), g_axes, 0)
    grad_gate, grad_up, grad_down = [
        share.reshape((experts,) + share.shape[2:]).astype(wide)
        for share in (share_gate, share_up, share_down)
    ]
    if even:
        share_out = rest[0].astype(low)[None]
        grad_out = gather_blocks(share_out, g_axes, 0).astype(wide).reshape(rows_o, model_width)
    else:
        stack = jnp.where(jnp.arange(groups)[:, None, None] == g_here, part_out[None], 0)
        share_out = lax.psum_scatter(
            stack.reshape(groups * q_cols, model_width), f_axes, scatter_dimension=0, tiled=True
        )
        grad_out = sum_all(share_out.astype(wide), g_axes)
    all_qkv = gather_blocks(share_qkv[None], g_axes, 0).astype(wide)
    grad_query = all_qkv[:, :, :, :q_cols]
    if even:
        grad_query = grad_query.reshape(groups, parts_c, rows_d, parts_f, q_cols // parts_f)
        grad_query = grad_query.transpose(2, 1, 3, 0, 4).reshape(rows_d, -1)
    else:
        grad_query = grad_query.transpose(2, 1, 0, 3).reshape(rows_d, -1)
    grad_kv = jnp.sum(all_qkv[:, :, :, q_cols:], axis=0).transpose(1, 0, 2)
    grad_key = grad_kv[:, :, :width].reshape(rows_d, -1)
    grad_value = grad_kv[:, :, width:].reshape(rows_d, -1)

    gains = sum_all(
        jnp.concatenate([d_gain_attn, d_gain_ffn, d_gain_query[0], d_gain_key[0]]), all_axes
    )
    return (
        output,
        grad_tokens,
        grad_query,
        grad_key,
        grad_value,
        grad_out,
        grad_router,
        grad_gate,
        grad_up,
        grad_down,
        gains[:model_width],
        gains[model_width : 2 * model_width],
        gains[2 * model_width : 2 * model_width + width],
        gains[2 * model_width + width :],
    )


def solution(mesh):
    def binary(letter, size):
        return tuple(letter + str(step) for step in range(size.bit_length() - 1))

    g_axes = binary("g", mesh.shape["grp"])
    c_axes = binary("c", mesh.shape["ctx"])
    f_axes = binary("f", mesh.shape["fsdp"])
    names = g_axes + c_axes + f_axes
    fine = Mesh(mesh.devices.reshape((2,) * len(names)), names)
    rows = P(g_axes + f_axes, c_axes, None)
    line = P(g_axes + f_axes, None)
    split = P(c_axes + f_axes, None)
    expert = P(None, c_axes + f_axes, None)
    whole = P()
    in_specs = (
        (rows, line, line, rows)
        + (split,) * 5
        + (expert,) * 3
        + (whole,) * 4
        + (rows,)
    )
    out_specs = (rows, rows) + (split,) * 5 + (expert,) * 3 + (whole,) * 4

    def device_part(*arrays):
        return per_device(g_axes, c_axes, f_axes, *arrays)

    return jax.shard_map(
        device_part, mesh=fine, in_specs=in_specs, out_specs=out_specs, check_vma=False
    )
```

time: 1810 us -> 1260 us (0.70)
  Pallas kernels: 0 us -> 972 us
  waiting for transfers between devices: 799 us -> 97 us
  matrix products: 375 us -> 17.5 us
  other arithmetic: 232 us -> 54.3 us
  local copies, waits for them, and re-layouts: 227 us -> 63.3 us
  starting transfers between devices: 114 us -> 29.4 us
  blocking collectives: 35 us -> 0 us
    pallas_call x0 -> x17, Pallas kernels: none -> 972 us  [the longest x7 687 us: transfer(): pl.pallas_call(functools.partial(flow_kernel, flows), out_shape=shapes, i...]
    ppermute x136 -> x15, waiting for transfers between devices: 701 us -> 25.5 us  [exchange(): arrived.append(lax.ppermute(pick(jnp.bitwise_xor(here, step)), axes, pairs))]
    dot_general x6 -> x0, matrix products: 100 us -> none  [the longest x1 28.3 us: per_device(): jnp.einsum('ikgd,jkd->kgij', d_mixed, value_low, preferred_element_type=j...]
    dot_general x12 -> x1, matrix products: 94 us -> 0.25 us  [dot_tn(): lax.dot_general(left, right, (((0,), (0,)), ((), ())), preferred_element_...]
    dot_general x12 -> x2, matrix products: 101 us -> 10.1 us  [dot_nt(): lax.dot_general(left, right, (((1,), (1,)), ((), ())), preferred_element_...]
    ppermute x136 -> x15, starting transfers between devices: 100 us -> 21.1 us  [exchange(): arrived.append(lax.ppermute(pick(jnp.bitwise_xor(here, step)), axes, pairs))]
    dot_general x12 -> x2, matrix products: 79.7 us -> 7.19 us  [dot(): return jnp.dot(left, right, preferred_element_type=jnp.float32)]
    unnamed x431 -> x111, local copies, waits for them, and re-layouts: 71.8 us -> 13 us
  transfers between devices with their start and end apart: 154 -> 28, of which waited for: 82 -> 8; matrix products, arithmetic and copies ran while one was open for 44% -> 9% of each run, Pallas kernels for 0% -> 59%
where the time goes in v2:
time: 1260 us; the launch traced here: 1250 us
  Pallas kernels  972 us (77%)
  waiting for transfers between devices  97 us (8%)
  local copies, waits for them, and re-layouts  63.3 us (5%)
  other arithmetic  54.3 us (4%)
  starting transfers between devices  29.4 us (2%)
  matrix products  17.5 us (1%)
  between operations  15.6 us (1%)
    pallas_call x7, Pallas kernels, transfer(): pl.pallas_call(functools.partial(flow_kernel, flows), out_shape=shapes, i...  687 us
    pallas_call x1, Pallas kernels, expert_rows(): pl.pallas_call(expert_kernel, grid=(amount // tile,), in_specs=[by_rows(m...  93.6 us
    pallas_call x5, Pallas kernels, weight_grad(): pl.pallas_call(functools.partial(weight_kernel, amount), grid=(columns //...  81 us
    pallas_call x2, Pallas kernels, attention_call(): pl.pallas_call(functools.partial(kernel, scale), grid=(seqs, length // ti...  72 us
    pallas_call x2, Pallas kernels, row_call(): pl.pallas_call(kernel, grid=(rows // tile,), in_specs=[whole_block(array....  38.3 us
    ppermute x5, waiting for transfers between devices, gather_blocks(): other = lax.ppermute(block, axes[0], SWAP)  37.7 us
    ppermute x6, waiting for transfers between devices, sum_all(): value = value + lax.ppermute(value, axis, SWAP)  33.2 us
    ppermute x15, waiting for transfers between devices, exchange(): arrived.append(lax.ppermute(pick(jnp.bitwise_xor(here, step)), axes, pairs))  25.5 us
  transfers between devices with their start and end apart: 28, of which 8 were waited for; matrix products, arithmetic and copies ran while one was open for 9% of the time, Pallas kernels for 59%

profile of v2, /device:TPU:0, one launch (start us, length us, event | category | flops | bytes accessed | tf_op | source)
XLA Modules:
  0.0 1249.6 jit_solution(820847308005987087)
XLA Ops:
  14.4 5.2 pad_maximum_fusion
  20.8 150.2 %shard_map.272 = (bf16[4,2,2,128,768]{4,3,2,1,0:T(8,128)(2,1)}, bf16[2,2,2,256,2048]{4,3,2,1,0:T(8,128)(2,1)}, bf16[16,128,128]{2,1,0:T(8,128)(2,1)S(1)}, s32[2,...) custom-call(bf16[4,128,768]{2,1,0:T(8,128)(2,1)S(1)} %pad_maximum_fu, ...), custom_call_target="tpu_custom_call" | custom-call | bytes 1048576 | tf_op jit(solution)/shard_map/pallas_call | solution.py:393
  191.6 14.1 %shard_map.273 = (f32[2048,640]{1,0:T(8,128)}, bf16[2048,512]{1,0:T(8,128)(2,1)S(1)}, bf16[2048,128]{1,0:T(8,128)(2,1)S(1)}, bf16[2048,128]{1,0:T(8,128)(2,1)S(1)}) custom-call(bf16[2048,2048]{1,0:T(8,128)(2,1)} %bitcast.270, bf16[2048,768]{1,0:T(8,128)(2,1)} %bitcast.283, f32[2048,128]{1,0:T(8,128)S(1)} %get-tuple-element.190.cosine_ref, ...), custom_call_target="tpu_custom_call" | custom-call | bytes 1048576 | tf_op jit(solution)/shard_map/pallas_call | solution.py:604
  209.6 32.1 %shard_map.274 = (bf16[2,1024,512]{2,1,0:T(8,128)(2,1)S(1)}, f32[2,4,1,1024]{3,2,1,0:T(1,128)S(1)}) custom-call(s32[2,1024,1]{2,1,0:T(8,128)S(1)} %copy.129.k_place, s32[2,1024,1]{2,1,0:T(8,128)S(1)} %copy.130.k_segment, s32[2,1,1024]{2,1,0:T(1,128)S(1)} %get-tuple-element.183.q_place, s32[2,1,1024]{2,1,0:T(1,128)S(1)} %get-tuple-element.182.q_segment, ...), custom_call_target="tpu_custom_call" | custom-call | bytes 1048576 | tf_op jit(solution)/shard_map/pallas_call | solution.py:690
  241.7 6.8 convolution_convert_fusion
  248.4 68.9 %shard_map.275 = f32[256,2048]{1,0:T(8,128)} custom-call(bf16[2,2,2,256,2048]{4,3,2,1,0:T(8,128)(2,1)} %bitcast.287), custom_call_target="tpu_custom_call" | custom-call | bytes 1048576 | tf_op jit(solution)/shard_map/pallas_call | solution.py:393
  321.3 79.8 %shard_map.276 = (bf16[2,2,2,2,256,2048]{5,4,3,2,1,0:T(8,128)(2,1)}, f32[2,2,2,2,16,256]{5,4,3,2,1,0:T(8,128)S(1)}) custom-call(bf16[256,2048]{1,0:T(8,128)(2,1)S(1)} %multiply_convert_fusion.refs_0_, f32[16,256]{1,0:T(8,128)S(1)} %fusion.24.refs_1_), custom_call_target="tpu_custom_call" | custom-call | bytes 1048576 | tf_op jit(solution)/shard_map/pallas_call | solution.py:393
  416.5 25.4 %collective-permute-done.2 = bf16[4,128,1536]{2,1,0:T(8,128)(2,1)S(1)} collective-permute-done((bf16[4,128,1536]{2,1,0:T(8,128)(2,1)}, bf16[4,128,1536]{2,1,0:T(8,128)(2,1)S(1)}, u32[]{:S(2)}, u32[]{:S(2)}) %collective-permute-start.2) | collective-permute-done | bytes 1572896 | tf_op jit(solution)/shard_map/ppermute | solution.py:69
  443.1 93.6 %shard_map.277 = (bf16[4096,768]{1,0:T(8,128)(2,1)}, bf16[4096,768]{1,0:T(8,128)(2,1)}, bf16[4096,768]{1,0:T(8,128)(2,1)}, f32[4096,1]{1,0:T(8,128)}, bf16[4096,...) custom-call(bf16[4096,2048]{1,0:T(8,128)(2,1)} %bitcast.265, bf16[4096,2048]{1,0:T(8,128)(2,1)} %bitcast.268, ...), custom_call_target="tpu_custom_call" | custom-call | bytes 1048576 | tf_op jit(solution)/shard_map/pallas_call | solution.py:484
  538.9 107.8 %shard_map.278 = (f32[256,2048]{1,0:T(8,128)}, f32[16,1,256]{2,1,0:T(1,128)S(1)}) custom-call(bf16[2,2,2,2,256,2048]{5,4,3,2,1,0:T(8,128)(2,1)} %bitcast.273, f32[16,1,256]{2,1,0:T(1,128)S(1)} %bitcast.255), custom_call_target="tpu_custom_call" | custom-call | bytes 1048576 | tf_op jit(solution)/shard_map/pallas_call | solution.py:393
  646.7 21.0 %shard_map.283 = bf16[768,2048]{1,0:T(8,128)(2,1)} custom-call(bf16[4096,768]{1,0:T(8,128)(2,1)} %get-tuple-element.85.refs_0_, bf16[4096,2048]{1,0:T(8,128)(2,1)} %bitcast.269), custom_call_target="tpu_custom_call" | custom-call | bytes 1048576 | tf_op jit(solution)/shard_map/pallas_call | solution.py:512
  667.7 19.0 %shard_map.284 = bf16[2048,768]{1,0:T(8,128)(2,1)} custom-call(bf16[4096,2048]{1,0:T(8,128)(2,1)} %bitcast.266, bf16[4096,768]{1,0:T(8,128)(2,1)} %get-tuple-element.88.refs_1_), custom_call_target="tpu_custom_call" | custom-call | bytes 1048576 | tf_op jit(solution)/shard_map/pallas_call | solution.py:512
  700.7 109.7 %shard_map.279 = (bf16[2,2,2,256,2048]{4,3,2,1,0:T(8,128)(2,1)}, f32[512,2048]{1,0:T(8,128)}) custom-call(bf16[256,2048]{1,0:T(8,128)(2,1)S(1)} %fusion.31.refs_0_, bf16[2,2,2,512,2048]{4,3,2,1,0:T(8,128)(2,1)} %bitcast.274), custom_call_target="tpu_custom_call" | custom-call | bytes 1048576 | tf_op jit(solution)/shard_map/pallas_call | solution.py:393
  812.0 9.1 convolution_convert_fusion.1
  821.1 19.0 %shard_map.286 = bf16[2048,768]{1,0:T(8,128)(2,1)} custom-call(bf16[4096,2048]{1,0:T(8,128)(2,1)} %bitcast.267, bf16[4096,768]{1,0:T(8,128)(2,1)} %get-tuple-element.94.refs_1_), custom_call_target="tpu_custom_call" | custom-call | bytes 1048576 | tf_op jit(solution)/shard_map/pallas_call | solution.py:512
  844.4 40.0 %shard_map.280 = (bf16[2,1024,512]{2,1,0:T(8,128)(2,1)}, f32[2,1024,128]{2,1,0:T(8,128)S(1)}, f32[2,1024,128]{2,1,0:T(8,128)S(1)}) custom-call(s32[2,1024,1]{2,1,0:T(8,128)S(1)} %copy.129.k_place, s32[2,1024,1]{2,1,0:T(8,128)S(1)} %copy.130.k_segment, s32[2,1,1024]{2,1,0:T(1,128)S(1)} %get-tuple-element.183.q_place, ...), custom_call_target="tpu_custom_call" | custom-call | bytes 1048576 | tf_op jit(solution)/shard_map/pallas_call | solution.py:690
  892.7 38.1 %shard_map.285 = (bf16[4,2,48,2048]{3,2,1,0:T(8,128)(2,1)S(1)}, bf16[4,2,128,768]{3,2,1,0:T(8,128)(2,1)}) custom-call(bf16[4,2,48,2048]{3,2,1,0:T(8,128)(2,1)} %pad_maximum_fusion.4.refs_0_, bf16[4,2,128,768]{3,2,1,0:T(8,128)(2,1)} %copy.142.refs_1_), custom_call_target="tpu_custom_call" | custom-call | bytes 1048576 | tf_op jit(solution)/shard_map/pallas_call | solution.py:393
  938.1 9.6 shard_map.287
  947.7 24.2 %shard_map.281 = (bf16[2048,768]{1,0:T(8,128)(2,1)}, bf16[2048,2048]{1,0:T(8,128)(2,1)}, f32[1,128]{1,0:T(1,128)S(1)}, f32[1,128]{1,0:T(1,128)S(1)}) custom-call(bf16[2048,512]{1,0:T(8,128)(2,1)} %bitcast.297, f32[2048,128]{1,0:T(8,128)S(1)} %bitcast.252, f32[2048,128]{1,0:T(8,128)S(1)} %bitcast.253, f32[2048,640]{1,0:T(8,128)} %get-tuple-element.82.lin_ref, ...), custom_call_target="tpu_custom_call" | custom-call | bytes 1048576 | tf_op jit(solution)/shard_map/pallas_call | solution.py:604
  972.0 12.5 shard_map.282
  996.7 29.1 %collective-permute-done.18 = f32[128,16]{0,1:T(8,128)S(1)} collective-permute-done((f32[128,16]{0,1:T(8,128)S(1)}, f32[128,16]{0,1:T(8,128)S(1)}, u32[]{:S(2)}, u32[]{:S(2)}) %collective-permute-start.18) | collective-permute-done | bytes 8224 | tf_op jit(solution)/shard_map/ppermute | solution.py:420
  1028.4 132.9 %shard_map.288 = (bf16[4,128,768]{2,1,0:T(8,128)(2,1)S(1)}, f32[256,2048]{1,0:T(8,128)}, bf16[4,2,128,768]{3,2,1,0:T(8,128)(2,1)}, f32[256,2048]{1,0:T(8,128)}, f32[128,2048]{1,0:T(8,128)S(1)}) custom-call(bf16[2,2,512,768]{3,2,1,0:T(8,128)(2,1)} %bitcast.282, bf16[2,2,2,256,2048]{4,3,2,1,0:T(8,128)(2,1)} %bitcast.290, ...), custom_call_target="tpu_custom_call" | custom-call | bytes 1048576 | tf_op jit(solution)/shard_map/pallas_call | solution.py:393
  1188.8 15.0 %collective-permute-done.16 = bf16[1,4,128,768]{3,2,1,0:T(8,128)(2,1)S(1)} collective-permute-done((bf16[1,4,128,768]{3,2,1,0:T(8,128)(2,1)S(1)}, bf16[1,4,128,768]{3,2,1,0:T(8,128)(2,1)S(1)}, u32[]{:S(2)}, u32[]{:S(2)}) %collective-permute-start.16) | collective-permute-done | bytes 786464 | tf_op jit(solution)/shard_map/ppermute | solution.py:411
  1214.1 22.1 %collective-permute-done.20 = bf16[1,8,128,768]{3,2,1,0:T(8,128)(2,1)} collective-permute-done((bf16[1,8,128,768]{3,2,1,0:T(8,128)(2,1)}, bf16[1,8,128,768]{3,2,1,0:T(8,128)(2,1)}, u32[]{:S(2)}, u32[]{:S(2)}) %collective-permute-start.20) | collective-permute-done | bytes 1572896 | tf_op jit(solution)/shard_map/ppermute | solution.py:411
  (260 shorter events, 148.8 us)
Async XLA Ops:
  7.2 435.9 %all-gather.3.cloned.1.call-start = ((), (), s32[]{:S(2)}) async-start(), calls=%async_computation.1 | async-start | bytes 17825792 | tf_op jit(solution)/shard_map/all_gather | solution.py:796
  7.9 982.9 %reduce-scatter.4.cloned.1.call-start = ((), (), s32[]{:S(2)}) async-start(), calls=%async_computation.2 | async-start | bytes 557056
  174.2 228.9 %collective-permute-start.3 = (bf16[4,48,2048]{2,1,0:T(8,128)(2,1)}, bf16[4,48,2048]{2,1,0:T(8,128)(2,1)}, u32[]{:S(2)}, u32[]{:S(2)}) collective-permute-start(bf16[4,48,2048]{2,1,0:T(8,128)(2,1)} %get-tuple-element.169), channel_id=1, source_target_pairs={{0,1},{1,0},{2,3},{3,2},{4,5},{5,4},{6,7},{7,6},{8,9},{9,8},{10,11... | collective-permute-start | bytes 2359304 | tf_op jit(solution)/shard_map/ppermute | solution.py:69
  176.6 230.3 %collective-permute-start.4 = (bf16[4,48,2048]{2,1,0:T(8,128)(2,1)}, bf16[4,48,2048]{2,1,0:T(8,128)(2,1)}, u32[]{:S(2)}, u32[]{:S(2)}) collective-permute-start(bf16[4,48,2048]{2,1,0:T(8,128)(2,1)} %get-tuple-element.168), channel_id=1, source_target_pairs={{0,2},{1,3},{2,0},{3,1},{4,6},{5,7},{6,4},{7,5},{8,10},{9,11},{10,... | collective-permute-start | bytes 2359304 | tf_op jit(solution)/shard_map/ppermute | solution.py:69
  176.6 232.4 %collective-permute-start.5 = (bf16[4,48,2048]{2,1,0:T(8,128)(2,1)}, bf16[4,48,2048]{2,1,0:T(8,128)(2,1)}, u32[]{:S(2)}, u32[]{:S(2)}) collective-permute-start(bf16[4,48,2048]{2,1,0:T(8,128)(2,1)} %get-tuple-element.167), channel_id=1, source_target_pairs={{0,3},{1,2},{2,1},{3,0},{4,7},{5,6},{6,5},{7,4},{8,11},{9,10},{10,... | collective-permute-start | bytes 2359304 | tf_op jit(solution)/shard_map/ppermute | solution.py:69
  185.2 226.0 %collective-permute-start = (bf16[4,128,1536]{2,1,0:T(8,128)(2,1)}, bf16[4,128,1536]{2,1,0:T(8,128)(2,1)}, u32[]{:S(2)}, u32[]{:S(2)}) collective-permute-start(bf16[4,128,1536]{2,1,0:T(8,128)(2,1)} %get-tuple-element.161), channel_id=1, source_target_pairs={{0,1},{1,0},{2,3},{3,2},{4,5},{5,4},{6,7},{7,6},{8,9},{9,8},{10,11... | collective-permute-start | bytes 4718600 | tf_op jit(solution)/shard_map/ppermute | solution.py:69
  186.2 227.6 %collective-permute-start.1 = (bf16[4,128,1536]{2,1,0:T(8,128)(2,1)}, bf16[4,128,1536]{2,1,0:T(8,128)(2,1)}, u32[]{:S(2)}, u32[]{:S(2)}) collective-permute-start(bf16[4,128,1536]{2,1,0:T(8,128)(2,1)} %get-tuple-element.160), channel_id=1, source_target_pairs={{0,2},{1,3},{2,0},{3,1},{4,6},{5,7},{6,4},{7,5},{8,10},{9,11},{10,... | collective-permute-start | bytes 4718600 | tf_op jit(solution)/shard_map/ppermute | solution.py:69
  403.1 38.8 %collective-permute-start.2 = (bf16[4,128,1536]{2,1,0:T(8,128)(2,1)}, bf16[4,128,1536]{2,1,0:T(8,128)(2,1)S(1)}, u32[]{:S(2)}, u32[]{:S(2)}) collective-permute-start(bf16[4,128,1536]{2,1,0:T(8,128)(2,1)} %get-tuple-element.159), channel_id=1, source_target_pairs={{0,3},{1,2},{2,1},{3,0},{4,7},{5,6},{6,5},{7,4},{8,11},{9,10},{10,... | collective-permute-start | bytes 4718600 | tf_op jit(solution)/shard_map/ppermute | solution.py:69
  689.9 120.5 %collective-permute-start.10 = (bf16[4,128,768]{2,1,0:T(8,128)(2,1)}, bf16[4,128,768]{2,1,0:T(8,128)(2,1)}, u32[]{:S(2)}, u32[]{:S(2)}) collective-permute-start(bf16[4,128,768]{2,1,0:T(8,128)(2,1)} %get-tuple-element.155), channel_id=1, source_target_pairs={{0,1},{1,0},{2,3},{3,2},{4,5},{5,4},{6,7},{7,6},{8,9},{9,8},{10,11... | collective-permute-start | bytes 2359304 | tf_op jit(solution)/shard_map/ppermute | solution.py:69
  691.4 193.1 %collective-permute-start.11 = (bf16[4,128,768]{2,1,0:T(8,128)(2,1)}, bf16[4,128,768]{2,1,0:T(8,128)(2,1)}, u32[]{:S(2)}, u32[]{:S(2)}) collective-permute-start(bf16[4,128,768]{2,1,0:T(8,128)(2,1)} %get-tuple-element.154), channel_id=1, source_target_pairs={{0,3},{1,2},{2,1},{3,0},{4,7},{5,6},{6,5},{7,4},{8,11},{9,10},{10,... | collective-permute-start | bytes 2359304 | tf_op jit(solution)/shard_map/ppermute | solution.py:69
  693.7 190.8 %collective-permute-start.9 = (bf16[4,128,768]{2,1,0:T(8,128)(2,1)}, bf16[4,128,768]{2,1,0:T(8,128)(2,1)}, u32[]{:S(2)}, u32[]{:S(2)}) collective-permute-start(bf16[4,128,768]{2,1,0:T(8,128)(2,1)} %get-tuple-element.153), channel_id=1, source_target_pairs={{0,2},{1,3},{2,0},{3,1},{4,6},{5,7},{6,4},{7,5},{8,10},{9,11},{10,... | collective-permute-start | bytes 2359304 | tf_op jit(solution)/shard_map/ppermute | solution.py:69
  697.1 191.9 %collective-permute-start.6 = (bf16[4,48,2048]{2,1,0:T(8,128)(2,1)}, bf16[4,48,2048]{2,1,0:T(8,128)(2,1)}, u32[]{:S(2)}, u32[]{:S(2)}) collective-permute-start(bf16[4,48,2048]{2,1,0:T(8,128)(2,1)} %get-tuple-element.156), channel_id=1, source_target_pairs={{0,2},{1,3},{2,0},{3,1},{4,6},{5,7},{6,4},{7,5},{8,10},{9,11},{10,... | collective-permute-start | bytes 2359304 | tf_op jit(solution)/shard_map/ppermute | solution.py:69
  700.0 188.9 %collective-permute-start.7 = (bf16[4,48,2048]{2,1,0:T(8,128)(2,1)}, bf16[4,48,2048]{2,1,0:T(8,128)(2,1)}, u32[]{:S(2)}, u32[]{:S(2)}) collective-permute-start(bf16[4,48,2048]{2,1,0:T(8,128)(2,1)} %get-tuple-element.158), channel_id=1, source_target_pairs={{0,1},{1,0},{2,3},{3,2},{4,5},{5,4},{6,7},{7,6},{8,9},{9,8},{10,11... | collective-permute-start | bytes 2359304 | tf_op jit(solution)/shard_map/ppermute | solution.py:69
  810.5 78.5 %collective-permute-start.8 = (bf16[4,48,2048]{2,1,0:T(8,128)(2,1)}, bf16[4,48,2048]{2,1,0:T(8,128)(2,1)}, u32[]{:S(2)}, u32[]{:S(2)}) collective-permute-start(bf16[4,48,2048]{2,1,0:T(8,128)(2,1)} %get-tuple-element.157), channel_id=1, source_target_pairs={{0,3},{1,2},{2,1},{3,0},{4,7},{5,6},{6,5},{7,4},{8,11},{9,10},{10,... | collective-permute-start | bytes 2359304 | tf_op jit(solution)/shard_map/ppermute | solution.py:69
  930.8 95.6 %collective-permute-start.12 = (bf16[1,8,48,2048]{3,2,1,0:T(8,128)(2,1)S(1)}, bf16[1,8,48,2048]{3,2,1,0:T(8,128)(2,1)}, u32[]{:S(2)}, u32[]{:S(2)}) collective-permute-start(bf16[1,8,48,2048]{3,2,1,0:T(8,128)(2,1)S(1)} %bitcast.250), channel_id=1, source_target_pairs={{0,16},{16,0},{1,17},{17,1},{2,18},{18,2},{3,19},{19,3},{4,20},{20... | collective-permute-start | bytes 4718600 | tf_op jit(solution)/shard_map/ppermute | solution.py:411
  933.7 57.9 %collective-permute-start.13 = (bf16[4,128,768]{2,1,0:T(8,128)(2,1)}, bf16[4,128,768]{2,1,0:T(8,128)(2,1)}, u32[]{:S(2)}, u32[]{:S(2)}) collective-permute-start(bf16[4,128,768]{2,1,0:T(8,128)(2,1)} %get-tuple-element.148), channel_id=1, source_target_pairs={{0,2},{1,3},{2,0},{3,1},{4,6},{5,7},{6,4},{7,5},{8,10},{9,11},{10,... | collective-permute-start | bytes 2359304 | tf_op jit(solution)/shard_map/ppermute | solution.py:69
  935.7 57.4 %collective-permute-start.14 = (bf16[4,128,768]{2,1,0:T(8,128)(2,1)}, bf16[4,128,768]{2,1,0:T(8,128)(2,1)}, u32[]{:S(2)}, u32[]{:S(2)}) collective-permute-start(bf16[4,128,768]{2,1,0:T(8,128)(2,1)} %get-tuple-element.150), channel_id=1, source_target_pairs={{0,1},{1,0},{2,3},{3,2},{4,5},{5,4},{6,7},{7,6},{8,9},{9,8},{10,11... | collective-permute-start | bytes 2359304 | tf_op jit(solution)/shard_map/ppermute | solution.py:69
  936.6 56.5 %collective-permute-start.15 = (bf16[4,128,768]{2,1,0:T(8,128)(2,1)}, bf16[4,128,768]{2,1,0:T(8,128)(2,1)}, u32[]{:S(2)}, u32[]{:S(2)}) collective-permute-start(bf16[4,128,768]{2,1,0:T(8,128)(2,1)} %get-tuple-element.149), channel_id=1, source_target_pairs={{0,3},{1,2},{2,1},{3,0},{4,7},{5,6},{6,5},{7,4},{8,11},{9,10},{10,... | collective-permute-start | bytes 2359304 | tf_op jit(solution)/shard_map/ppermute | solution.py:69
  990.2 174.1 %collective-permute-start.19 = (bf16[1,8,128,768]{3,2,1,0:T(8,128)(2,1)S(1)}, bf16[1,8,128,768]{3,2,1,0:T(8,128)(2,1)}, u32[]{:S(2)}, u32[]{:S(2)}) collective-permute-start(bf16[1,8,128,768]{3,2,1,0:T(8,128)(2,1)S(1)} %bitcast.298), channel_id=1, source_target_pairs={{0,16},{16,0},{1,17},{17,1},{2,18},{18,2},{3,19},{19,3},{4,20},{20... | collective-permute-start | bytes 4718600 | tf_op jit(solution)/shard_map/ppermute | solution.py:411
  991.6 34.2 %collective-permute-start.18 = (f32[128,16]{0,1:T(8,128)S(1)}, f32[128,16]{0,1:T(8,128)S(1)}, u32[]{:S(2)}, u32[]{:S(2)}) collective-permute-start(f32[128,16]{0,1:T(8,128)S(1)} %convert_element_type.194), channel_id=1, source_target_pairs={{0,16},{16,0},{1,17},{17,1},{2,18},{18,2},{3,19},{19,3},{4,20},{20... | collective-permute-start | bytes 24584 | tf_op jit(solution)/shard_map/ppermute | solution.py:420
  1167.5 6.7 collective-permute-start.22
  1172.1 14.9 %collective-permute-start.17 = (bf16[1,128,2048]{2,1,0:T(8,128)(2,1)S(1)}, bf16[1,128,2048]{2,1,0:T(8,128)(2,1)S(1)}, u32[]{:S(2)}, u32[]{:S(2)}) collective-permute-start(bf16[1,128,2048]{2,1,0:T(8,128)(2,1)S(1)} %convert_bitcast_fusion), channel_id=1, source_target_pairs={{0,16},{16,0},{1,17},{17,1},{2,18},{18,2},{3,19},{19,3},{4,20},{20... | collective-permute-start | bytes 1572872 | tf_op jit(solution)/shard_map/ppermute | solution.py:411
  1173.3 30.6 %collective-permute-start.16 = (bf16[1,4,128,768]{3,2,1,0:T(8,128)(2,1)S(1)}, bf16[1,4,128,768]{3,2,1,0:T(8,128)(2,1)S(1)}, u32[]{:S(2)}, u32[]{:S(2)}) collective-permute-start(bf16[1,4,128,768]{3,2,1,0:T(8,128)(2,1)S(1)} %bitcast.254), channel_id=1, source_target_pairs={{0,16},{16,0},{1,17},{17,1},{2,18},{18,2},{3,19},{19,3},{4,20},{20... | collective-permute-start | bytes 2359304 | tf_op jit(solution)/shard_map/ppermute | solution.py:411
  1184.1 52.2 %collective-permute-start.20 = (bf16[1,8,128,768]{3,2,1,0:T(8,128)(2,1)}, bf16[1,8,128,768]{3,2,1,0:T(8,128)(2,1)}, u32[]{:S(2)}, u32[]{:S(2)}) collective-permute-start(bf16[1,8,128,768]{3,2,1,0:T(8,128)(2,1)} %bitcast.100), channel_id=1, source_target_pairs={{0,16},{16,0},{1,17},{17,1},{2,18},{18,2},{3,19},{19,3},{4,20},{20... | collective-permute-start | bytes 4718600 | tf_op jit(solution)/shard_map/ppermute | solution.py:411
  (56 other events, 621.9 us)
Sparse Core Ops, SparseCore 0:
  9.6 295.2 all-gather.2
  843.5 56.1 reduce-scatter.3

commit v3 on v2

--- a/solution.py
+++ b/solution.py
@@ -16,19 +16,14 @@
 ROW_TILE = 16
 MIB = 1 << 20
 WAIT_LAST = 8
-BRIEF = pl.CostEstimate(flops=0, bytes_accessed=MIB, transcendentals=0)
+LONG = 16
+BRIEF = pl.CostEstimate(flops=0, bytes_accessed=0, transcendentals=0)
 
 
 def normed(values, gain):
     return values * lax.rsqrt(jnp.mean(values * values, axis=-1, keepdims=True) + epsilon) * gain
 
 
-def angles(place, width):
-    steps = jnp.arange(width // 2).astype(jnp.float32)
-    inverse = jnp.exp(steps * (-2.0 * math.log(1000000.0) / width))
-    return place.astype(jnp.float32)[:, None] * inverse[None, :]
-
-
 def dot(left, right):
     return jnp.dot(left, right, preferred_element_type=jnp.float32)
 
@@ -41,8 +36,8 @@
     return lax.dot_general(left, right, (((0,), (0,)), ((), ())), preferred_element_type=jnp.float32)
 
 
-def after(value, *anchors):
-    return lax.optimization_barrier((value,) + anchors)[0]
+def zero_of(anchor):
+    return jnp.minimum(jnp.abs(anchor[(0,) * anchor.ndim].astype(wide)), 0.0)
 
 
 def flat_index(axes):
@@ -58,31 +53,6 @@
 
 def take_at(stack, index, at):
     return lax.dynamic_index_in_dim(stack, index, at, keepdims=False)
-
-
-def exchange(axes, pick):
-    amount = 1 << len(axes)
-    here = flat_index(axes)
-    arrived = [pick(here)]
-    for step in range(1, amount):
-        pairs = [(place, place ^ step) for place in range(amount)]
-        arrived.append(lax.ppermute(pick(jnp.bitwise_xor(here, step)), axes, pairs))
-    return arrived
-
-
-def laid_out(blocks, here, at):
-    if len(blocks) == 1:
-        return jnp.expand_dims(blocks[0], at)
-    if len(blocks) == 2:
-        first = here == 0
-        return jnp.stack(
-            [jnp.where(first, blocks[0], blocks[1]), jnp.where(first, blocks[1], blocks[0])], axis=at
-        )
-    one = blocks[0]
-    held = jnp.zeros(one.shape[:at] + (len(blocks),) + one.shape[at:], one.dtype)
-    for step, block in enumerate(blocks):
-        held = lax.dynamic_update_index_in_dim(held, block, jnp.bitwise_xor(here, step), at)
-    return held
 
 
 def sems(amount):
@@ -105,7 +75,7 @@
 
 
 class Direct:
-    def __init__(self, axes, operand, block, pick, rounds=0):
+    def __init__(self, axes, operand, block, pick=None, rounds=0):
         self.axes, self.block, self.pick, self.rounds = axes, block, pick, rounds
         self.amount = 1 << len(axes)
         self.operands = [operand]
@@ -130,7 +100,7 @@
                 place = lax.axis_index(axis)
                 other = other * 2 + (1 - place if axis in self.steps[step] else place)
             copy = remote(
-                operands[0].at[self.pick(other)],
+                operands[0].at[step if self.pick is None else self.pick(other)],
                 target,
                 send.at[step],
                 recv.at[step],
@@ -141,9 +111,8 @@
         return copies
 
     def keep(self, operands, target, local, held):
-        load = pltpu.make_async_copy(
-            operands[0].at[self.pick(flat_index(self.axes))], held, local.at[0]
-        )
+        own = 0 if self.pick is None else self.pick(flat_index(self.axes))
+        load = pltpu.make_async_copy(operands[0].at[own], held, local.at[0])
         load.start()
         load.wait()
         store = pltpu.make_async_copy(held, target, local.at[1])
@@ -164,8 +133,8 @@
 
 
 class Spread(Direct):
-    def __init__(self, axes, others, operand, block):
-        super().__init__(axes, operand, block, lambda place: place)
+    def __init__(self, axes, others, operand, block, pick=lambda place: place):
+        super().__init__(axes, operand, block, pick)
         self.others = others
         self.results = [
             jax.ShapeDtypeStruct((self.amount,) + (2,) * len(others) + block, operand.dtype)
@@ -247,11 +216,11 @@
 
 
 class Reduce:
-    def __init__(self, axes, operand, parts, owners=()):
-        self.axes, self.parts, self.owners = axes, parts, owners
+    def __init__(self, axes, operand, parts, ready=None, last=None, by_distance=False):
+        self.axes, self.parts, self.by_distance = axes, parts, by_distance
         count, columns = operand.shape[-2:]
         self.operands = [operand]
-        self.results = [jax.ShapeDtypeStruct((count, columns), low if owners else wide)]
+        self.results = [jax.ShapeDtypeStruct((count, columns), wide)]
         self.scratch = []
         for lo, hi, order in parts:
             for stage in range(len(axes)):
@@ -262,20 +231,18 @@
         amount = len(parts) * len(axes)
         self.flips = [(axis,) for axis in axes]
         self.last = None
-        if owners:
-            block = (count >> len(owners), columns)
-            shape = jax.ShapeDtypeStruct((1 << len(owners),) + block, low)
-            self.last = Direct(owners, shape, block, lambda place: place)
+        if last is not None:
+            self.last = last(ready)
             self.results = self.last.results
             self.flips = self.flips + self.last.flips
-            self.scratch += [pltpu.VMEM(shape.shape, low)] + self.last.scratch
+            self.scratch += [pltpu.VMEM(ready.shape, low)] + self.last.scratch
         self.scratch += [sems(amount), sems(amount), sems(len(parts) + 1)]
 
     def run(self, operands, results, scratch):
         stages = len(self.axes)
         send, recv, local = scratch[-3:]
         total = scratch[len(self.parts) * (stages + 1)]
-        place = {axis: lax.axis_index(axis) for axis in self.axes}
+        place = {axis: 0 if self.by_distance else lax.axis_index(axis) for axis in self.axes}
         copies, loads = {}, []
 
         def buffers(number):
@@ -361,7 +328,147 @@
             copy.wait_send()
 
 
-def flow_kernel(flows, *refs):
+class ReduceBoth(Reduce):
+    def __init__(self, axes, operand, other, parts):
+        super().__init__(axes, operand, parts, by_distance=True)
+        self.operands = [operand, other]
+        shape = operand.shape
+        self.scratch = [pltpu.VMEM(shape, low), pltpu.VMEM(shape, low)]
+        for lo, hi, order in parts:
+            for stage in range(len(axes)):
+                left = len(axes) - 1 - stage
+                self.scratch.append(pltpu.VMEM((2,) * left + (hi - lo, shape[-1]), low))
+        self.scratch.append(pltpu.VMEM(shape[-2:], wide))
+        amount = len(parts) * len(axes)
+        self.scratch += [sems(amount), sems(amount), sems(2 * len(parts) + 1)]
+
+    def run(self, operands, results, scratch):
+        stages = len(self.axes)
+        held, added, *slots = scratch[:-4]
+        total, send, recv, local = scratch[-4:]
+        copies, loads = {}, []
+        every = (slice(None),) * stages
+
+        def start(number, stage):
+            lo, hi, order = self.parts[number]
+            spot = tuple(
+                0 if axis in order[:stage] else 1 if axis == order[stage] else slice(None)
+                for axis in self.axes
+            )
+            slot = number * stages + stage
+            copies[number, stage] = remote(
+                held.at[spot + (pl.ds(lo, hi - lo),)],
+                slots[slot],
+                send.at[slot],
+                recv.at[slot],
+                (order[stage],),
+            )
+            copies[number, stage].start()
+
+        def add_all(lo, hi, free, spot_of, source, last):
+            for code in range(1 << len(free)):
+                bits = {axis: code >> bit & 1 for bit, axis in enumerate(free)}
+                spot = tuple(bits.get(axis, 0) for axis in self.axes)
+                source_spot = spot_of(bits)
+
+                def add(step, carry, spot=spot, source_spot=source_spot):
+                    at = pl.multiple_of(step * ROW_TILE, ROW_TILE)
+                    rows = pl.ds(pl.multiple_of(at + lo, ROW_TILE), ROW_TILE)
+                    value = held[spot + (rows,)].astype(wide)
+                    shift = rows if source is added else pl.ds(at, ROW_TILE)
+                    value = value + source[source_spot + (shift,)].astype(wide)
+                    if last:
+                        total[rows] = value
+                    else:
+                        held[spot + (rows,)] = value.astype(low)
+                    return carry
+
+                lax.fori_loop(0, (hi - lo) // ROW_TILE, add, 0)
+
+        for number, (lo, hi, order) in enumerate(self.parts):
+            span = every + (pl.ds(lo, hi - lo),)
+            for which, (operand, buffer) in enumerate(zip(operands, (held, added))):
+                load = pltpu.make_async_copy(
+                    operand.at[span], buffer.at[span], local.at[2 * number + which]
+                )
+                load.start()
+                loads.append(load)
+        for number, (lo, hi, order) in enumerate(self.parts):
+            loads[2 * number].wait()
+            loads[2 * number + 1].wait()
+            add_all(
+                lo, hi, self.axes, lambda bits: tuple(bits[axis] for axis in self.axes), added, False
+            )
+            start(number, 0)
+        yield
+        for stage in range(stages):
+            for number, (lo, hi, order) in enumerate(self.parts):
+                copies[number, stage].wait_recv()
+                free = [axis for axis in self.axes if axis not in order[: stage + 1]]
+                add_all(
+                    lo,
+                    hi,
+                    free,
+                    lambda bits, free=free: tuple(bits[axis] for axis in free),
+                    slots[number * stages + stage],
+                    stage == stages - 1,
+                )
+                if stage + 1 < stages:
+                    start(number, stage + 1)
+            yield
+        store = pltpu.make_async_copy(total, results[0], local.at[2 * len(self.parts)])
+        store.start()
+        store.wait()
+        for copy in copies.values():
+            copy.wait_send()
+
+
+class Task:
+    flips = ()
+
+
+class WeightGrad(Task):
+    def __init__(self, lefts, rights, left_half, right_half, rows, tile=256):
+        self.amount, self.rows, self.tile = len(lefts), rows, tile
+        self.halves = left_half, right_half
+        self.operands = list(lefts) + list(rights)
+        self.columns, self.width = lefts[0].shape[-1], rights[0].shape[-1]
+        self.blocks = lefts[0].shape[0]
+        self.results = [jax.ShapeDtypeStruct((self.columns, self.width), low)]
+        shape = (self.amount, self.blocks, rows, self.width)
+        self.scratch = [pltpu.VMEM(shape, low), sems(self.amount)]
+
+    def run(self, operands, results, scratch, lo=0, hi=None):
+        held, done = scratch
+        at = pl.ds(self.halves[1] * self.rows, self.rows)
+        copies = [
+            pltpu.make_async_copy(right.at[:, at], held.at[number], done.at[number])
+            for number, right in enumerate(operands[self.amount :])
+        ]
+        for copy in copies:
+            copy.start()
+        for copy in copies:
+            copy.wait()
+
+        def body(*refs):
+            total = 0.0
+            for number, left_ref in enumerate(refs[:-1]):
+                right = held[number].reshape(-1, self.width)
+                total = total + dot_tn(left_ref[...].reshape(-1, self.tile), right)
+            refs[-1][...] = total.astype(low)
+
+        block = pl.BlockSpec(
+            (self.blocks, self.rows, self.tile), lambda step: (0, self.halves[0], step)
+        )
+        pltpu.emit_pipeline(
+            body,
+            grid=(self.columns // self.tile,),
+            in_specs=[block] * self.amount,
+            out_specs=[pl.BlockSpec((self.tile, self.width), lambda step: (step, 0))],
+        )(*operands[: self.amount], results[0])
+
+
+def flow_kernel(flows, plan, *refs):
     refs = list(refs)
 
     def cut(amount):
@@ -381,44 +488,39 @@
             barrier, inc=1, device_id=toward(flips), device_id_type=pl.DeviceIdType.MESH
         )
     pl.semaphore_wait(barrier, len(partners))
-    running = [flow.run(*parts) for flow, *parts in zip(flows, operands, results, scratch)]
-    while running:
-        running = [run for run in running if next(run, run) is not run]
-
-
-def transfer(number, flows):
+    tasks = [part for part in zip(flows, operands, results, scratch) if isinstance(part[0], Task)]
+    runs = [
+        flow.run(*parts)
+        for flow, *parts in zip(flows, operands, results, scratch)
+        if not isinstance(flow, Task)
+    ]
+    for run in runs:
+        next(run)
+    for number in plan:
+        if number < 0:
+            flow, *parts = tasks[-1 - number]
+            flow.run(*parts)
+        elif number < len(runs):
+            next(runs[number], None)
+    while runs:
+        runs = [run for run in runs if next(run, run) is not run]
+
+
+def transfer(number, flows, plan=()):
     arrays = [array for flow in flows for array in flow.operands]
     shapes = [shape for flow in flows for shape in flow.results]
     anywhere = pl.BlockSpec(memory_space=pl.ANY)
     return pl.pallas_call(
-        functools.partial(flow_kernel, flows),
+        functools.partial(flow_kernel, flows, plan),
         out_shape=shapes,
         in_specs=[anywhere] * len(arrays),
         out_specs=[anywhere] * len(shapes),
         scratch_shapes=[one for flow in flows for one in flow.scratch],
         compiler_params=pltpu.CompilerParams(
-            collective_id=number, has_side_effects=True, vmem_limit_bytes=52 * MIB
+            collective_id=number, has_side_effects=True, vmem_limit_bytes=60 * MIB
         ),
         cost_estimate=BRIEF,
     )(*arrays)
-
-
-def gather_blocks(block, axes, at):
-    if not axes:
-        return block
-    if len(axes) > 1:
-        return lax.all_gather(block, axes, axis=at, tiled=True)
-    other = lax.ppermute(block, axes[0], SWAP)
-    first = lax.axis_index(axes[0]) == 0
-    return jnp.concatenate(
-        [jnp.where(first, block, other), jnp.where(first, other, block)], axis=at
-    )
-
-
-def sum_all(value, axes):
-    for axis in axes:
-        value = value + lax.ppermute(value, axis, SWAP)
-    return value
 
 
 def tile_of(rows, most):
@@ -433,18 +535,40 @@
 
 
 def expert_kernel(
+    near,
+    ids_ref,
     rows_ref,
     grad_ref,
     gate_ref,
-    in_ref,
-    down_ref,
+    pieces_in,
+    pieces_down,
     hidden_ref,
-    d_act_ref,
-    d_up_ref,
+    d_in_ref,
     d_gate_ref,
     made_ref,
     back_ref,
+    in_ref,
+    down_ref,
+    done,
 ):
+    @pl.when(pl.program_id(0) == 0)
+    def _():
+        copies = []
+        for pieces, held in ((pieces_in, in_ref), (pieces_down, down_ref)):
+            amount, parts, rows = pieces.shape[:3]
+            for spot in range(amount):
+                for part in range(parts):
+                    block = (part // near * amount + spot) * near + part % near
+                    copy = pltpu.make_async_copy(
+                        pieces.at[spot, part],
+                        held.at[pl.ds(block * rows, rows)],
+                        done.at[len(copies)],
+                    )
+                    copy.start()
+                    copies.append(copy)
+        for copy in copies:
+            copy.wait()
+
     hidden_width = down_ref.shape[0]
     gate = gate_ref[...]
     acts = dot(rows_ref[...], in_ref[...])
@@ -459,56 +583,69 @@
     d_act_gate = d_hidden * act_up * (sigmoid * (1.0 + act_gate * (1.0 - sigmoid)))
     d_in = jnp.concatenate([d_act_gate.astype(low), (d_hidden * silu_gate).astype(low)], axis=1)
     hidden_ref[...] = hidden_low
-    d_act_ref[...] = d_in[:, :hidden_width]
-    d_up_ref[...] = d_in[:, hidden_width:]
+    d_in_ref[...] = d_in
     back_ref[...] = dot_nt(d_in, in_ref[...]).astype(low)
     made_ref[...] = dot(hidden_low, down_ref[...]).astype(low)
 
 
-def expert_rows(rows, grad_rows, gate, full_in, full_down):
-    amount, model_width = rows.shape
-    hidden_width = full_down.shape[0]
-    tile = tile_of(amount, 256)
-
-    def by_rows(columns):
-        return pl.BlockSpec((tile, columns), lambda step: (step, 0))
+def expert_rows(rows, gate, pieces_in, pieces_down, near, ids):
+    blocks, tile, model_width = rows.shape
+    tile = tile // 2
+    pieces = (pieces_in, pieces_down)
+    amount = blocks * tile
+    hidden_width = pieces_in.shape[3] // 2
+
+    def half(which):
+        return pl.BlockSpec((None, tile, model_width), lambda step, ids: (ids[step], which, 0))
+
+    def by_place(columns):
+        return pl.BlockSpec((tile, columns), lambda step, ids: (ids[step], 0))
+
+    def by_distance(columns):
+        return pl.BlockSpec((tile, columns), lambda step, ids: (step, 0))
 
     outs = [
-        (hidden_width, low),
-        (hidden_width, low),
-        (hidden_width, low),
-        (1, wide),
-        (model_width, low),
-        (model_width, low),
+        (by_place, hidden_width, low),
+        (by_place, 2 * hidden_width, low),
+        (by_distance, 1, wide),
+        (by_distance, model_width, low),
+        (by_distance, model_width, low),
     ]
+    anywhere = pl.BlockSpec(memory_space=pl.ANY)
     return pl.pallas_call(
-        expert_kernel,
-        grid=(amount // tile,),
-        in_specs=[
-            by_rows(model_width),
-            by_rows(model_width),
-            by_rows(1),
-            whole_block(full_in.shape),
-            whole_block(full_down.shape),
-        ],
-        out_specs=[by_rows(columns) for columns, _ in outs],
-        out_shape=[jax.ShapeDtypeStruct((amount, columns), kind) for columns, kind in outs],
+        functools.partial(expert_kernel, near),
+        grid_spec=pltpu.PrefetchScalarGridSpec(
+            num_scalar_prefetch=1,
+            grid=(blocks,),
+            in_specs=[half(0), half(1), by_place(1)]
+            + [anywhere] * len(pieces),
+            out_specs=[spec(columns) for spec, columns, _ in outs],
+            scratch_shapes=[
+                pltpu.VMEM((model_width, 2 * hidden_width), low),
+                pltpu.VMEM((hidden_width, model_width), low),
+                sems(sum(piece.shape[0] * piece.shape[1] for piece in pieces)),
+            ],
+        ),
+        out_shape=[jax.ShapeDtypeStruct((amount, columns), kind) for _, columns, kind in outs],
         compiler_params=pltpu.CompilerParams(vmem_limit_bytes=52 * MIB),
-        cost_estimate=BRIEF,
-    )(rows, grad_rows, gate, full_in, full_down)
+        cost_estimate=pl.CostEstimate(
+            flops=LONG * 18 * amount * model_width * hidden_width,
+            bytes_accessed=14 * amount * model_width,
+            transcendentals=0,
+        ),
+    )(ids, rows, rows, gate, *pieces)
 
 
 def weight_kernel(amount, *refs):
-    total = dot_tn(refs[0][...], refs[amount][...])
-    for step in range(1, amount):
-        total = total + dot_tn(refs[step][...], refs[amount + step][...])
+    total = 0.0
+    for left, right in zip(refs[:amount], refs[amount:-1]):
+        total = total + dot_tn(left[...], right[...])
     refs[-1][...] = total.astype(low)
 
 
 def weight_grad(lefts, rights, tile=256):
     amount = len(lefts)
     columns, out_columns = lefts[0].shape[1], rights[0].shape[1]
-    rows = sum(left.shape[0] for left in lefts)
     return pl.pallas_call(
         functools.partial(weight_kernel, amount),
         grid=(columns // tile,),
@@ -521,6 +658,31 @@
     )(*lefts, *rights)
 
 
+def widen_kernel(pieces_ref, *out_refs):
+    columns = out_refs[0].shape[1]
+    for number, out_ref in enumerate(out_refs):
+        span = slice(number * columns, (number + 1) * columns)
+        out_ref[...] = pieces_ref[:, span].astype(wide)
+
+
+def by_expert(pieces, amount):
+    team, rows, columns = pieces.shape[0], pieces.shape[-2], pieces.shape[-1]
+    pieces = pieces.reshape(team, -1, rows, columns)
+    groups = pieces.shape[1]
+    out = (groups * team, rows, columns // amount)
+    return pl.pallas_call(
+        widen_kernel,
+        grid=(groups, team),
+        in_specs=[pl.BlockSpec((None, None, rows, columns), lambda group, place: (place, group, 0, 0))],
+        out_specs=[
+            pl.BlockSpec((None,) + out[1:], lambda group, place: (group * team + place, 0, 0))
+        ]
+        * amount,
+        out_shape=[jax.ShapeDtypeStruct(out, wide)] * amount,
+        cost_estimate=BRIEF,
+    )(pieces)
+
+
 def turned(values, cosine, sine):
     return values * cosine + pltpu.roll(values, values.shape[1] // 2, 1) * sine
 
@@ -534,10 +696,26 @@
 
 
 def prep_kernel(
-    heads, rows_ref, w_ref, cosine_ref, sine_ref, gain_q, gain_k, lin_ref, query_ref, keyed_ref, value_ref
+    heads,
+    rows_ref,
+    w_ref,
+    place_ref,
+    inverse_ref,
+    sign_ref,
+    gain_q,
+    gain_k,
+    lin_ref,
+    query_ref,
+    keyed_ref,
+    value_ref,
+    cosine_ref,
+    sine_ref,
 ):
     width = gain_q.shape[1]
-    cosine, sine = cosine_ref[...], sine_ref[...]
+    angle = place_ref[...].astype(wide) * inverse_ref[...]
+    cosine, sine = jnp.cos(angle), jnp.sin(angle) * sign_ref[...]
+    cosine_ref[...] = cosine
+    sine_ref[...] = sine
     lin = dot(rows_ref[...], w_ref[...])
     lin_ref[...] = lin[:, : (heads + 1) * width]
     for head in range(heads + 1):
@@ -564,10 +742,13 @@
     sine_ref,
     gain_q,
     gain_k,
+    rows_ref,
+    gain_ref,
     d_lin_ref,
     d_one_ref,
     d_gain_q,
     d_gain_k,
+    d_gain,
 ):
     width = gain_q.shape[1]
     cosine, sine = cosine_ref[...], sine_ref[...]
@@ -576,23 +757,26 @@
     def _():
         d_gain_q[...] = jnp.zeros_like(d_gain_q)
         d_gain_k[...] = jnp.zeros_like(d_gain_k)
+        d_gain[...] = jnp.zeros_like(d_gain)
 
     for head in range(heads + 1):
         span = slice(head * width, (head + 1) * width)
         values = lin_ref[:, span]
         if head < heads:
-            grads, gain, d_gain = d_query_ref[:, span].astype(wide), gain_q[...], d_gain_q
+            grads, gain, d_head = d_query_ref[:, span].astype(wide), gain_q[...], d_gain_q
         else:
-            grads, gain, d_gain = d_keyed_ref[...] * scale, gain_k[...], d_gain_k
+            grads, gain, d_head = d_keyed_ref[...] * scale, gain_k[...], d_gain_k
         grads = turned_back(grads, cosine, sine)
         factor = head_scale(values)
         plain = values * factor
-        d_gain[...] += jnp.sum(grads * plain, axis=0, keepdims=True)
+        d_head[...] += jnp.sum(grads * plain, axis=0, keepdims=True)
         grads = grads * gain
         mean = jnp.mean(grads * plain, axis=1, keepdims=True)
         d_lin_ref[:, span] = (factor * (grads - plain * mean)).astype(low)
     d_lin_ref[:, (heads + 1) * width :] = d_value_ref[...].astype(low)
-    d_one_ref[...] = dot_nt(d_lin_ref[...], w_ref[...]).astype(low)
+    d_one = dot_nt(d_lin_ref[...], w_ref[...])
+    d_one_ref[...] = d_one.astype(low)
+    d_gain[...] += jnp.sum(d_one * rows_ref[...].astype(wide), axis=0, keepdims=True) / gain_ref[...]
 
 
 def row_call(kernel, rows, tiled, fixed, outs, sums):
@@ -745,6 +929,7 @@
     plane_axes = g_axes + c_axes
     cluster_axes = g_axes + team_axes
     all_axes = g_axes + c_axes + f_axes
+    all_axes_but_core = c_axes[:-1] + f_axes[::-1] + g_axes
     g_here = flat_index(g_axes)
     core = c_axes[-1:]
     plane_shape = (2,) * len(plane_axes) + (count, model_width)
@@ -786,19 +971,18 @@
     resid = tokens[0].astype(jnp.float32)
     norm_one, back_one = jax.vjp(normed, resid, gain_attn)
 
-    def own_experts(place):
-        return flat_index(g_axes) * parts_c + place
-
-    def by_team(pieces):
-        return pieces.reshape((groups * parts_c, parts_near) + pieces.shape[1:])
+    def own_expert(place):
+        return flat_index(g_axes) * team + place
 
     mine_out = take(w_out.reshape(groups, -1, model_width), g_here) if even else w_out
-    all_grads = lax.all_gather(cotangent[0], cluster_axes, axis=0, tiled=True)
-    w_qkv, all_one, full_router, marks, w_mix, got_in, got_down = transfer(
+    all_one, w_qkv, pieces_down, w_mix, got_in, full_router, marks = transfer(
         1,
         [
+            Gather(plane_axes, norm_one.astype(low), core_last(plane_parts)),
             Spread(c_axes, f_axes, mine_qkv, (rows_d, qkv_cols)),
-            Gather(plane_axes, norm_one.astype(low), core_last(plane_parts)),
+            Spread(team_axes, far_axes, w_down, w_down.shape[1:], own_expert),
+            Gather(f_axes, mine_out, [(0, mine_out.shape[0], f_axes)]),
+            Direct(team_axes, own_in, own_in.shape[1:], own_expert),
             Direct(own_axes, wide_router[None], wide_router.shape, lambda place: 0),
             Direct(
                 g_axes,
@@ -806,10 +990,8 @@
                 (2,) + places.shape[1:],
                 lambda place: 0,
             ),
-            Gather(f_axes, mine_out, [(0, mine_out.shape[0], f_axes)]),
-            Direct(c_axes, by_team(own_in), (parts_near,) + own_in.shape[1:], own_experts, 2),
-            Direct(c_axes, by_team(w_down), (parts_near,) + w_down.shape[1:], own_experts, 2),
         ],
+        (1, 0, 2, 0, 3, 1),
     )
     w_qkv = w_qkv.reshape(model_width, qkv_cols)
     all_one = all_one.reshape(-1, model_width)
@@ -818,30 +1000,30 @@
     w_mix = w_mix.reshape(-1, model_width)
     if not even:
         w_mix = take(w_mix.reshape(groups, q_cols, model_width), g_here)
-    f_here = flat_index(f_axes)
-    near_here = flat_index(near_axes)
-
-    def whole_expert(got):
-        arrived = exchange(f_axes, lambda other: take_at(got, other % parts_near, 1))
-        return laid_out(arrived, f_here, 1)
-
-    full_in = whole_expert(got_in).reshape(model_width, 2 * hidden_width)
-    full_down = whole_expert(got_down).reshape(hidden_width, model_width)
+
+    def from_far(got):
+        return lax.all_gather(got, far_axes, axis=0, tiled=False) if far_axes else got[None]
+
+    pieces_in = from_far(got_in)
+    pieces_down = pieces_down.reshape((team, -1) + w_down.shape[1:]).transpose(1, 0, 2, 3)
+    if rows_f % ROW_TILE:
+        pieces_down = pieces_down.reshape((-1, parts_c, parts_near) + w_down.shape[1:])
+        pieces_down = pieces_down.transpose(1, 0, 2, 3, 4).reshape(1, 1, hidden_width, model_width)
 
     place, segment = marks[:, 0], marks[:, 1]
     length = place.shape[1]
-    angle = angles(place.reshape(-1), width)
-    cosine, sine = jnp.cos(angle), jnp.sin(angle)
-    cosine = jnp.concatenate([cosine, cosine], axis=1)
-    sine = jnp.concatenate([-sine, sine], axis=1)
-    tables = (cosine, sine, gain_query[None], gain_key[None])
     rows = groups * length
-    lin, query_low, keyed_low, value_low = row_call(
+    steps = jnp.arange(width // 2).astype(wide)
+    inverse = jnp.exp(steps * (-2.0 * math.log(1000000.0) / width))
+    inverse = jnp.concatenate([inverse, inverse])[None]
+    sign = jnp.where(jnp.arange(width) < width // 2, -1.0, 1.0)[None]
+    head_gains = (gain_query[None], gain_key[None])
+    lin, query_low, keyed_low, value_low, cosine, sine = row_call(
         functools.partial(prep_kernel, heads),
         rows,
-        (all_one, w_qkv) + tables,
-        (1, 4, 5),
-        [(q_cols + width, wide), (q_cols, low), (width, low), (width, low)],
+        (all_one, w_qkv, place.reshape(rows, 1), inverse, sign) + head_gains,
+        (1, 3, 4, 5, 6),
+        [(q_cols + width, wide), (q_cols, low), (width, low), (width, low), (width, wide), (width, wide)],
         [],
     )
     query_low = query_low.reshape(groups, length, q_cols)
@@ -872,48 +1054,62 @@
     powers = jnp.where(chosen, jnp.exp(logits - jnp.max(logits, axis=-1, keepdims=True)), 0.0)
     gates = powers / jnp.sum(powers, axis=-1, keepdims=True)
 
-    all_two, all_gates = transfer(
+    grad_parts = [(lo + count, hi + count, order) for lo, hi, order in cluster_parts]
+    own_rows, all_gates = transfer(
         3,
         [
-            Gather(cluster_axes, normed_two, core_last(cluster_parts)),
+            Gather(
+                turn,
+                jnp.concatenate([normed_two, cotangent[0]], axis=0),
+                cluster_parts + grad_parts,
+            ),
             Gather(cluster_axes, gates.T, [(0, experts, turn + core)]),
         ],
     )
-    all_two = all_two.reshape(-1, model_width)
-    gate = lax.dynamic_index_in_dim(
-        all_gates.reshape(-1, experts, count), flat_index(cluster_axes), 1, keepdims=False
-    )
-    hiddens, d_acts, d_ups, d_gate, made, back = expert_rows(
-        all_two, all_grads, gate.reshape(-1, 1), full_in, full_down
-    )
-    d_rows_two, d_gates = transfer(
+    blocks = 1 << len(turn)
+    own_rows = own_rows.reshape(blocks, 2 * count, model_width)
+    far_rows = lax.ppermute(own_rows, core[0], SWAP)
+    gate_stack = take_at(all_gates, flat_index(cluster_axes), len(cluster_axes))
+    core_here, core_spot = lax.axis_index(core[0]), cluster_axes.index(core[0])
+    ids = jnp.bitwise_xor(jnp.arange(blocks), flat_index(turn)).astype(jnp.int32)
+    sides = []
+    for side, side_rows in ((core_here, own_rows), (1 - core_here, far_rows)):
+        gate = take_at(gate_stack, side, core_spot).reshape(-1, 1)
+        sides.append(expert_rows(side_rows, gate, pieces_in, pieces_down, parts_near, ids))
+        ids = ids + zero_of(sides[0][2]).astype(jnp.int32)
+    hiddens, d_ins, d_gate_parts, made_parts, back_parts = zip(*sides)
+    half_shape = (2,) * len(turn) + (count, model_width)
+    far_back = lax.ppermute(back_parts[1], core[0], SWAP)
+    far_made = lax.ppermute(made_parts[1], core[0], SWAP)
+    d_gates = jnp.stack(d_gate_parts).reshape(experts, 1, count)
+    both_rows = [own_rows, far_rows]
+    hiddens = [part.reshape(blocks, count, hidden_width) for part in hiddens]
+    d_ins = [part.reshape(blocks, count, 2 * hidden_width) for part in d_ins]
+    back = [part.reshape(half_shape) for part in (back_parts[0], far_back)]
+    d_rows_two, d_gates, part_down, part_in = transfer(
         4,
         [
-            Reduce(cluster_axes, back.reshape(cluster_shape), core_first(cluster_parts)),
-            Direct(
-                cluster_axes, d_gate.reshape(experts, 1, count), (1, count), lambda place: place
-            ),
+            ReduceBoth(turn, *back, cluster_parts),
+            Direct(core + turn, d_gates, (1, count)),
+            WeightGrad(hiddens, both_rows, 0, 1, count),
+            WeightGrad(both_rows, d_ins, 0, 0, count),
         ],
-    )
-
-    def over_fsdp(part, rows):
-        stack = part.reshape(parts_c, parts_f, rows, -1)
-        arrived = exchange(f_axes, lambda other: take_at(stack, other, 1))
-        sums = []
-        for near in range(parts_near):
-            total = arrived[near].astype(wide)
-            for step in range(near + parts_near, parts_f, parts_near):
-                total = total + arrived[step].astype(wide)
-            sums.append(total.astype(low))
-        return laid_out(sums, near_here, 1)
-
-    part_down = weight_grad([after(hiddens, d_rows_two)], [all_grads])
-    part_gate = weight_grad([all_two], [after(d_acts, part_down)])
-    part_up = weight_grad([all_two], [after(d_ups, part_gate)])
-    share_down = over_fsdp(part_down, rows_f)
-    share_gate = over_fsdp(part_gate, rows_d)
-    share_up = over_fsdp(part_up, rows_d)
-    d_gates = d_gates.reshape(experts, count).T
+        (-1, 0, -2),
+    )
+    d_gates = d_gates.reshape((2,) * len(cluster_axes) + (count,))
+    spots = [(core + turn).index(axis) for axis in cluster_axes]
+    d_gates = d_gates.transpose(spots + [len(spots)]).reshape(experts, count).T
+
+    reduced = zero_of(d_rows_two).astype(low)
+
+    def to_far(part, rows):
+        stack = part.reshape(parts_c, -1, parts_near, rows, part.shape[1]) + reduced
+        stack = stack.transpose(1, 0, 2, 3, 4).reshape(-1, team, rows, part.shape[1])
+        if not far_axes:
+            return stack[0]
+        return lax.psum_scatter(stack, far_axes, scatter_dimension=0, tiled=False)
+
+    share_down, share_in = to_far(part_down, rows_f), to_far(part_in, rows_d)
 
     d_logits = (gates * (d_gates - jnp.sum(gates * d_gates, axis=-1, keepdims=True))).astype(low)
     part_router = dot_tn(normed_two, d_logits)
@@ -921,16 +1117,16 @@
     d_resid_one, d_gain_ffn = back_two(d_normed_two)
     d_resid_one = d_resid_one + cotangent[0].astype(jnp.float32)
     wide_part = jnp.pad(part_router.astype(low), ((0, 0), (0, width - experts)))
-    share_router = lax.psum_scatter(wide_part, own_axes, scatter_dimension=0, tiled=True)
-    grad_router = sum_all(share_router[:, :experts].astype(jnp.float32), g_axes)
-
-    made_shape = (2,) * len(plane_axes) + (parts_near * count, model_width)
-    made_parts = [(lo * parts_near, hi * parts_near, order) for lo, hi, order in plane_parts]
+
+    made_axes = turn[: len(turn) - len(near_axes)]
+    made_shape = (2,) * len(made_axes) + (parts_near * count, model_width)
+    made = (made_parts[0].reshape(made_shape), far_made.reshape(made_shape))
+    made_spans = [(lo * parts_near, hi * parts_near, order) for lo, hi, order in plane_parts]
     d_branch, made = transfer(
         5,
         [
             Gather(plane_axes, d_resid_one.astype(low), core_last(plane_parts)),
-            Reduce(plane_axes, made.reshape(made_shape), core_first(made_parts)),
+            ReduceBoth(made_axes, *made, made_spans),
         ],
     )
     d_branch = d_branch.reshape(-1, model_width)
@@ -950,15 +1146,7 @@
         scale,
         10,
     )
-    def to_owner(share):
-        return Direct(c_axes, share, share.shape[1:], lambda place: place)
-
-    share_down, share_gate = transfer(
-        6, [to_owner(after(share_down, d_query)), to_owner(after(share_gate, d_query))]
-    )
-    share_down = gather_blocks(share_down.reshape((1, -1) + share_down.shape[2:]), g_axes, 0)
-    share_gate = gather_blocks(share_gate.reshape((1, -1) + share_gate.shape[2:]), g_axes, 0)
-    d_lin, d_one, d_gain_query, d_gain_key = row_call(
+    d_lin, d_one, d_gain_query, d_gain_key, d_gain_attn = row_call(
         functools.partial(unprep_kernel, heads, scale),
         rows,
         (
@@ -967,11 +1155,14 @@
             d_value.reshape(rows, width),
             lin,
             w_qkv,
+            cosine,
+            sine,
         )
-        + tables,
-        (4, 7, 8),
+        + head_gains
+        + (all_one, gain_attn[None]),
+        (4, 7, 8, 10),
         [(qkv_cols, low), (model_width, low)],
-        [width, width],
+        [width, width, model_width],
     )
     d_one = d_one.reshape(plane_shape)
     part_out = weight_grad([mixed_rows], [d_branch])
@@ -981,47 +1172,69 @@
         stack = part.reshape(parts_c, parts_f, rows_d, -1).transpose(1, 0, 2, 3)
         return stack.reshape((2,) * len(f_axes) + (parts_c * rows_d, -1))
 
+    turn_back = plane_axes[len(g_axes) : -1] + g_axes
+    def over_groups(shape):
+        return Gather(g_axes, shape, [(0, shape.shape[0], g_axes)])
+
+    def to_column_owners(shape):
+        return Spread(c_axes, g_axes, shape, shape.shape[1:])
+
     flows = [
+        Spread(team_axes, g_axes, share_down, share_down.shape[1:]),
+        Spread(team_axes, g_axes, share_in, share_in.shape[1:]),
+        Reduce(plane_axes, d_one, core_first([(lo, hi, turn_back) for lo, hi, _ in plane_parts])),
         Reduce(
             f_axes,
-            after(by_f(part_qkv), share_down),
+            by_f(part_qkv),
             [(0, parts_c * rows_d, f_axes[::-1])],
-            c_axes,
+            jax.ShapeDtypeStruct((parts_c, rows_d, qkv_cols), low),
+            to_column_owners,
         ),
-        Reduce(plane_axes, d_one, core_first(plane_parts)),
-        to_owner(share_up),
+        Reduce(
+            own_axes,
+            wide_part.reshape((2,) * len(own_axes) + (rows_d, width)),
+            [(0, rows_d, own_axes)],
+            jax.ShapeDtypeStruct((rows_d, width), low),
+            over_groups,
+        ),
     ]
+    if even:
+        rows = q_cols // parts_f
+        stack = part_out.reshape((2,) * len(f_axes) + (rows, model_width))
+        shape = jax.ShapeDtypeStruct((rows, model_width), low)
+        flows.append(Reduce(f_axes, stack, [(0, rows, f_axes[::-1])], shape, over_groups))
     if near_axes:
         near_shape = (2,) * len(near_axes) + (count, model_width)
         near_flow = Reduce(
-            near_axes, made.astype(low).reshape(near_shape), [(0, count, near_axes)]
+            near_axes, made.astype(low).reshape(near_shape), [(0, count, near_axes)], by_distance=True
         )
         flows.append(near_flow)
+    gains = jnp.concatenate([d_gain_attn[0], d_gain_ffn, d_gain_query[0], d_gain_key[0]])
+    lines = -(-gains.size // (8 * width)) * 8
+    gains = jnp.pad(gains, (0, lines * width - gains.size)).reshape(lines, width)
+    flows.insert(5, Gather(all_axes, gains, [(0, lines, core + all_axes_but_core)]))
+    all_down, all_in, d_one, all_qkv, share_router, gains, *rest = transfer(
+        7, flows, (2, 0, 1, 2, 3, 7, 6, 4, 5, 3, 3, 6, 6, 4, 5, 3, 4, 5)
+    )
+    gains = jnp.sum(gains.reshape(-1, lines * width), axis=0)
+    share_router = share_router.reshape(groups, rows_d, width)[:, :, :experts]
+    grad_router = jnp.sum(share_router.astype(wide), axis=0)
+    if near_axes:
+        made = rest.pop()
+    output = (resid_one + made).astype(low)[None]
+    d_resid = back_one(d_one)[0]
+    grad_tokens = (d_resid + d_resid_one)[None]
+    grad_down, = by_expert(all_down, 1)
+    grad_gate, grad_up = by_expert(all_in, 2)
     if even:
-        rows = q_cols // parts_f
-        stack = part_out.reshape((2,) * len(f_axes) + (rows, model_width))
-        flows.append(Reduce(f_axes, stack, [(0, rows, f_axes[::-1])]))
-    share_qkv, d_one, share_up, *rest = transfer(7, flows)
-    if near_axes:
-        made = rest.pop(0)
-    output = (resid_one + made).astype(low)[None]
-    d_resid, d_gain_attn = back_one(d_one)
-    grad_tokens = (d_resid + d_resid_one)[None]
-    share_up = gather_blocks(share_up.reshape((1, -1) + share_up.shape[2:]), g_axes, 0)
-    grad_gate, grad_up, grad_down = [
-        share.reshape((experts,) + share.shape[2:]).astype(wide)
-        for share in (share_gate, share_up, share_down)
-    ]
-    if even:
-        share_out = rest[0].astype(low)[None]
-        grad_out = gather_blocks(share_out, g_axes, 0).astype(wide).reshape(rows_o, model_width)
+        grad_out = rest[0].astype(wide).reshape(rows_o, model_width)
     else:
         stack = jnp.where(jnp.arange(groups)[:, None, None] == g_here, part_out[None], 0)
         share_out = lax.psum_scatter(
             stack.reshape(groups * q_cols, model_width), f_axes, scatter_dimension=0, tiled=True
         )
-        grad_out = sum_all(share_out.astype(wide), g_axes)
-    all_qkv = gather_blocks(share_qkv[None], g_axes, 0).astype(wide)
+        grad_out = lax.psum(share_out.astype(wide), g_axes)
+    all_qkv = all_qkv.reshape(parts_c, groups, rows_d, qkv_cols).transpose(1, 0, 2, 3).astype(wide)
     grad_query = all_qkv[:, :, :, :q_cols]
     if even:
         grad_query = grad_query.reshape(groups, parts_c, rows_d, parts_f, q_cols // parts_f)
@@ -1032,9 +1245,6 @@
     grad_key = grad_kv[:, :, :width].reshape(rows_d, -1)
     grad_value = grad_kv[:, :, width:].reshape(rows_d, -1)
 
-    gains = sum_all(
-        jnp.concatenate([d_gain_attn, d_gain_ffn, d_gain_query[0], d_gain_key[0]]), all_axes
-    )
     return (
         output,
         grad_tokens,
@@ -1049,7 +1259,7 @@
         gains[:model_width],
         gains[model_width : 2 * model_width],
         gains[2 * model_width : 2 * model_width + width],
-        gains[2 * model_width + width :],
+        gains[2 * model_width + width : 2 * model_width + 2 * width],
     )
 
 

time: 1260 us -> 1210 us (0.960)
  Pallas kernels: 972 us -> 1060 us
  waiting for transfers between devices: 97 us -> 14.8 us
  starting transfers between devices: 29.4 us -> 0.77 us
  other arithmetic: 54.3 us -> 38.8 us
    pallas_call x8 -> x10, Pallas kernels: 781 us -> 920 us  [the longest x6 794 us: transfer(): pl.pallas_call(functools.partial(flow_kernel, flows, plan), out_shape=sha...]
    ppermute x26 -> x3, waiting for transfers between devices: 96.3 us -> 14.7 us  [the longest x1 9.59 us: per_device(): far_back = lax.ppermute(back_parts[1], core[0], SWAP)]
    pallas_call x5 -> x2, Pallas kernels: 81 us -> 22.4 us  [weight_grad(): pl.pallas_call(functools.partial(weight_kernel, amount), grid=(columns //...]
    ppermute x26 -> x3, starting transfers between devices: 29.4 us -> 0.65 us  [the longest x1 0.43 us: per_device(): far_rows = lax.ppermute(own_rows, core[0], SWAP)]
    dynamic_update_slice x6 -> x0, local copies, waits for them, and re-layouts: 12.9 us -> none  [laid_out(): lax.dynamic_update_index_in_dim(held, block, jnp.bitwise_xor(here, step),...]
  transfers between devices with their start and end apart: 28 -> 6, of which waited for: 8 -> 2; matrix products, arithmetic and copies ran while one was open for 9% -> 5% of each run, Pallas kernels for 59% -> 40%
where the time goes in v3:
time: 1210 us
  Pallas kernels  1060 us (88%)
  local copies, waits for them, and re-layouts  62.5 us (5%)
  other arithmetic  38.8 us (3%)
  matrix products  19.5 us (2%)
  between operations  16.1 us (1%)
  waiting for transfers between devices  14.8 us (1%)
    pallas_call x6, Pallas kernels, transfer(): pl.pallas_call(functools.partial(flow_kernel, flows, plan), out_shape=sha...  794 us
    pallas_call x2, Pallas kernels, expert_rows(): pl.pallas_call(functools.partial(expert_kernel, near), grid_spec=pltpu.Pr...  103 us
    pallas_call x2, Pallas kernels, attention_call(): pl.pallas_call(functools.partial(kernel, scale), grid=(seqs, length // ti...  71.9 us
    pallas_call x2, Pallas kernels, row_call(): pl.pallas_call(kernel, grid=(rows // tile,), in_specs=[whole_block(array....  41.3 us
  transfers between devices with their start and end apart: 6, of which 2 were waited for; matrix products, arithmetic and copies ran while one was open for 5% of the time, Pallas kernels for 40%

profile of v3, /device:TPU:0, one launch (start us, length us, event | category | flops | bytes accessed | tf_op | source)
XLA Modules:
  0.0 1208.0 jit_solution(7258464609314661549)
XLA Ops:
  22.2 5.1 pad_maximum_fusion.refs_4_
  28.3 189.8 %shard_map.272 = (bf16[2,2,2,256,2048]{4,3,2,1,0:T(8,128)(2,1)}, bf16[4,2,2,128,768]{4,3,2,1,0:T(8,128)(2,1)}, bf16[8,2,48,2048]{3,2,1,0:T(8,128)(2,1)}, bf16[2,...) custom-call(bf16[256,2048]{1,0:T(8,128)(2,1)} %fusion.5.refs_0_, ...), custom_call_target="tpu_custom_call" | custom-call | tf_op jit(solution)/shard_map/pallas_call | solution.py:513
  222.3 16.3 %shard_map.273 = (f32[2048,640]{1,0:T(8,128)}, bf16[2048,512]{1,0:T(8,128)(2,1)}, bf16[2048,128]{1,0:T(8,128)(2,1)S(1)}, bf16[2048,128]{1,0:T(8,128)(2,1)S(1)}, ...) custom-call(bf16[2048,2048]{1,0:T(8,128)(2,1)} %bitcast.174, bf16[2048,768]{1,0:T(8,128)(2,1)} %bitcast.188, ...), custom_call_target="tpu_custom_call" | custom-call | tf_op jit(solution)/shard_map/pallas_call | solution.py:788
  242.7 31.6 %shard_map.274 = (bf16[2,1024,512]{2,1,0:T(8,128)(2,1)S(1)}, f32[2,4,1,1024]{3,2,1,0:T(1,128)S(1)}) custom-call(s32[2,1024,1]{2,1,0:T(8,128)S(1)} %copy.131.k_place, s32[2,1024,1]{2,1,0:T(8,128)S(1)} %copy.132.k_segment, s32[2,1,1024]{2,1,0:T(1,128)S(1)} %get-tuple-element.175.q_place, s32[2,1,1024]{2,1,0:T(1,128)S(1)} %get-tuple-element.172.q_segment, ...), custom_call_target="tpu_custom_call" | custom-call | tf_op jit(solution)/shard_map/pallas_call | solution.py:874
  274.3 6.8 convolution_convert_fusion
  281.1 48.4 %shard_map.275 = f32[256,2048]{1,0:T(8,128)} custom-call(bf16[2,2,2,256,2048]{4,3,2,1,0:T(8,128)(2,1)} %bitcast.192), custom_call_target="tpu_custom_call" | custom-call | tf_op jit(solution)/shard_map/pallas_call | solution.py:513
  336.3 141.6 %shard_map.276 = (bf16[2,2,2,512,2048]{4,3,2,1,0:T(8,128)(2,1)}, f32[2,2,2,2,16,256]{5,4,3,2,1,0:T(8,128)}) custom-call(bf16[512,2048]{1,0:T(8,128)(2,1)} %pad_maximum_fusion.1.refs_0_, f32[16,256]{1,0:T(8,128)} %fusion.19.refs_1_), custom_call_target="tpu_custom_call" | custom-call | tf_op jit(solution)/shard_map/pallas_call | solution.py:513
  486.0 51.9 %shard_map.277 = (bf16[2048,768]{1,0:T(8,128)(2,1)}, bf16[2048,1536]{1,0:T(8,128)(2,1)}, f32[2048,1]{1,0:T(8,128)S(1)}, bf16[2048,2048]{1,0:T(8,128)(2,1)}, bf16[2048,2048]{1,0:T(8,128)(2,1)}) custom-call(s32[8]{0:T(128)S(1)} %iota_xor_fusion.ids_ref, bf16[8,512,2048]{2,1,0:T(8,128)(2,1)} %bitcast.178, bf16[8,512,2048]{2,1,0:T(8,128)(2,1)} %bitcast.179, ...), custom_call_target="tpu_custom_call" | custom-call | flops 927712935936 | bytes 58720256 | tf_op jit(solution)/shard_map/pallas_call | solution.py:615
  540.0 51.5 %shard_map.278 = (bf16[2048,768]{1,0:T(8,128)(2,1)}, bf16[2048,1536]{1,0:T(8,128)(2,1)}, f32[2048,1]{1,0:T(8,128)S(1)}, bf16[2048,2048]{1,0:T(8,128)(2,1)}, bf16[2048,2048]{1,0:T(8,128)(2,1)}) custom-call(s32[8]{0:T(128)S(1)} %broadcast_add_fusion.2.ids_ref, bf16[8,512,2048]{2,1,0:T(8,128)(2,1)} %collective-permute-done.rows_ref.grad_ref.refs_6_.refs_8_, ...), custom_call_target="tpu_custom_call" | custom-call | flops 927712935936 | bytes 58720256 | tf_op jit(solution)/shard_map/pallas_call | solution.py:615
  596.5 9.6 collective-permute-done.1
  606.1 91.0 %shard_map.279 = (f32[256,2048]{1,0:T(8,128)}, f32[16,1,256]{2,1,0:T(1,128)}, bf16[768,2048]{1,0:T(8,128)(2,1)}, bf16[2048,1536]{1,0:T(8,128)(2,1)}) custom-call(bf16[2,2,2,256,2048]{4,3,2,1,0:T(8,128)(2,1)} %bitcast.201, bf16[2,2,2,256,2048]{4,3,2,1,0:T(8,128)(2,1)} %bitcast.39.refs_1_, f32[16,1,256]{2,1,0:T(1,128)} %bitcast.224, ...), custom_call_target="tpu_custom_call" | custom-call | tf_op jit(solution)/shard_map/pallas_call | solution.py:513
  718.3 5.1 collective-permute-done.2
  723.4 109.4 %shard_map.280 = (bf16[2,2,2,256,2048]{4,3,2,1,0:T(8,128)(2,1)}, f32[512,2048]{1,0:T(8,128)}) custom-call(bf16[256,2048]{1,0:T(8,128)(2,1)} %fusion.25.refs_0_, bf16[2,2,512,2048]{3,2,1,0:T(8,128)(2,1)} %bitcast.195, bf16[2,2,512,2048]{3,2,1,0:T(8,128)(2,1)} %bitcast.57.refs_2_), custom_call_target="tpu_custom_call" | custom-call | tf_op jit(solution)/shard_map/pallas_call | solution.py:513
  832.8 10.0 shard_map.284
  842.8 7.4 convolution_convert_fusion.1
  850.2 40.4 %shard_map.281 = (bf16[2,1024,512]{2,1,0:T(8,128)(2,1)}, f32[2,1024,128]{2,1,0:T(8,128)S(1)}, f32[2,1024,128]{2,1,0:T(8,128)S(1)}) custom-call(s32[2,1024,1]{2,1,0:T(8,128)S(1)} %copy.131.k_place, s32[2,1024,1]{2,1,0:T(8,128)S(1)} %copy.132.k_segment, s32[2,1,1024]{2,1,0:T(1,128)S(1)} %copy-done.15, s32[2,1,1024]{2,1,0:T(1,128)S(1)} %get-tuple-element.172.q_segment, ...), custom_call_target="tpu_custom_call" | custom-call | tf_op jit(solution)/shard_map/pallas_call | solution.py:874
  890.6 25.0 %shard_map.282 = (bf16[2048,768]{1,0:T(8,128)(2,1)}, bf16[2048,2048]{1,0:T(8,128)(2,1)}, f32[1,128]{1,0:T(1,128)S(1)}, f32[1,128]{1,0:T(1,128)S(1)}, f32[1,2048]{1,0:T(1,128)S(1)}) custom-call(bf16[2048,512]{1,0:T(8,128)(2,1)} %bitcast.215, f32[2048,128]{1,0:T(8,128)S(1)} %bitcast.163, f32[2048,128]{1,0:T(8,128)S(1)} %bitcast.164, ...), custom_call_target="tpu_custom_call" | custom-call | tf_op jit(solution)/shard_map/pallas_call | solution.py:788
  915.6 12.5 %shard_map.283 = bf16[2048,768]{1,0:T(8,128)(2,1)} custom-call(bf16[2048,2048]{1,0:T(8,128)(2,1)} %bitcast.176, bf16[2048,768]{1,0:T(8,128)(2,1)} %get-tuple-element.101.refs_1_), custom_call_target="tpu_custom_call" | custom-call | tf_op jit(solution)/shard_map/pallas_call | solution.py:649
  928.0 4.1 copy.143
  935.3 214.1 %shard_map.285 = (bf16[8,2,48,2048]{3,2,1,0:T(8,128)(2,1)}, bf16[8,2,128,1536]{3,2,1,0:T(8,128)(2,1)}, f32[256,2048]{1,0:T(8,128)}, bf16[4,2,128,768]{3,2,1,0:T(...) custom-call(bf16[8,48,2048]{2,1,0:T(8,128)(2,1)} %bitcast.216, ...), custom_call_target="tpu_custom_call" | custom-call | tf_op jit(solution)/shard_map/pallas_call | solution.py:513
  1161.9 4.5 copy.145
  1172.3 10.3 shard_map.287
  1182.7 11.9 shard_map.286
  1194.6 6.7 fusion.2
  (215 shorter events, 87.0 us)
Async XLA Ops:
  7.2 10.9 copy-start
  7.2 478.8 %all-gather.3.cloned.1.call-start = ((), (), s32[]{:S(2)}) async-start(), calls=%async_computation.4 | async-start | bytes 9437184 | tf_op jit(solution)/shard_map/all_gather | solution.py:1005
  8.8 6.9 copy-start.53
  8.9 12.1 %copy-start.51 = (f32[256]{0:T(256)}, f32[256]{0:T(256)S(1)}, u32[]{:S(2)}) copy-start(f32[256]{0:T(256)S(1)} %fusion.23) | copy-start | bytes 3076
  218.2 717.1 %reduce-scatter.3.cloned.1.call-start = ((), (), s32[]{:S(2)}) async-start(), calls=%async_computation.2 | async-start | bytes 4718592 | tf_op jit(solution)/shard_map/reduce_scatter | solution.py:1110
  218.9 23.8 %copy-start.14 = (s32[2,1,1024]{2,1,0:T(1,128)}, s32[2,1,1024]{2,1,0:T(1,128)S(1)}, u32[]{:S(2)}) copy-start(s32[2,1,1024]{2,1,0:T(1,128)S(1)} %get-tuple-element.175.q_place) | copy-start | bytes 24580
  242.7 31.6 %copy-start.60 = (bf16[2,2,128,2048]{3,2,1,0:T(8,128)(2,1)S(1)}, bf16[2,2,128,2048]{3,2,1,0:T(8,128)(2,1)}, u32[]{:S(2)}) copy-start(bf16[2,2,128,2048]{3,2,1,0:T(8,128)(2,1)} %get-tuple-element.72) | copy-start | bytes 6291460
  274.3 6.9 copy-start.3
  281.1 48.4 %copy-start.57 = (s32[1,256,8]{1,2,0:T(8,128)S(1)}, s32[1,256,8]{1,2,0:T(8,128)}, u32[]{:S(2)}) copy-start(s32[1,256,8]{1,2,0:T(8,128)} %param.20) | copy-start | bytes 24580
  281.1 48.5 %copy-start.23 = (bf16[1,256,2048]{2,1,0:T(8,128)(2,1)S(1)}, bf16[1,256,2048]{2,1,0:T(8,128)(2,1)}, u32[]{:S(2)}) copy-start(bf16[1,256,2048]{2,1,0:T(8,128)(2,1)} %param.17) | copy-start | bytes 3145732
  477.9 62.1 %collective-permute-start = (bf16[8,512,2048]{2,1,0:T(8,128)(2,1)}, bf16[8,512,2048]{2,1,0:T(8,128)(2,1)}, u32[]{:S(2)}, u32[]{:S(2)}) collective-permute-start(bf16[8,512,2048]{2,1,0:T(8,128)(2,1)} %bitcast.177), channel_id=1, source_target_pairs={{0,4},{4,0},{1,5},{5,1},{2,6},{6,2},{3,7},{7,3},{8,12},{12,8},{9,1... | collective-permute-start | bytes 50331656 | tf_op jit(solution)/shard_map/ppermute | solution.py:1071
  592.6 13.5 %collective-permute-start.1 = (bf16[2048,2048]{1,0:T(8,128)(2,1)}, bf16[2048,2048]{1,0:T(8,128)(2,1)}, u32[]{:S(2)}, u32[]{:S(2)}) collective-permute-start(bf16[2048,2048]{1,0:T(8,128)(2,1)} %get-tuple-element.80), channel_id=1, source_target_pairs={{0,4},{4,0},{1,5},{5,1},{2,6},{6,2},{3,7},{7,3},{8,12},{12,8},{9,1... | collective-permute-start | bytes 25165832 | tf_op jit(solution)/shard_map/ppermute | solution.py:1082
  703.2 232.1 %reduce-scatter.5.cloned.1.call-start = ((), (), s32[]{:S(2)}) async-start(), calls=%async_computation.3 | async-start | bytes 9437184 | tf_op jit(solution)/shard_map/reduce_scatter | solution.py:1110
  709.8 13.6 %collective-permute-start.2 = (bf16[2048,2048]{1,0:T(8,128)(2,1)}, bf16[2048,2048]{1,0:T(8,128)(2,1)}, u32[]{:S(2)}, u32[]{:S(2)}) collective-permute-start(bf16[2048,2048]{1,0:T(8,128)(2,1)} %get-tuple-element.91), channel_id=1, source_target_pairs={{0,4},{4,0},{1,5},{5,1},{2,6},{6,2},{3,7},{7,3},{8,12},{12,8},{9,1... | collective-permute-start | bytes 25165832 | tf_op jit(solution)/shard_map/ppermute | solution.py:1083
  832.8 10.0 copy-start.30
  842.8 7.4 copy-start.5
  842.8 7.4 copy-start.15
  850.2 40.4 %copy-start.9 = (f32[2048,128]{1,0:T(8,128)S(1)}, f32[2048,128]{1,0:T(8,128)}, u32[]{:S(2)}) copy-start(f32[2048,128]{1,0:T(8,128)} %copy-done.8) | copy-start | bytes 3145732
  850.2 40.4 %copy-start.11 = (f32[2048,128]{1,0:T(8,128)S(1)}, f32[2048,128]{1,0:T(8,128)}, u32[]{:S(2)}) copy-start(f32[2048,128]{1,0:T(8,128)} %copy-done.10) | copy-start | bytes 3145732
  850.2 40.4 %copy-start.13 = (f32[2048]{0:T(1024)S(1)}, f32[2048]{0:T(1024)}, u32[]{:S(2)}) copy-start(f32[2048]{0:T(1024)} %param.29) | copy-start | bytes 24580
  850.2 40.4 %copy-start.17 = (f32[128]{0:T(128)S(1)}, f32[128]{0:T(128)}, u32[]{:S(2)}) copy-start(f32[128]{0:T(128)} %param.31) | copy-start | bytes 1540
  850.2 40.4 %copy-start.19 = (f32[128]{0:T(128)S(1)}, f32[128]{0:T(128)}, u32[]{:S(2)}) copy-start(f32[128]{0:T(128)} %param.32) | copy-start | bytes 1540
  1182.7 11.9 copy-start.52
  1194.6 6.7 copy-start.1
  (43 other events, 94.4 us)
Sparse Core Ops, SparseCore 0:
  218.3 147.1 all-gather.2
  703.3 76.0 reduce-scatter.2
  782.3 144.4 reduce-scatter.4

commit v4 on v3

--- a/solution.py
+++ b/solution.py
@@ -15,6 +15,7 @@
 SWAP = [(0, 1), (1, 0)]
 ROW_TILE = 16
 MIB = 1 << 20
+TILE = 256
 WAIT_LAST = 8
 LONG = 16
 BRIEF = pl.CostEstimate(flops=0, bytes_accessed=0, transcendentals=0)
@@ -428,21 +429,20 @@
 
 
 class WeightGrad(Task):
-    def __init__(self, lefts, rights, left_half, right_half, rows, tile=256):
-        self.amount, self.rows, self.tile = len(lefts), rows, tile
-        self.halves = left_half, right_half
+    def __init__(self, lefts, rights, turns=1):
+        self.amount, self.turns = len(lefts), turns
         self.operands = list(lefts) + list(rights)
-        self.columns, self.width = lefts[0].shape[-1], rights[0].shape[-1]
-        self.blocks = lefts[0].shape[0]
+        self.blocks, self.rows, self.columns = lefts[0].shape
+        self.width = rights[0].shape[-1]
         self.results = [jax.ShapeDtypeStruct((self.columns, self.width), low)]
-        shape = (self.amount, self.blocks, rows, self.width)
+        shape = (self.amount, self.blocks, self.rows, self.width)
         self.scratch = [pltpu.VMEM(shape, low), sems(self.amount)]
 
-    def run(self, operands, results, scratch, lo=0, hi=None):
+    def run(self, operands, results, scratch):
         held, done = scratch
-        at = pl.ds(self.halves[1] * self.rows, self.rows)
+        steps = self.columns // TILE
         copies = [
-            pltpu.make_async_copy(right.at[:, at], held.at[number], done.at[number])
+            pltpu.make_async_copy(right, held.at[number], done.at[number])
             for number, right in enumerate(operands[self.amount :])
         ]
         for copy in copies:
@@ -454,17 +454,18 @@
             total = 0.0
             for number, left_ref in enumerate(refs[:-1]):
                 right = held[number].reshape(-1, self.width)
-                total = total + dot_tn(left_ref[...].reshape(-1, self.tile), right)
+                total = total + dot_tn(left_ref[...].reshape(-1, TILE), right)
             refs[-1][...] = total.astype(low)
 
-        block = pl.BlockSpec(
-            (self.blocks, self.rows, self.tile), lambda step: (0, self.halves[0], step)
-        )
+        def place(step):
+            return (step % self.turns * (steps // self.turns) + step // self.turns, 0)
+
+        block = pl.BlockSpec((self.blocks, self.rows, TILE), lambda step: (0, 0, step))
         pltpu.emit_pipeline(
             body,
-            grid=(self.columns // self.tile,),
+            grid=(steps,),
             in_specs=[block] * self.amount,
-            out_specs=[pl.BlockSpec((self.tile, self.width), lambda step: (step, 0))],
+            out_specs=[pl.BlockSpec((TILE, self.width), place)],
         )(*operands[: self.amount], results[0])
 
 
@@ -540,7 +541,8 @@
     rows_ref,
     grad_ref,
     gate_ref,
-    pieces_in,
+    pieces_gate,
+    pieces_up,
     pieces_down,
     hidden_ref,
     d_in_ref,
@@ -554,14 +556,19 @@
     @pl.when(pl.program_id(0) == 0)
     def _():
         copies = []
-        for pieces, held in ((pieces_in, in_ref), (pieces_down, down_ref)):
-            amount, parts, rows = pieces.shape[:3]
+        half = pieces_gate.shape[3]
+        for pieces, held, lo in (
+            (pieces_gate, in_ref, 0),
+            (pieces_up, in_ref, half),
+            (pieces_down, down_ref, 0),
+        ):
+            amount, parts, rows, columns = pieces.shape
             for spot in range(amount):
                 for part in range(parts):
                     block = (part // near * amount + spot) * near + part % near
                     copy = pltpu.make_async_copy(
                         pieces.at[spot, part],
-                        held.at[pl.ds(block * rows, rows)],
+                        held.at[pl.ds(block * rows, rows), pl.ds(lo, columns)],
                         done.at[len(copies)],
                     )
                     copy.start()
@@ -588,15 +595,12 @@
     made_ref[...] = dot(hidden_low, down_ref[...]).astype(low)
 
 
-def expert_rows(rows, gate, pieces_in, pieces_down, near, ids):
+def expert_rows(rows, grad_rows, gate, pieces, near, ids):
     blocks, tile, model_width = rows.shape
-    tile = tile // 2
-    pieces = (pieces_in, pieces_down)
     amount = blocks * tile
-    hidden_width = pieces_in.shape[3] // 2
-
-    def half(which):
-        return pl.BlockSpec((None, tile, model_width), lambda step, ids: (ids[step], which, 0))
+    hidden_width = pieces[0].shape[3]
+
+    block = pl.BlockSpec((None, tile, model_width), lambda step, ids: (ids[step], 0, 0))
 
     def by_place(columns):
         return pl.BlockSpec((tile, columns), lambda step, ids: (ids[step], 0))
@@ -617,7 +621,7 @@
         grid_spec=pltpu.PrefetchScalarGridSpec(
             num_scalar_prefetch=1,
             grid=(blocks,),
-            in_specs=[half(0), half(1), by_place(1)]
+            in_specs=[block, block, by_place(1)]
             + [anywhere] * len(pieces),
             out_specs=[spec(columns) for spec, columns, _ in outs],
             scratch_shapes=[
@@ -633,36 +637,73 @@
             bytes_accessed=14 * amount * model_width,
             transcendentals=0,
         ),
-    )(ids, rows, rows, gate, *pieces)
+    )(ids, rows, grad_rows, gate, *pieces)
 
 
 def weight_kernel(amount, *refs):
     total = 0.0
     for left, right in zip(refs[:amount], refs[amount:-1]):
         total = total + dot_tn(left[...], right[...])
-    refs[-1][...] = total.astype(low)
-
-
-def weight_grad(lefts, rights, tile=256):
+    refs[-1][...] = total.astype(low).reshape(refs[-1].shape)
+
+
+def weight_grad(lefts, rights, groups=1, parts=1, tile=256):
     amount = len(lefts)
     columns, out_columns = lefts[0].shape[1], rights[0].shape[1]
+    piece = columns // (groups * parts)
+    tile = min(tile, piece * parts)
+    if tile < piece:
+        groups, parts, piece = columns // tile, 1, tile
+    runs = piece * parts // tile
     return pl.pallas_call(
         functools.partial(weight_kernel, amount),
         grid=(columns // tile,),
         in_specs=[pl.BlockSpec((left.shape[0], tile), lambda step: (0, step)) for left in lefts]
         + [whole_block(right.shape) for right in rights],
-        out_specs=pl.BlockSpec((tile, out_columns), lambda step: (step, 0)),
-        out_shape=jax.ShapeDtypeStruct((columns, out_columns), low),
+        out_specs=pl.BlockSpec(
+            (tile // piece, 1, piece, out_columns), lambda step: (step % runs, step // runs, 0, 0)
+        ),
+        out_shape=jax.ShapeDtypeStruct((parts, groups, piece, out_columns), low),
         compiler_params=pltpu.CompilerParams(vmem_limit_bytes=52 * MIB),
         cost_estimate=BRIEF,
     )(*lefts, *rights)
 
 
 def widen_kernel(pieces_ref, *out_refs):
-    columns = out_refs[0].shape[1]
+    columns = out_refs[0].shape[2]
     for number, out_ref in enumerate(out_refs):
         span = slice(number * columns, (number + 1) * columns)
-        out_ref[...] = pieces_ref[:, span].astype(wide)
+        out_ref[...] = pieces_ref[:, :, span].astype(wide)
+
+
+def widen_heads_kernel(parts, piece_ref, query_ref, key_ref, value_ref):
+    groups, width = piece_ref.shape[0], key_ref.shape[1]
+    columns = piece_ref.shape[2] - 2 * width
+    piece = columns // parts
+    for part in range(parts):
+        for group in range(groups):
+            at = (part * groups + group) * piece
+            span = slice(part * piece, (part + 1) * piece)
+            query_ref[:, at : at + piece] = piece_ref[group, :, span].astype(wide)
+    for number, out_ref in enumerate((key_ref, value_ref)):
+        span = slice(columns + number * width, columns + (number + 1) * width)
+        total = piece_ref[0, :, span].astype(wide)
+        for group in range(1, groups):
+            total = total + piece_ref[group, :, span].astype(wide)
+        out_ref[...] = total
+
+
+def by_head(pieces, parts, width):
+    owners, groups, rows, columns = pieces.shape
+    spans = [groups * (columns - 2 * width), width, width]
+    return pl.pallas_call(
+        functools.partial(widen_heads_kernel, parts),
+        grid=(owners,),
+        in_specs=[pl.BlockSpec((None, groups, rows, columns), lambda step: (step, 0, 0, 0))],
+        out_specs=[pl.BlockSpec((rows, span), lambda step: (0, step)) for span in spans],
+        out_shape=[jax.ShapeDtypeStruct((rows, owners * span), wide) for span in spans],
+        cost_estimate=BRIEF,
+    )(pieces)
 
 
 def by_expert(pieces, amount):
@@ -672,10 +713,10 @@
     out = (groups * team, rows, columns // amount)
     return pl.pallas_call(
         widen_kernel,
-        grid=(groups, team),
-        in_specs=[pl.BlockSpec((None, None, rows, columns), lambda group, place: (place, group, 0, 0))],
+        grid=(groups, team // 4),
+        in_specs=[pl.BlockSpec((4, None, rows, columns), lambda group, place: (place, group, 0, 0))],
         out_specs=[
-            pl.BlockSpec((None,) + out[1:], lambda group, place: (group * team + place, 0, 0))
+            pl.BlockSpec((4,) + out[1:], lambda group, place: (group * (team // 4) + place, 0, 0))
         ]
         * amount,
         out_shape=[jax.ShapeDtypeStruct(out, wide)] * amount,
@@ -966,7 +1007,6 @@
         ],
         axis=2,
     )
-    own_in = jnp.concatenate([w_gate, w_up], axis=2)
     wide_router = jnp.pad(w_router, ((0, 0), (0, width - experts)))
     resid = tokens[0].astype(jnp.float32)
     norm_one, back_one = jax.vjp(normed, resid, gain_attn)
@@ -975,14 +1015,17 @@
         return flat_index(g_axes) * team + place
 
     mine_out = take(w_out.reshape(groups, -1, model_width), g_here) if even else w_out
-    all_one, w_qkv, pieces_down, w_mix, got_in, full_router, marks = transfer(
+    grad_parts = [(lo, hi, near_axes + order) for lo, hi, order in plane_parts]
+    all_one, w_qkv, own_grads, pieces_down, w_mix, got_gate, got_up, full_router, marks = transfer(
         1,
         [
             Gather(plane_axes, norm_one.astype(low), core_last(plane_parts)),
             Spread(c_axes, f_axes, mine_qkv, (rows_d, qkv_cols)),
+            Gather(turn, cotangent[0], grad_parts),
             Spread(team_axes, far_axes, w_down, w_down.shape[1:], own_expert),
             Gather(f_axes, mine_out, [(0, mine_out.shape[0], f_axes)]),
-            Direct(team_axes, own_in, own_in.shape[1:], own_expert),
+            Direct(team_axes, w_gate, w_gate.shape[1:], own_expert),
+            Direct(team_axes, w_up, w_up.shape[1:], own_expert),
             Direct(own_axes, wide_router[None], wide_router.shape, lambda place: 0),
             Direct(
                 g_axes,
@@ -991,8 +1034,11 @@
                 lambda place: 0,
             ),
         ],
-        (1, 0, 2, 0, 3, 1),
-    )
+        (1, 0, 2, 3, 0, 2, 4, 1, 0),
+    )
+    blocks = 1 << len(turn)
+    own_grads = own_grads.reshape(blocks, count, model_width)
+    far_grads = lax.ppermute(own_grads, core[0], SWAP)
     w_qkv = w_qkv.reshape(model_width, qkv_cols)
     all_one = all_one.reshape(-1, model_width)
     full_router = full_router.reshape(model_width, width)[:, :experts]
@@ -1004,7 +1050,7 @@
     def from_far(got):
         return lax.all_gather(got, far_axes, axis=0, tiled=False) if far_axes else got[None]
 
-    pieces_in = from_far(got_in)
+    pieces_gate, pieces_up = from_far(got_gate), from_far(got_up)
     pieces_down = pieces_down.reshape((team, -1) + w_down.shape[1:]).transpose(1, 0, 2, 3)
     if rows_f % ROW_TILE:
         pieces_down = pieces_down.reshape((-1, parts_c, parts_near) + w_down.shape[1:])
@@ -1054,35 +1100,34 @@
     powers = jnp.where(chosen, jnp.exp(logits - jnp.max(logits, axis=-1, keepdims=True)), 0.0)
     gates = powers / jnp.sum(powers, axis=-1, keepdims=True)
 
-    grad_parts = [(lo + count, hi + count, order) for lo, hi, order in cluster_parts]
-    own_rows, all_gates = transfer(
+    own_two, all_gates = transfer(
         3,
         [
-            Gather(
-                turn,
-                jnp.concatenate([normed_two, cotangent[0]], axis=0),
-                cluster_parts + grad_parts,
-            ),
+            Gather(turn, normed_two, cluster_parts),
             Gather(cluster_axes, gates.T, [(0, experts, turn + core)]),
         ],
     )
-    blocks = 1 << len(turn)
-    own_rows = own_rows.reshape(blocks, 2 * count, model_width)
-    far_rows = lax.ppermute(own_rows, core[0], SWAP)
+    own_two = own_two.reshape(blocks, count, model_width)
+    far_two = lax.ppermute(own_two, core[0], SWAP)
     gate_stack = take_at(all_gates, flat_index(cluster_axes), len(cluster_axes))
     core_here, core_spot = lax.axis_index(core[0]), cluster_axes.index(core[0])
     ids = jnp.bitwise_xor(jnp.arange(blocks), flat_index(turn)).astype(jnp.int32)
     sides = []
-    for side, side_rows in ((core_here, own_rows), (1 - core_here, far_rows)):
+    pieces = (pieces_gate, pieces_up, pieces_down)
+    for side, side_rows, side_grads in (
+        (core_here, own_two, own_grads),
+        (1 - core_here, far_two, far_grads),
+    ):
         gate = take_at(gate_stack, side, core_spot).reshape(-1, 1)
-        sides.append(expert_rows(side_rows, gate, pieces_in, pieces_down, parts_near, ids))
+        sides.append(expert_rows(side_rows, side_grads, gate, pieces, parts_near, ids))
         ids = ids + zero_of(sides[0][2]).astype(jnp.int32)
     hiddens, d_ins, d_gate_parts, made_parts, back_parts = zip(*sides)
     half_shape = (2,) * len(turn) + (count, model_width)
     far_back = lax.ppermute(back_parts[1], core[0], SWAP)
     far_made = lax.ppermute(made_parts[1], core[0], SWAP)
+    far_parts = 1 << len(far_axes)
+    straight = parts_near * rows_d == TILE
     d_gates = jnp.stack(d_gate_parts).reshape(experts, 1, count)
-    both_rows = [own_rows, far_rows]
     hiddens = [part.reshape(blocks, count, hidden_width) for part in hiddens]
     d_ins = [part.reshape(blocks, count, 2 * hidden_width) for part in d_ins]
     back = [part.reshape(half_shape) for part in (back_parts[0], far_back)]
@@ -1091,8 +1136,8 @@
         [
             ReduceBoth(turn, *back, cluster_parts),
             Direct(core + turn, d_gates, (1, count)),
-            WeightGrad(hiddens, both_rows, 0, 1, count),
-            WeightGrad(both_rows, d_ins, 0, 0, count),
+            WeightGrad(hiddens, [own_grads, far_grads]),
+            WeightGrad([own_two, far_two], d_ins, far_parts if straight else 1),
         ],
         (-1, 0, -2),
     )
@@ -1102,14 +1147,17 @@
 
     reduced = zero_of(d_rows_two).astype(low)
 
-    def to_far(part, rows):
-        stack = part.reshape(parts_c, -1, parts_near, rows, part.shape[1]) + reduced
-        stack = stack.transpose(1, 0, 2, 3, 4).reshape(-1, team, rows, part.shape[1])
+    def to_far(part, rows, done=False):
+        stack = part
+        if not done:
+            stack = part.reshape(parts_c, -1, parts_near, rows, part.shape[1]) + reduced
+            stack = stack.transpose(1, 0, 2, 3, 4)
+        stack = stack.reshape(-1, team, rows, part.shape[1])
         if not far_axes:
             return stack[0]
         return lax.psum_scatter(stack, far_axes, scatter_dimension=0, tiled=False)
 
-    share_down, share_in = to_far(part_down, rows_f), to_far(part_in, rows_d)
+    share_in, share_down = to_far(part_in, rows_d, straight), to_far(part_down, rows_f)
 
     d_logits = (gates * (d_gates - jnp.sum(gates * d_gates, axis=-1, keepdims=True))).astype(low)
     part_router = dot_tn(normed_two, d_logits)
@@ -1165,12 +1213,8 @@
         [width, width, model_width],
     )
     d_one = d_one.reshape(plane_shape)
-    part_out = weight_grad([mixed_rows], [d_branch])
-    part_qkv = weight_grad([all_one], [d_lin])
-
-    def by_f(part):
-        stack = part.reshape(parts_c, parts_f, rows_d, -1).transpose(1, 0, 2, 3)
-        return stack.reshape((2,) * len(f_axes) + (parts_c * rows_d, -1))
+    part_out = weight_grad([mixed_rows], [d_branch]).reshape(q_cols, model_width)
+    part_qkv = weight_grad([all_one], [d_lin], parts_c, parts_f)
 
     turn_back = plane_axes[len(g_axes) : -1] + g_axes
     def over_groups(shape):
@@ -1185,7 +1229,7 @@
         Reduce(plane_axes, d_one, core_first([(lo, hi, turn_back) for lo, hi, _ in plane_parts])),
         Reduce(
             f_axes,
-            by_f(part_qkv),
+            part_qkv.reshape((2,) * len(f_axes) + (parts_c * rows_d, qkv_cols)),
             [(0, parts_c * rows_d, f_axes[::-1])],
             jax.ShapeDtypeStruct((parts_c, rows_d, qkv_cols), low),
             to_column_owners,
@@ -1234,17 +1278,9 @@
             stack.reshape(groups * q_cols, model_width), f_axes, scatter_dimension=0, tiled=True
         )
         grad_out = lax.psum(share_out.astype(wide), g_axes)
-    all_qkv = all_qkv.reshape(parts_c, groups, rows_d, qkv_cols).transpose(1, 0, 2, 3).astype(wide)
-    grad_query = all_qkv[:, :, :, :q_cols]
-    if even:
-        grad_query = grad_query.reshape(groups, parts_c, rows_d, parts_f, q_cols // parts_f)
-        grad_query = grad_query.transpose(2, 1, 3, 0, 4).reshape(rows_d, -1)
-    else:
-        grad_query = grad_query.transpose(2, 1, 0, 3).reshape(rows_d, -1)
-    grad_kv = jnp.sum(all_qkv[:, :, :, q_cols:], axis=0).transpose(1, 0, 2)
-    grad_key = grad_kv[:, :, :width].reshape(rows_d, -1)
-    grad_value = grad_kv[:, :, width:].reshape(rows_d, -1)
-
+    grad_query, grad_key, grad_value = by_head(
+        all_qkv.reshape(parts_c, groups, rows_d, qkv_cols), parts_f if even else 1, width
+    )
     return (
         output,
         grad_tokens,

time: 1210 us -> 1150 us (0.950)
  Pallas kernels: 1060 us -> 1030 us
  local copies, waits for them, and re-layouts: 62.5 us -> 35.7 us
    pallas_call x6, Pallas kernels: 794 us -> 774 us  [transfer(): pl.pallas_call(functools.partial(flow_kernel, flows, plan), out_shape=sha...]
  transfers between devices with their start and end apart: 6 -> 8, of which waited for: 2 -> 3; matrix products, arithmetic and copies ran while one was open for 5% -> 4% of each run, Pallas kernels for 40% -> 38%
where the time goes in v4:
time: 1150 us
  Pallas kernels  1030 us (90%)
  local copies, waits for them, and re-layouts  35.7 us (3%)
  other arithmetic  28.8 us (3%)
  matrix products  20 us (2%)
  waiting for transfers between devices  17 us (1%)
  between operations  16.2 us (1%)
    pallas_call x6, Pallas kernels, transfer(): pl.pallas_call(functools.partial(flow_kernel, flows, plan), out_shape=sha...  774 us
    pallas_call x2, Pallas kernels, expert_rows(): pl.pallas_call(functools.partial(expert_kernel, near), grid_spec=pltpu.Pr...  104 us
    pallas_call x2, Pallas kernels, attention_call(): pl.pallas_call(functools.partial(kernel, scale), grid=(seqs, length // ti...  71.6 us
    pallas_call x2, Pallas kernels, row_call(): pl.pallas_call(kernel, grid=(rows // tile,), in_specs=[whole_block(array....  41 us
  transfers between devices with their start and end apart: 8, of which 3 were waited for; matrix products, arithmetic and copies ran while one was open for 4% of the time, Pallas kernels for 38%

profile of v4, /device:TPU:0, one launch (start us, length us, event | category | flops | bytes accessed | tf_op | source)
XLA Modules:
  0.0 1147.6 jit_solution(3966962869120215783)
XLA Ops:
  19.8 214.9 %shard_map.272 = (bf16[2,2,2,256,2048]{4,3,2,1,0:T(8,128)(2,1)}, bf16[4,2,2,128,768]{4,3,2,1,0:T(8,128)(2,1)}, bf16[2,2,2,256,2048]{4,3,2,1,0:T(8,128)(2,1)}, bf...) custom-call(bf16[256,2048]{1,0:T(8,128)(2,1)} %fusion.5.refs_0_, ...), custom_call_target="tpu_custom_call" | custom-call | tf_op jit(solution)/shard_map/pallas_call | solution.py:514
  239.1 16.1 %shard_map.273 = (f32[2048,640]{1,0:T(8,128)}, bf16[2048,512]{1,0:T(8,128)(2,1)}, bf16[2048,128]{1,0:T(8,128)(2,1)S(1)}, bf16[2048,128]{1,0:T(8,128)(2,1)S(1)}, ...) custom-call(bf16[2048,2048]{1,0:T(8,128)(2,1)} %bitcast.160, bf16[2048,768]{1,0:T(8,128)(2,1)} %bitcast.166, ...), custom_call_target="tpu_custom_call" | custom-call | tf_op jit(solution)/shard_map/pallas_call | solution.py:829
  259.2 31.6 %shard_map.274 = (bf16[2,1024,512]{2,1,0:T(8,128)(2,1)S(1)}, f32[2,4,1,1024]{3,2,1,0:T(1,128)S(1)}) custom-call(s32[2,1024,1]{2,1,0:T(8,128)S(1)} %copy.94.k_place, s32[2,1024,1]{2,1,0:T(8,128)S(1)} %copy.95.k_segment, s32[2,1,1024]{2,1,0:T(1,128)S(1)} %get-tuple-element.169.q_place, s32[2,1,1024]{2,1,0:T(1,128)S(1)} %get-tuple-element.166.q_segment, ...), custom_call_target="tpu_custom_call" | custom-call | tf_op jit(solution)/shard_map/pallas_call | solution.py:915
  290.8 6.8 convolution_convert_fusion
  297.6 49.0 %shard_map.275 = f32[256,2048]{1,0:T(8,128)} custom-call(bf16[2,2,2,256,2048]{4,3,2,1,0:T(8,128)(2,1)} %bitcast.177), custom_call_target="tpu_custom_call" | custom-call | tf_op jit(solution)/shard_map/pallas_call | solution.py:514
  353.1 95.7 %shard_map.276 = (bf16[2,2,2,256,2048]{4,3,2,1,0:T(8,128)(2,1)}, f32[2,2,2,2,16,256]{5,4,3,2,1,0:T(8,128)}) custom-call(bf16[256,2048]{1,0:T(8,128)(2,1)} %copy-done.26, f32[16,256]{1,0:T(8,128)} %fusion.19.refs_1_), custom_call_target="tpu_custom_call" | custom-call | tf_op jit(solution)/shard_map/pallas_call | solution.py:514
  449.3 4.0 copy.110
  456.9 51.7 %shard_map.277 = (bf16[2048,768]{1,0:T(8,128)(2,1)}, bf16[2048,1536]{1,0:T(8,128)(2,1)}, f32[2048,1]{1,0:T(8,128)S(1)}, bf16[2048,2048]{1,0:T(8,128)(2,1)}, bf16[2048,2048]{1,0:T(8,128)(2,1)}) custom-call(s32[8]{0:T(128)S(1)} %iota_xor_fusion.ids_ref, bf16[8,256,2048]{2,1,0:T(8,128)(2,1)} %bitcast.173, bf16[8,256,2048]{2,1,0:T(8,128)(2,1)} %bitcast.170, ...), custom_call_target="tpu_custom_call" | custom-call | flops 927712935936 | bytes 58720256 | tf_op jit(solution)/shard_map/pallas_call | solution.py:619
  510.7 52.1 %shard_map.278 = (bf16[2048,768]{1,0:T(8,128)(2,1)}, bf16[2048,1536]{1,0:T(8,128)(2,1)}, f32[2048,1]{1,0:T(8,128)S(1)}, bf16[2048,2048]{1,0:T(8,128)(2,1)}, bf16[2048,2048]{1,0:T(8,128)(2,1)}) custom-call(s32[8]{0:T(128)S(1)} %broadcast_add_fusion.1.ids_ref, bf16[8,256,2048]{2,1,0:T(8,128)(2,1)} %collective-permute-done.rows_ref.refs_8_, ...), custom_call_target="tpu_custom_call" | custom-call | flops 927712935936 | bytes 58720256 | tf_op jit(solution)/shard_map/pallas_call | solution.py:619
  567.7 9.6 collective-permute-done.2
  577.3 90.5 %shard_map.279 = (f32[256,2048]{1,0:T(8,128)}, f32[16,1,256]{2,1,0:T(1,128)}, bf16[768,2048]{1,0:T(8,128)(2,1)}, bf16[2048,1536]{1,0:T(8,128)(2,1)}) custom-call(bf16[2,2,2,256,2048]{4,3,2,1,0:T(8,128)(2,1)} %bitcast.175, bf16[2,2,2,256,2048]{4,3,2,1,0:T(8,128)(2,1)} %bitcast.41.refs_1_, f32[16,1,256]{2,1,0:T(1,128)} %bitcast.204, ...), custom_call_target="tpu_custom_call" | custom-call | tf_op jit(solution)/shard_map/pallas_call | solution.py:514
  677.6 3.9 multiply_reduce_fusion
  683.3 4.8 collective-permute-done.3
  688.1 109.2 %shard_map.280 = (bf16[2,2,2,256,2048]{4,3,2,1,0:T(8,128)(2,1)}, f32[512,2048]{1,0:T(8,128)}) custom-call(bf16[256,2048]{1,0:T(8,128)(2,1)} %fusion.25.refs_0_, bf16[2,2,512,2048]{3,2,1,0:T(8,128)(2,1)} %bitcast.180, bf16[2,2,512,2048]{3,2,1,0:T(8,128)(2,1)} %bitcast.57.refs_2_), custom_call_target="tpu_custom_call" | custom-call | tf_op jit(solution)/shard_map/pallas_call | solution.py:514
  797.3 9.6 shard_map.284
  807.0 7.4 convolution_convert_fusion.1
  814.4 40.0 %shard_map.281 = (bf16[2,1024,512]{2,1,0:T(8,128)(2,1)}, f32[2,1024,128]{2,1,0:T(8,128)S(1)}, f32[2,1024,128]{2,1,0:T(8,128)S(1)}) custom-call(s32[2,1024,1]{2,1,0:T(8,128)S(1)} %copy.94.k_place, s32[2,1024,1]{2,1,0:T(8,128)S(1)} %copy.95.k_segment, s32[2,1,1024]{2,1,0:T(1,128)S(1)} %copy-done.15, s32[2,1,1024]{2,1,0:T(1,128)S(1)} %get-tuple-element.166.q_segment, ...), custom_call_target="tpu_custom_call" | custom-call | tf_op jit(solution)/shard_map/pallas_call | solution.py:915
  854.4 25.0 %shard_map.282 = (bf16[2048,768]{1,0:T(8,128)(2,1)}, bf16[2048,2048]{1,0:T(8,128)(2,1)}, f32[1,128]{1,0:T(1,128)S(1)}, f32[1,128]{1,0:T(1,128)S(1)}, f32[1,2048]{1,0:T(1,128)S(1)}) custom-call(bf16[2048,512]{1,0:T(8,128)(2,1)} %bitcast.198, f32[2048,128]{1,0:T(8,128)S(1)} %bitcast.149, f32[2048,128]{1,0:T(8,128)S(1)} %bitcast.150, ...), custom_call_target="tpu_custom_call" | custom-call | tf_op jit(solution)/shard_map/pallas_call | solution.py:829
  879.3 12.7 %shard_map.283 = bf16[4,4,128,768]{3,2,1,0:T(8,128)(2,1)} custom-call(bf16[2048,2048]{1,0:T(8,128)(2,1)} %bitcast.162, bf16[2048,768]{1,0:T(8,128)(2,1)} %get-tuple-element.108.refs_1_), custom_call_target="tpu_custom_call" | custom-call | tf_op jit(solution)/shard_map/pallas_call | solution.py:658
  896.6 214.4 %shard_map.285 = (bf16[8,2,48,2048]{3,2,1,0:T(8,128)(2,1)}, bf16[8,2,128,1536]{3,2,1,0:T(8,128)(2,1)}, f32[256,2048]{1,0:T(8,128)}, bf16[4,2,128,768]{3,2,1,0:T(...) custom-call(bf16[8,48,2048]{2,1,0:T(8,128)(2,1)} %bitcast.199, ...), custom_call_target="tpu_custom_call" | custom-call | tf_op jit(solution)/shard_map/pallas_call | solution.py:514
  1117.8 3.8 shard_map.286
  1121.5 5.0 shard_map.288
  1126.6 7.9 shard_map.287
  1134.5 6.4 fusion.2
  (201 shorter events, 59.4 us)
Async XLA Ops:
  7.2 7.9 copy-start
  7.2 449.7 %all-gather.5.cloned.1.call-start = ((), (), s32[]{:S(2)}) async-start(), calls=%async_computation.4 | async-start | bytes 4718592 | tf_op jit(solution)/shard_map/all_gather | solution.py:1051
  8.9 8.7 copy-start.49
  234.8 222.1 %all-gather.7.cloned.1.call-start = ((), (), s32[]{:S(2)}) async-start(), calls=%async_computation.5 | async-start | bytes 4718592 | tf_op jit(solution)/shard_map/all_gather | solution.py:1051
  234.8 275.9 %collective-permute-start.1 = (bf16[8,256,2048]{2,1,0:T(8,128)(2,1)}, bf16[8,256,2048]{2,1,0:T(8,128)(2,1)}, u32[]{:S(2)}, u32[]{:S(2)}) collective-permute-start(bf16[8,256,2048]{2,1,0:T(8,128)(2,1)} %bitcast.169), channel_id=1, source_target_pairs={{0,4},{4,0},{1,5},{5,1},{2,6},{6,2},{3,7},{7,3},{8,12},{12,8},{9,1... | collective-permute-start | bytes 25165832 | tf_op jit(solution)/shard_map/ppermute | solution.py:1041
  235.5 659.7 %reduce-scatter.3.cloned.1.call-start = ((), (), s32[]{:S(2)}) async-start(), calls=%async_computation.2 | async-start | bytes 4718592 | tf_op jit(solution)/shard_map/reduce_scatter | solution.py:1158
  235.6 23.6 %copy-start.14 = (s32[2,1,1024]{2,1,0:T(1,128)}, s32[2,1,1024]{2,1,0:T(1,128)S(1)}, u32[]{:S(2)}) copy-start(s32[2,1,1024]{2,1,0:T(1,128)S(1)} %get-tuple-element.169.q_place) | copy-start | bytes 24580
  259.2 31.6 %copy-start.58 = (bf16[2,2,128,2048]{3,2,1,0:T(8,128)(2,1)S(1)}, bf16[2,2,128,2048]{3,2,1,0:T(8,128)(2,1)}, u32[]{:S(2)}) copy-start(bf16[2,2,128,2048]{3,2,1,0:T(8,128)(2,1)} %get-tuple-element.77) | copy-start | bytes 6291460
  297.6 49.0 %copy-start.55 = (s32[1,256,8]{1,2,0:T(8,128)S(1)}, s32[1,256,8]{1,2,0:T(8,128)}, u32[]{:S(2)}) copy-start(s32[1,256,8]{1,2,0:T(8,128)} %param.20) | copy-start | bytes 24580
  352.5 100.8 %copy-start.46 = (f32[256]{0:T(256)}, f32[256]{0:T(256)S(1)}, u32[]{:S(2)}) copy-start(f32[256]{0:T(256)S(1)} %fusion.21) | copy-start | bytes 3076
  448.8 61.9 %collective-permute-start = (bf16[8,256,2048]{2,1,0:T(8,128)(2,1)}, bf16[8,256,2048]{2,1,0:T(8,128)(2,1)}, u32[]{:S(2)}, u32[]{:S(2)}) collective-permute-start(bf16[8,256,2048]{2,1,0:T(8,128)(2,1)} %bitcast.172), channel_id=1, source_target_pairs={{0,4},{4,0},{1,5},{5,1},{2,6},{6,2},{3,7},{7,3},{8,12},{12,8},{9,1... | collective-permute-start | bytes 25165832 | tf_op jit(solution)/shard_map/ppermute | solution.py:1111
  563.8 13.5 %collective-permute-start.2 = (bf16[2048,2048]{1,0:T(8,128)(2,1)}, bf16[2048,2048]{1,0:T(8,128)(2,1)}, u32[]{:S(2)}, u32[]{:S(2)}) collective-permute-start(bf16[2048,2048]{1,0:T(8,128)(2,1)} %get-tuple-element.87), channel_id=1, source_target_pairs={{0,4},{4,0},{1,5},{5,1},{2,6},{6,2},{3,7},{7,3},{8,12},{12,8},{9,1... | collective-permute-start | bytes 25165832 | tf_op jit(solution)/shard_map/ppermute | solution.py:1126
  673.9 222.7 %reduce-scatter.5.cloned.1.call-start = ((), (), s32[]{:S(2)}) async-start(), calls=%async_computation.3 | async-start | bytes 9437184 | tf_op jit(solution)/shard_map/reduce_scatter | solution.py:1158
  674.5 13.6 %collective-permute-start.3 = (bf16[2048,2048]{1,0:T(8,128)(2,1)}, bf16[2048,2048]{1,0:T(8,128)(2,1)}, u32[]{:S(2)}, u32[]{:S(2)}) collective-permute-start(bf16[2048,2048]{1,0:T(8,128)(2,1)} %get-tuple-element.98), channel_id=1, source_target_pairs={{0,4},{4,0},{1,5},{5,1},{2,6},{6,2},{3,7},{7,3},{8,12},{12,8},{9,1... | collective-permute-start | bytes 25165832 | tf_op jit(solution)/shard_map/ppermute | solution.py:1127
  797.3 9.6 copy-start.28
  814.3 40.0 %copy-start.9 = (f32[2048,128]{1,0:T(8,128)S(1)}, f32[2048,128]{1,0:T(8,128)}, u32[]{:S(2)}) copy-start(f32[2048,128]{1,0:T(8,128)} %copy-done.8) | copy-start | bytes 3145732
  814.3 40.0 %copy-start.11 = (f32[2048,128]{1,0:T(8,128)S(1)}, f32[2048,128]{1,0:T(8,128)}, u32[]{:S(2)}) copy-start(f32[2048,128]{1,0:T(8,128)} %copy-done.10) | copy-start | bytes 3145732
  814.3 40.0 %copy-start.13 = (f32[2048]{0:T(1024)S(1)}, f32[2048]{0:T(1024)}, u32[]{:S(2)}) copy-start(f32[2048]{0:T(1024)} %param.29) | copy-start | bytes 24580
  814.4 40.0 %copy-start.17 = (f32[128]{0:T(128)S(1)}, f32[128]{0:T(128)}, u32[]{:S(2)}) copy-start(f32[128]{0:T(128)} %param.31) | copy-start | bytes 1540
  814.4 40.0 %copy-start.19 = (f32[128]{0:T(128)S(1)}, f32[128]{0:T(128)}, u32[]{:S(2)}) copy-start(f32[128]{0:T(128)} %param.32) | copy-start | bytes 1540
  879.3 12.7 %copy-start.29 = (f32[512,2048]{1,0:T(8,128)S(1)}, f32[512,2048]{1,0:T(8,128)}, u32[]{:S(2)}) copy-start(f32[512,2048]{1,0:T(8,128)} %get-tuple-element.112) | copy-start | bytes 12582916
  896.6 216.8 %copy-start.24 = (bf16[1,256,2048]{2,1,0:T(8,128)(2,1)S(1)}, bf16[1,256,2048]{2,1,0:T(8,128)(2,1)}, u32[]{:S(2)}) copy-start(bf16[1,256,2048]{2,1,0:T(8,128)(2,1)} %param.17) | copy-start | bytes 3145732
  1126.6 7.9 copy-start.22
  1126.6 7.9 copy-start.50
  (43 other events, 125.3 us)
Sparse Core Ops, SparseCore 0:
  234.9 77.8 all-gather.4
  314.3 78.6 all-gather.6
  674.0 75.8 reduce-scatter.2
  752.2 144.4 reduce-scatter.4

commit v5 on v4

--- a/solution.py
+++ b/solution.py
@@ -330,8 +330,10 @@
 
 
 class ReduceBoth(Reduce):
-    def __init__(self, axes, operand, other, parts):
+    def __init__(self, axes, operand, other, parts, first=()):
         super().__init__(axes, operand, parts, by_distance=True)
+        self.first = first
+        self.flips = self.flips + [(axis,) for axis in first]
         self.operands = [operand, other]
         shape = operand.shape
         self.scratch = [pltpu.VMEM(shape, low), pltpu.VMEM(shape, low)]
@@ -341,12 +343,12 @@
                 self.scratch.append(pltpu.VMEM((2,) * left + (hi - lo, shape[-1]), low))
         self.scratch.append(pltpu.VMEM(shape[-2:], wide))
         amount = len(parts) * len(axes)
-        self.scratch += [sems(amount), sems(amount), sems(2 * len(parts) + 1)]
+        self.scratch += [sems(amount), sems(amount), sems(2 * len(parts) + 1), sems(len(parts))]
 
     def run(self, operands, results, scratch):
         stages = len(self.axes)
-        held, added, *slots = scratch[:-4]
-        total, send, recv, local = scratch[-4:]
+        held, added, *slots = scratch[:-5]
+        total, send, recv, local, far = scratch[-5:]
         copies, loads = {}, []
         every = (slice(None),) * stages
 
@@ -389,11 +391,22 @@
         for number, (lo, hi, order) in enumerate(self.parts):
             span = every + (pl.ds(lo, hi - lo),)
             for which, (operand, buffer) in enumerate(zip(operands, (held, added))):
-                load = pltpu.make_async_copy(
-                    operand.at[span], buffer.at[span], local.at[2 * number + which]
-                )
+                if which and self.first:
+                    load = remote(
+                        operand.at[span],
+                        added.at[span],
+                        far.at[number],
+                        local.at[2 * number + which],
+                        self.first,
+                    )
+                else:
+                    load = pltpu.make_async_copy(
+                        operand.at[span], buffer.at[span], local.at[2 * number + which]
+                    )
                 load.start()
                 loads.append(load)
+        if self.first:
+            yield
         for number, (lo, hi, order) in enumerate(self.parts):
             loads[2 * number].wait()
             loads[2 * number + 1].wait()
@@ -424,49 +437,215 @@
             copy.wait_send()
 
 
+class Later:
+    def __init__(self, flow):
+        self.flow, self.flips = flow, flow.flips
+        self.operands, self.results, self.scratch = flow.operands, flow.results, flow.scratch
+
+    def run(self, *parts):
+        yield
+        yield from self.flow.run(*parts)
+
+
+class Fed(Later):
+    def __init__(self, flow, source):
+        super().__init__(flow)
+        self.source, self.operands = source, []
+
+    def run(self, operands, results, scratch):
+        yield
+        yield from self.flow.run([self.source()], results, scratch)
+
+
+class PairSum:
+    def __init__(self, axis, task, groups, rows):
+        self.axis, self.task, self.groups, self.rows = axis, task, groups, rows
+        shape = (groups, rows, task.width)
+        self.operands, self.flips = [], [(axis,)]
+        self.results = [jax.ShapeDtypeStruct(shape, low)]
+        self.scratch = [pltpu.VMEM(shape, low), pltpu.VMEM(shape, low)]
+        self.scratch += [sems(groups), sems(groups), sems(groups + 1)]
+
+    def run(self, operands, results, scratch):
+        held, added, send, recv, local = scratch
+        source, place = self.task.refs[1][0], lax.axis_index(self.axis)
+        yield
+
+        def part(group, whose):
+            at = pl.multiple_of((group * 2 + whose) * self.rows, self.rows)
+            return source.at[pl.ds(at, self.rows)]
+
+        copies = []
+        for group in range(self.groups):
+            copy = remote(
+                part(group, 1 - place), added.at[group], send.at[group], recv.at[group], (self.axis,)
+            )
+            load = pltpu.make_async_copy(part(group, place), held.at[group], local.at[group])
+            copy.start()
+            load.start()
+            copies += [copy, load]
+        yield
+        for copy in copies:
+            copy.wait()
+        for group in range(self.groups):
+
+            def add(step, carry, group=group):
+                at = pl.ds(pl.multiple_of(step * ROW_TILE, ROW_TILE), ROW_TILE)
+                value = held[group, at].astype(wide) + added[group, at].astype(wide)
+                held[group, at] = value.astype(low)
+                return carry
+
+            lax.fori_loop(0, self.rows // ROW_TILE, add, 0)
+        store = pltpu.make_async_copy(held, results[0], local.at[self.groups])
+        store.start()
+        store.wait()
+
+
 class Task:
     flips = ()
 
 
 class WeightGrad(Task):
-    def __init__(self, lefts, rights, turns=1):
-        self.amount, self.turns = len(lefts), turns
-        self.operands = list(lefts) + list(rights)
+    def __init__(self, lefts, rights, turns=1, pieces=1, source=None, out=None, room=None):
+        self.amount, self.turns, self.pieces, self.calls = len(lefts), turns, pieces, 0
+        self.source, self.room = source, room
+        self.operands = list(lefts) + (list(rights) if source is None else [])
         self.blocks, self.rows, self.columns = lefts[0].shape
         self.width = rights[0].shape[-1]
-        self.results = [jax.ShapeDtypeStruct((self.columns, self.width), low)]
+        self.out = out or ((self.columns, self.width), (TILE, self.width), self.place)
+        self.results = [jax.ShapeDtypeStruct(self.out[0], low)]
         shape = (self.amount, self.blocks, self.rows, self.width)
-        self.scratch = [pltpu.VMEM(shape, low), sems(self.amount)]
+        self.scratch = [sems(self.amount)] + ([] if room else [pltpu.VMEM(shape, low)])
 
     def run(self, operands, results, scratch):
-        held, done = scratch
+        done = scratch[0]
+        held = self.room.refs[2][1] if self.room else scratch[1]
+        span = slice(0, self.width)
+        if self.calls == 0:
+            rights = operands[self.amount :] if self.source is None else [self.source()]
+            copies = [
+                pltpu.make_async_copy(
+                    right, held.at[number, :, :, pl.ds(0, self.width)], done.at[number]
+                )
+                for number, right in enumerate(rights)
+            ]
+            for copy in copies:
+                copy.start()
+            for copy in copies:
+                copy.wait()
+        share = self.columns // TILE // self.pieces
+        first = self.calls * share
+        self.calls = (self.calls + 1) % self.pieces
+
+        def body(*refs):
+            total = 0.0
+            for number, left_ref in enumerate(refs[:-1]):
+                right = held[number, :, :, span].reshape(-1, self.width)
+                total = total + dot_tn(left_ref[...].reshape(-1, TILE), right)
+            refs[-1][...] = total.astype(low).reshape(refs[-1].shape)
+
+        block = pl.BlockSpec((self.blocks, self.rows, TILE), lambda step: (0, 0, step + first))
+        pltpu.emit_pipeline(
+            body,
+            grid=(share,),
+            in_specs=[block] * self.amount,
+            out_specs=[pl.BlockSpec(self.out[1], lambda step: self.out[2](step + first))],
+        )(*operands[: self.amount], results[0])
+
+    def place(self, step):
         steps = self.columns // TILE
+        return (step % self.turns * (steps // self.turns) + step // self.turns, 0)
+
+
+class HeadsBack(Task):
+    def __init__(self, heads, scale, tiled, w_qkv, gains, ffn_lines, axes):
+        self.heads, self.scale, self.axes = heads, scale, axes
+        self.operands = list(tiled) + [w_qkv, ffn_lines] + list(gains)
+        self.tiled = len(tiled)
+        self.rows, self.width = tiled[1].shape
+        self.model_width, self.columns = w_qkv.shape
+        self.blocks = 1 << len(axes)
+        self.tile = self.rows // self.blocks
+        self.results = [
+            jax.ShapeDtypeStruct((self.blocks, self.tile, self.columns), low),
+            jax.ShapeDtypeStruct((2,) * len(axes) + (self.tile, self.model_width), low),
+        ]
+        own, ffn = self.model_width // self.width, ffn_lines.shape[0]
+        self.lines = -(-(own + ffn + 2) // 8) * 8
+        row = pltpu.VMEM((1, self.width), wide)
+        long_row = pltpu.VMEM((1, self.model_width), wide)
+        self.scratch = [pltpu.VMEM((self.lines, self.width), wide), pltpu.VMEM(w_qkv.shape, low)]
+        self.scratch += [row, row, long_row, row, row, long_row, sems(5)]
+
+    def run(self, operands, results, scratch):
+        lines, w_ref, gain_q, gain_k, gain, d_gain_q, d_gain_k, d_gain, done = scratch
+        w_hbm, ffn, *gains = operands[self.tiled :]
+        own, count = self.model_width // self.width, ffn.shape[0]
+        lines[...] = jnp.zeros_like(lines)
+        targets = [w_ref, lines.at[pl.ds(own, count)], gain_q, gain_k, gain]
         copies = [
-            pltpu.make_async_copy(right, held.at[number], done.at[number])
-            for number, right in enumerate(operands[self.amount :])
+            pltpu.make_async_copy(source, target, done.at[number])
+            for number, (source, target) in enumerate(zip([w_hbm, ffn] + gains, targets))
         ]
         for copy in copies:
             copy.start()
         for copy in copies:
             copy.wait()
-
-        def body(*refs):
-            total = 0.0
-            for number, left_ref in enumerate(refs[:-1]):
-                right = held[number].reshape(-1, self.width)
-                total = total + dot_tn(left_ref[...].reshape(-1, TILE), right)
-            refs[-1][...] = total.astype(low)
-
-        def place(step):
-            return (step % self.turns * (steps // self.turns) + step // self.turns, 0)
-
-        block = pl.BlockSpec((self.blocks, self.rows, TILE), lambda step: (0, 0, step))
+        for total in (d_gain_q, d_gain_k, d_gain):
+            total[...] = jnp.zeros_like(total)
+
+        def body(
+            d_query_ref,
+            d_keyed_ref,
+            d_value_ref,
+            lin_ref,
+            cosine_ref,
+            sine_ref,
+            rows_ref,
+            d_lin_ref,
+            d_one_ref,
+        ):
+            cosine, sine = cosine_ref[...], sine_ref[...]
+            for head in range(self.heads + 1):
+                span = slice(head * self.width, (head + 1) * self.width)
+                values = lin_ref[:, span]
+                if head < self.heads:
+                    grads, own_gain, d_head = d_query_ref[:, span].astype(wide), gain_q, d_gain_q
+                else:
+                    grads, own_gain, d_head = d_keyed_ref[...] * self.scale, gain_k, d_gain_k
+                grads = turned_back(grads, cosine, sine)
+                factor = head_scale(values)
+                plain = values * factor
+                d_head[...] += jnp.sum(grads * plain, axis=0, keepdims=True)
+                grads = grads * own_gain[...]
+                mean = jnp.mean(grads * plain, axis=1, keepdims=True)
+                d_lin_ref[:, span] = (factor * (grads - plain * mean)).astype(low)
+            d_lin_ref[:, (self.heads + 1) * self.width :] = d_value_ref[...].astype(low)
+            d_one = dot_nt(d_lin_ref[...], w_ref[...])
+            d_one_ref[...] = d_one.astype(low)
+            share = jnp.sum(d_one * rows_ref[...].astype(wide), axis=0, keepdims=True)
+            d_gain[...] += share / gain[...]
+
+        def by_bits(step):
+            bits = [step // (self.blocks >> (bit + 1)) % 2 for bit in range(len(self.axes))]
+            return tuple(bits) + (0, 0)
+
         pltpu.emit_pipeline(
             body,
-            grid=(steps,),
-            in_specs=[block] * self.amount,
-            out_specs=[pl.BlockSpec((TILE, self.width), place)],
-        )(*operands[: self.amount], results[0])
+            grid=(self.blocks,),
+            in_specs=[
+                pl.BlockSpec((self.tile, array.shape[1]), lambda step: (step, 0))
+                for array in operands[: self.tiled]
+            ],
+            out_specs=[
+                pl.BlockSpec((None, self.tile, self.columns), lambda step: (step, 0, 0)),
+                pl.BlockSpec((None,) * len(self.axes) + (self.tile, self.model_width), by_bits),
+            ],
+        )(*operands[: self.tiled], *results)
+        for line in range(own):
+            lines[line : line + 1] = d_gain[:, line * self.width : (line + 1) * self.width]
+        lines[own + count : own + count + 1] = d_gain_q[...]
+        lines[own + count + 1 : own + count + 2] = d_gain_k[...]
 
 
 def flow_kernel(flows, plan, *refs):
@@ -489,6 +668,8 @@
             barrier, inc=1, device_id=toward(flips), device_id_type=pl.DeviceIdType.MESH
         )
     pl.semaphore_wait(barrier, len(partners))
+    for flow, *parts in zip(flows, operands, results, scratch):
+        flow.refs = parts
     tasks = [part for part in zip(flows, operands, results, scratch) if isinstance(part[0], Task)]
     runs = [
         flow.run(*parts)
@@ -769,55 +950,6 @@
         else:
             keyed_ref[...] = made
     value_ref[...] = lin[:, (heads + 1) * width :].astype(low)
-
-
-def unprep_kernel(
-    heads,
-    scale,
-    d_query_ref,
-    d_keyed_ref,
-    d_value_ref,
-    lin_ref,
-    w_ref,
-    cosine_ref,
-    sine_ref,
-    gain_q,
-    gain_k,
-    rows_ref,
-    gain_ref,
-    d_lin_ref,
-    d_one_ref,
-    d_gain_q,
-    d_gain_k,
-    d_gain,
-):
-    width = gain_q.shape[1]
-    cosine, sine = cosine_ref[...], sine_ref[...]
-
-    @pl.when(pl.program_id(0) == 0)
-    def _():
-        d_gain_q[...] = jnp.zeros_like(d_gain_q)
-        d_gain_k[...] = jnp.zeros_like(d_gain_k)
-        d_gain[...] = jnp.zeros_like(d_gain)
-
-    for head in range(heads + 1):
-        span = slice(head * width, (head + 1) * width)
-        values = lin_ref[:, span]
-        if head < heads:
-            grads, gain, d_head = d_query_ref[:, span].astype(wide), gain_q[...], d_gain_q
-        else:
-            grads, gain, d_head = d_keyed_ref[...] * scale, gain_k[...], d_gain_k
-        grads = turned_back(grads, cosine, sine)
-        factor = head_scale(values)
-        plain = values * factor
-        d_head[...] += jnp.sum(grads * plain, axis=0, keepdims=True)
-        grads = grads * gain
-        mean = jnp.mean(grads * plain, axis=1, keepdims=True)
-        d_lin_ref[:, span] = (factor * (grads - plain * mean)).astype(low)
-    d_lin_ref[:, (heads + 1) * width :] = d_value_ref[...].astype(low)
-    d_one = dot_nt(d_lin_ref[...], w_ref[...])
-    d_one_ref[...] = d_one.astype(low)
-    d_gain[...] += jnp.sum(d_one * rows_ref[...].astype(wide), axis=0, keepdims=True) / gain_ref[...]
 
 
 def row_call(kernel, rows, tiled, fixed, outs, sums):
@@ -1123,24 +1255,27 @@
         ids = ids + zero_of(sides[0][2]).astype(jnp.int32)
     hiddens, d_ins, d_gate_parts, made_parts, back_parts = zip(*sides)
     half_shape = (2,) * len(turn) + (count, model_width)
-    far_back = lax.ppermute(back_parts[1], core[0], SWAP)
     far_made = lax.ppermute(made_parts[1], core[0], SWAP)
     far_parts = 1 << len(far_axes)
     straight = parts_near * rows_d == TILE
     d_gates = jnp.stack(d_gate_parts).reshape(experts, 1, count)
     hiddens = [part.reshape(blocks, count, hidden_width) for part in hiddens]
     d_ins = [part.reshape(blocks, count, 2 * hidden_width) for part in d_ins]
-    back = [part.reshape(half_shape) for part in (back_parts[0], far_back)]
-    d_rows_two, d_gates, part_down, part_in = transfer(
-        4,
-        [
-            ReduceBoth(turn, *back, cluster_parts),
-            Direct(core + turn, d_gates, (1, count)),
-            WeightGrad(hiddens, [own_grads, far_grads]),
-            WeightGrad([own_two, far_two], d_ins, far_parts if straight else 1),
-        ],
-        (-1, 0, -2),
-    )
+    back = [part.reshape(half_shape) for part in back_parts]
+    down_task = WeightGrad(hiddens, [own_grads, far_grads])
+    in_task = WeightGrad(
+        [own_two, far_two], d_ins, far_parts if straight else 1, 2, room=down_task
+    )
+    flows = [
+        ReduceBoth(turn, *back, cluster_parts, core),
+        Direct(core + turn, d_gates, (1, count)),
+        down_task,
+        in_task,
+    ]
+    in_pair = len(far_axes) == 1 and parts_near * rows_f % ROW_TILE == 0
+    if in_pair:
+        flows.append(PairSum(far_axes[0], down_task, parts_c, parts_near * rows_f))
+    d_rows_two, d_gates, part_down, part_in, *sums = transfer(4, flows, (-1, 2, 0, -2, 0, -2, 0))
     d_gates = d_gates.reshape((2,) * len(cluster_axes) + (count,))
     spots = [(core + turn).index(axis) for axis in cluster_axes]
     d_gates = d_gates.transpose(spots + [len(spots)]).reshape(experts, count).T
@@ -1157,7 +1292,11 @@
             return stack[0]
         return lax.psum_scatter(stack, far_axes, scatter_dimension=0, tiled=False)
 
-    share_in, share_down = to_far(part_in, rows_d, straight), to_far(part_down, rows_f)
+    share_in = to_far(part_in, rows_d, straight)
+    if in_pair:
+        share_down = sums[0].reshape(team, rows_f, model_width)
+    else:
+        share_down = to_far(part_down, rows_f)
 
     d_logits = (gates * (d_gates - jnp.sum(gates * d_gates, axis=-1, keepdims=True))).astype(low)
     part_router = dot_tn(normed_two, d_logits)
@@ -1194,27 +1333,41 @@
         scale,
         10,
     )
-    d_lin, d_one, d_gain_query, d_gain_key, d_gain_attn = row_call(
-        functools.partial(unprep_kernel, heads, scale),
-        rows,
+    heads_back = HeadsBack(
+        heads,
+        scale,
         (
             d_query.reshape(rows, q_cols),
             d_keyed.reshape(rows, width),
             d_value.reshape(rows, width),
             lin,
-            w_qkv,
             cosine,
             sine,
-        )
-        + head_gains
-        + (all_one, gain_attn[None]),
-        (4, 7, 8, 10),
-        [(qkv_cols, low), (model_width, low)],
-        [width, width, model_width],
-    )
-    d_one = d_one.reshape(plane_shape)
+            all_one,
+        ),
+        w_qkv,
+        head_gains + (gain_attn[None],),
+        d_gain_ffn.reshape(-1, width),
+        plane_axes,
+    )
     part_out = weight_grad([mixed_rows], [d_branch]).reshape(q_cols, model_width)
-    part_qkv = weight_grad([all_one], [d_lin], parts_c, parts_f)
+    pieces_tile = TILE // rows_d
+    runs = parts_f // pieces_tile
+    spare = len(f_axes) - (pieces_tile.bit_length() - 1)
+    qkv_shape = (2,) * len(f_axes) + (parts_c * rows_d, qkv_cols)
+
+    def qkv_place(step):
+        bits = [step % runs // (runs >> (bit + 1)) % 2 for bit in range(spare)]
+        return tuple(bits) + (0,) * (len(f_axes) - spare) + (step // runs, 0)
+
+    qkv_block = (None,) * spare + (2,) * (len(f_axes) - spare) + (rows_d, qkv_cols)
+    stack = (1 << len(plane_axes), count)
+    qkv_task = WeightGrad(
+        [all_one.reshape(stack + (model_width,))],
+        [jax.ShapeDtypeStruct(stack + (qkv_cols,), low)],
+        source=lambda: heads_back.refs[1][0],
+        out=(qkv_shape, qkv_block, qkv_place),
+    )
 
     turn_back = plane_axes[len(g_axes) : -1] + g_axes
     def over_groups(shape):
@@ -1226,13 +1379,23 @@
     flows = [
         Spread(team_axes, g_axes, share_down, share_down.shape[1:]),
         Spread(team_axes, g_axes, share_in, share_in.shape[1:]),
-        Reduce(plane_axes, d_one, core_first([(lo, hi, turn_back) for lo, hi, _ in plane_parts])),
-        Reduce(
-            f_axes,
-            part_qkv.reshape((2,) * len(f_axes) + (parts_c * rows_d, qkv_cols)),
-            [(0, parts_c * rows_d, f_axes[::-1])],
-            jax.ShapeDtypeStruct((parts_c, rows_d, qkv_cols), low),
-            to_column_owners,
+        Fed(
+            Reduce(
+                plane_axes,
+                heads_back.results[1],
+                core_first([(lo, hi, turn_back) for lo, hi, _ in plane_parts]),
+            ),
+            lambda: heads_back.refs[1][1],
+        ),
+        Fed(
+            Reduce(
+                f_axes,
+                qkv_task.results[0],
+                [(0, parts_c * rows_d, f_axes[::-1])],
+                jax.ShapeDtypeStruct((parts_c, rows_d, qkv_cols), low),
+                to_column_owners,
+            ),
+            lambda: qkv_task.refs[1][0],
         ),
         Reduce(
             own_axes,
@@ -1246,21 +1409,24 @@
         rows = q_cols // parts_f
         stack = part_out.reshape((2,) * len(f_axes) + (rows, model_width))
         shape = jax.ShapeDtypeStruct((rows, model_width), low)
-        flows.append(Reduce(f_axes, stack, [(0, rows, f_axes[::-1])], shape, over_groups))
+        flows.append(Later(Reduce(f_axes, stack, [(0, rows, f_axes[::-1])], shape, over_groups)))
     if near_axes:
         near_shape = (2,) * len(near_axes) + (count, model_width)
         near_flow = Reduce(
             near_axes, made.astype(low).reshape(near_shape), [(0, count, near_axes)], by_distance=True
         )
-        flows.append(near_flow)
-    gains = jnp.concatenate([d_gain_attn[0], d_gain_ffn, d_gain_query[0], d_gain_key[0]])
-    lines = -(-gains.size // (8 * width)) * 8
-    gains = jnp.pad(gains, (0, lines * width - gains.size)).reshape(lines, width)
-    flows.insert(5, Gather(all_axes, gains, [(0, lines, core + all_axes_but_core)]))
+        flows.append(Later(near_flow))
+    lines = jax.ShapeDtypeStruct((heads_back.lines, width), wide)
+    gains_flow = Gather(all_axes, lines, [(0, heads_back.lines, core + all_axes_but_core)])
+    flows.insert(5, Fed(gains_flow, lambda: heads_back.refs[2][0]))
+    flows += [heads_back, qkv_task]
     all_down, all_in, d_one, all_qkv, share_router, gains, *rest = transfer(
-        7, flows, (2, 0, 1, 2, 3, 7, 6, 4, 5, 3, 3, 6, 6, 4, 5, 3, 4, 5)
-    )
-    gains = jnp.sum(gains.reshape(-1, lines * width), axis=0)
+        7,
+        flows,
+        (-1, 0, 2, -2, 2, 3, 1, 6, 5, 3, 2, 6, 7, 3, 3, 6, 6, 3, 4, 5, 4, 5, 4, 5, 4, 5),
+    )
+    rest = rest[:-3]
+    gains = jnp.sum(gains.reshape(-1, heads_back.lines * width), axis=0)
     share_router = share_router.reshape(groups, rows_d, width)[:, :, :experts]
     grad_router = jnp.sum(share_router.astype(wide), axis=0)
     if near_axes:

time: 1150 us -> 1110 us (0.965)
  Pallas kernels: 1030 us -> 1010 us
  waiting for transfers between devices: 17 us -> 2.35 us
    pallas_call x2 -> x1, Pallas kernels: 41 us -> 15.5 us  [row_call(): pl.pallas_call(kernel, grid=(rows // tile,), in_specs=[whole_block(array....]
    pallas_call x6, Pallas kernels: 774 us -> 789 us  [transfer(): pl.pallas_call(functools.partial(flow_kernel, flows, plan), out_shape=sha...]
    pallas_call x2 -> x1, Pallas kernels: 22.3 us -> 9.57 us  [weight_grad(): pl.pallas_call(functools.partial(weight_kernel, amount), grid=(columns //...]
  transfers between devices with their start and end apart: 8 -> 6, of which waited for: 3 -> 1; matrix products, arithmetic and copies ran while one was open for 4% -> 4% of each run, Pallas kernels for 38% -> 36%
where the time goes in v5:
time: 1110 us; the launch traced here: 1100 us
  Pallas kernels  1010 us (91%)
  local copies, waits for them, and re-layouts  31.9 us (3%)
  other arithmetic  27.8 us (3%)
  matrix products  18.7 us (2%)
  between operations  15.6 us (1%)
    pallas_call x6, Pallas kernels, transfer(): pl.pallas_call(functools.partial(flow_kernel, flows, plan), out_shape=sha...  789 us
    pallas_call x2, Pallas kernels, expert_rows(): pl.pallas_call(functools.partial(expert_kernel, near), grid_spec=pltpu.Pr...  104 us
    pallas_call x2, Pallas kernels, attention_call(): pl.pallas_call(functools.partial(kernel, scale), grid=(seqs, length // ti...  71.4 us
  transfers between devices with their start and end apart: 6, of which 1 were waited for; matrix products, arithmetic and copies ran while one was open for 4% of the time, Pallas kernels for 36%

profile of v5, /device:TPU:0, one launch (start us, length us, event | category | flops | bytes accessed | tf_op | source)
XLA Modules:
  0.0 1102.7 jit_solution(7551421635520804770)
XLA Ops:
  7.2 2.6 reshape.221
  19.1 214.9 %shard_map.272 = (bf16[2,2,2,256,2048]{4,3,2,1,0:T(8,128)(2,1)}, bf16[4,2,2,128,768]{4,3,2,1,0:T(8,128)(2,1)}, bf16[2,2,2,256,2048]{4,3,2,1,0:T(8,128)(2,1)}, bf...) custom-call(bf16[256,2048]{1,0:T(8,128)(2,1)} %fusion.5.refs_0_, ...), custom_call_target="tpu_custom_call" | custom-call | tf_op jit(solution)/shard_map/pallas_call | solution.py:695
  235.4 15.5 %shard_map.273 = (f32[2048,640]{1,0:T(8,128)}, bf16[2048,512]{1,0:T(8,128)(2,1)}, bf16[2048,128]{1,0:T(8,128)(2,1)S(1)}, bf16[2048,128]{1,0:T(8,128)(2,1)S(1)}, ...) custom-call(bf16[2048,2048]{1,0:T(8,128)(2,1)} %bitcast.143, bf16[2048,768]{1,0:T(8,128)(2,1)} %bitcast.146, ...), custom_call_target="tpu_custom_call" | custom-call | tf_op jit(solution)/shard_map/pallas_call | solution.py:961
  254.1 31.6 %shard_map.274 = (bf16[2,1024,512]{2,1,0:T(8,128)(2,1)S(1)}, f32[2,4,1,1024]{3,2,1,0:T(1,128)S(1)}) custom-call(s32[2,1024,1]{2,1,0:T(8,128)S(1)} %copy.91.k_place, s32[2,1024,1]{2,1,0:T(8,128)S(1)} %copy.92.k_segment, s32[2,1,1024]{2,1,0:T(1,128)S(1)} %get-tuple-element.159.q_place, s32[2,1,1024]{2,1,0:T(1,128)S(1)} %get-tuple-element.156.q_segment, ...), custom_call_target="tpu_custom_call" | custom-call | tf_op jit(solution)/shard_map/pallas_call | solution.py:1047
  285.7 6.8 convolution_convert_fusion
  292.5 48.3 %shard_map.275 = f32[256,2048]{1,0:T(8,128)} custom-call(bf16[2,2,2,256,2048]{4,3,2,1,0:T(8,128)(2,1)} %bitcast.157), custom_call_target="tpu_custom_call" | custom-call | tf_op jit(solution)/shard_map/pallas_call | solution.py:695
  346.5 96.4 %shard_map.276 = (bf16[2,2,2,256,2048]{4,3,2,1,0:T(8,128)(2,1)}, f32[2,2,2,2,16,256]{5,4,3,2,1,0:T(8,128)}) custom-call(bf16[256,2048]{1,0:T(8,128)(2,1)} %copy-done.18, f32[16,256]{1,0:T(8,128)} %fusion.19.refs_1_), custom_call_target="tpu_custom_call" | custom-call | tf_op jit(solution)/shard_map/pallas_call | solution.py:695
  445.7 4.0 copy.106
  451.1 51.9 %shard_map.277 = (bf16[2048,768]{1,0:T(8,128)(2,1)}, bf16[2048,1536]{1,0:T(8,128)(2,1)}, f32[2048,1]{1,0:T(8,128)S(1)}, bf16[2048,2048]{1,0:T(8,128)(2,1)}, bf16[2048,2048]{1,0:T(8,128)(2,1)}) custom-call(s32[8]{0:T(128)S(1)} %iota_xor_fusion.ids_ref, bf16[8,256,2048]{2,1,0:T(8,128)(2,1)} %bitcast.152, bf16[8,256,2048]{2,1,0:T(8,128)(2,1)} %bitcast.149, ...), custom_call_target="tpu_custom_call" | custom-call | flops 927712935936 | bytes 58720256 | tf_op jit(solution)/shard_map/pallas_call | solution.py:800
  505.1 2.2 reduce.1
  507.3 51.7 %shard_map.278 = (bf16[2048,768]{1,0:T(8,128)(2,1)}, bf16[2048,1536]{1,0:T(8,128)(2,1)}, f32[2048,1]{1,0:T(8,128)S(1)}, bf16[2048,2048]{1,0:T(8,128)(2,1)}, bf16[2048,2048]{1,0:T(8,128)(2,1)}) custom-call(s32[8]{0:T(128)S(1)} %broadcast_add_fusion.ids_ref, bf16[8,256,2048]{2,1,0:T(8,128)(2,1)} %collective-permute-done.rows_ref.refs_8_, ...), custom_call_target="tpu_custom_call" | custom-call | flops 927712935936 | bytes 58720256 | tf_op jit(solution)/shard_map/pallas_call | solution.py:800
  562.2 124.8 %shard_map.279 = (f32[256,2048]{1,0:T(8,128)}, f32[16,1,256]{2,1,0:T(1,128)}, bf16[768,2048]{1,0:T(8,128)(2,1)}, bf16[2048,1536]{1,0:T(8,128)(2,1)}, bf16[4,96,2048]{2,1,0:T(8,128)(2,1)}) custom-call(bf16[2,2,2,256,2048]{4,3,2,1,0:T(8,128)(2,1)} %bitcast.154, bf16[2,2,2,256,2048]{4,3,2,1,0:T(8,128)(2,1)} %bitcast.155, f32[16,1,256]{2,1,0:T(1,128)} %bitcast.185, ...), custom_call_target="tpu_custom_call" | custom-call | tf_op jit(solution)/shard_map/pallas_call | solution.py:695
  692.4 4.2 multiply_reduce_fusion
  696.6 2.4 fusion.25
  700.7 109.3 %shard_map.280 = (bf16[2,2,2,256,2048]{4,3,2,1,0:T(8,128)(2,1)}, f32[512,2048]{1,0:T(8,128)}) custom-call(bf16[256,2048]{1,0:T(8,128)(2,1)} %get-tuple-element.146.refs_0_, bf16[2,2,512,2048]{3,2,1,0:T(8,128)(2,1)} %bitcast.160, bf16[2,2,512,2048]{3,2,1,0:T(8,128)(2,1)} %bitcast.54.refs_2_), custom_call_target="tpu_custom_call" | custom-call | tf_op jit(solution)/shard_map/pallas_call | solution.py:695
  810.0 9.6 shard_map.281
  819.6 4.0 convert_element_type.67
  823.5 5.8 convolution_convert_fusion.1
  829.3 39.8 %shard_map.282 = (bf16[2,1024,512]{2,1,0:T(8,128)(2,1)}, f32[2,1024,128]{2,1,0:T(8,128)S(1)}, f32[2,1024,128]{2,1,0:T(8,128)S(1)}) custom-call(s32[2,1024,1]{2,1,0:T(8,128)S(1)} %copy.91.k_place, s32[2,1024,1]{2,1,0:T(8,128)S(1)} %copy.92.k_segment, s32[2,1,1024]{2,1,0:T(1,128)S(1)} %get-tuple-element.159.q_place, ...), custom_call_target="tpu_custom_call" | custom-call | tf_op jit(solution)/shard_map/pallas_call | solution.py:1047
  871.1 195.3 %shard_map.283 = (bf16[8,2,48,2048]{3,2,1,0:T(8,128)(2,1)}, bf16[8,2,128,1536]{3,2,1,0:T(8,128)(2,1)}, f32[256,2048]{1,0:T(8,128)}, bf16[4,2,128,768]{3,2,1,0:T(...) custom-call(bf16[8,48,2048]{2,1,0:T(8,128)(2,1)} %bitcast.179, ...), custom_call_target="tpu_custom_call" | custom-call | tf_op jit(solution)/shard_map/pallas_call | solution.py:695
  1068.6 7.7 shard_map.285
  1076.3 5.1 shard_map.286
  1083.6 3.8 shard_map.284
  1089.7 6.0 fusion.2
  (184 shorter events, 43.4 us)
Async XLA Ops:
  7.2 7.1 copy-start
  7.2 443.9 %all-gather.5.cloned.1.call-start = ((), (), s32[]{:S(2)}) async-start(), calls=%async_computation.2 | async-start | bytes 4718592 | tf_op jit(solution)/shard_map/all_gather | solution.py:1183
  234.1 217.0 %all-gather.7.cloned.1.call-start = ((), (), s32[]{:S(2)}) async-start(), calls=%async_computation.3 | async-start | bytes 4718592 | tf_op jit(solution)/shard_map/all_gather | solution.py:1183
  234.8 636.2 %reduce-scatter.2.cloned.1.call-start = ((), (), s32[]{:S(2)}) async-start(), calls=%async_computation.1 | async-start | bytes 9437184 | tf_op jit(solution)/shard_map/reduce_scatter | solution.py:1293
  254.1 31.6 %copy-start.54 = (bf16[2,2,128,2048]{3,2,1,0:T(8,128)(2,1)S(1)}, bf16[2,2,128,2048]{3,2,1,0:T(8,128)(2,1)}, u32[]{:S(2)}) copy-start(bf16[2,2,128,2048]{3,2,1,0:T(8,128)(2,1)} %get-tuple-element.72) | copy-start | bytes 6291460
  285.7 6.8 copy-start.2
  292.5 48.3 %copy-start.50 = (s32[1,256,8]{1,2,0:T(8,128)S(1)}, s32[1,256,8]{1,2,0:T(8,128)}, u32[]{:S(2)}) copy-start(s32[1,256,8]{1,2,0:T(8,128)} %param.20) | copy-start | bytes 24580
  292.5 48.4 %copy-start.16 = (bf16[1,256,2048]{2,1,0:T(8,128)(2,1)S(1)}, bf16[1,256,2048]{2,1,0:T(8,128)(2,1)}, u32[]{:S(2)}) copy-start(bf16[1,256,2048]{2,1,0:T(8,128)(2,1)} %param.17) | copy-start | bytes 3145732
  442.9 64.3 %collective-permute-start = (bf16[8,256,2048]{2,1,0:T(8,128)(2,1)}, bf16[8,256,2048]{2,1,0:T(8,128)(2,1)}, u32[]{:S(2)}, u32[]{:S(2)}) collective-permute-start(bf16[8,256,2048]{2,1,0:T(8,128)(2,1)} %bitcast.151), channel_id=1, source_target_pairs={{0,4},{4,0},{1,5},{5,1},{2,6},{6,2},{3,7},{7,3},{8,12},{12,8},{9,1... | collective-permute-start | bytes 25165832 | tf_op jit(solution)/shard_map/ppermute | solution.py:1243
  443.4 63.9 %collective-permute-start.1 = (bf16[8,256,2048]{2,1,0:T(8,128)(2,1)}, bf16[8,256,2048]{2,1,0:T(8,128)(2,1)}, u32[]{:S(2)}, u32[]{:S(2)}) collective-permute-start(bf16[8,256,2048]{2,1,0:T(8,128)(2,1)} %bitcast.148), channel_id=1, source_target_pairs={{0,4},{4,0},{1,5},{5,1},{2,6},{6,2},{3,7},{7,3},{8,12},{12,8},{9,1... | collective-permute-start | bytes 25165832 | tf_op jit(solution)/shard_map/ppermute | solution.py:1173
  507.3 54.3 %copy-start.35 = (f32[2048]{0:T(1024)S(1)}, f32[2048]{0:T(1024)}, u32[]{:S(2)}) copy-start(f32[2048]{0:T(1024)} %reduce.1) | copy-start | bytes 24580
  687.1 5.3 copy-start.33
  687.1 5.3 copy-start.39
  687.1 13.6 %collective-permute-start.2 = (bf16[2048,2048]{1,0:T(8,128)(2,1)}, bf16[2048,2048]{1,0:T(8,128)(2,1)}, u32[]{:S(2)}, u32[]{:S(2)}) collective-permute-start(bf16[2048,2048]{1,0:T(8,128)(2,1)} %get-tuple-element.93), channel_id=1, source_target_pairs={{0,4},{4,0},{1,5},{5,1},{2,6},{6,2},{3,7},{7,3},{8,12},{12,8},{9,1... | collective-permute-start | bytes 25165832 | tf_op jit(solution)/shard_map/ppermute | solution.py:1258
  692.4 4.2 copy-start.19
  692.4 4.2 copy-start.21
  810.0 13.6 %copy-start.20 = (bf16[2,2,2,256,2048]{4,3,2,1,0:T(8,128)(2,1)S(1)}, bf16[2,2,2,256,2048]{4,3,2,1,0:T(8,128)(2,1)}, u32[]{:S(2)}) copy-start(bf16[2,2,2,256,2048]{4,3,2,1,0:T(8,128)(2,1)} %get-tuple-element.94) | copy-start | bytes 25165828
  823.5 5.8 copy-start.4
  1076.3 5.2 copy-start.17
  1076.3 5.2 copy-start.31
  1081.5 5.9 copy-start.23
  1083.6 5.4 copy-start.34
  1083.6 6.1 copy-start.45
  1089.7 6.0 copy-start.1
  (38 other events, 74.0 us)
Sparse Core Ops, SparseCore 0:
  234.2 77.8 all-gather.4
  313.7 78.6 all-gather.6
  687.2 144.0 reduce-scatter.1

commit v6 on v5

--- a/solution.py
+++ b/solution.py
@@ -1,4 +1,5 @@
 import functools
+import itertools
 import math
 
 import jax
@@ -330,9 +331,9 @@
 
 
 class ReduceBoth(Reduce):
-    def __init__(self, axes, operand, other, parts, first=()):
+    def __init__(self, axes, operand, other, parts, first=(), hold=False):
         super().__init__(axes, operand, parts, by_distance=True)
-        self.first = first
+        self.first, self.hold = first, hold
         self.flips = self.flips + [(axis,) for axis in first]
         self.operands = [operand, other]
         shape = operand.shape
@@ -413,8 +414,13 @@
             add_all(
                 lo, hi, self.axes, lambda bits: tuple(bits[axis] for axis in self.axes), added, False
             )
-            start(number, 0)
+            if not self.hold:
+                start(number, 0)
         yield
+        if self.hold:
+            for number in range(len(self.parts)):
+                start(number, 0)
+            yield
         for stage in range(stages):
             for number, (lo, hi, order) in enumerate(self.parts):
                 copies[number, stage].wait_recv()
@@ -505,6 +511,128 @@
     flips = ()
 
 
+def bit_spots(blocks):
+    return list(itertools.product((0, 1), repeat=blocks.bit_length() - 1))
+
+
+def bits_of(step, blocks):
+    amount = blocks.bit_length() - 1
+    return tuple(step // (blocks >> (bit + 1)) % 2 for bit in range(amount))
+
+
+class Branch(Task):
+    def __init__(self, source, w_mix, seqs, blocks, count):
+        self.source, self.seqs, self.blocks, self.count = source, seqs, blocks, count
+        self.columns, self.model_width = w_mix.shape
+        self.operands = [w_mix]
+        shape = (seqs, blocks // seqs * count, self.columns)
+        self.results = [jax.ShapeDtypeStruct(shape, low)]
+        self.scratch = [pltpu.VMEM(w_mix.shape, low), sems(1)]
+
+    def run(self, operands, results, scratch):
+        w_ref, done = scratch
+        copy = pltpu.make_async_copy(operands[0], w_ref, done.at[0])
+        copy.start()
+        copy.wait()
+        each = self.blocks // self.seqs
+
+        def body(rows_ref, out_ref):
+            out_ref[...] = dot_nt(rows_ref[...], w_ref[...]).astype(low)
+
+        free = (None,) * (self.blocks.bit_length() - 1)
+        pltpu.emit_pipeline(
+            body,
+            grid=(self.blocks,),
+            in_specs=[
+                pl.BlockSpec(
+                    free + (self.count, self.model_width),
+                    lambda step: bits_of(step, self.blocks) + (0, 0),
+                )
+            ],
+            out_specs=[
+                pl.BlockSpec(
+                    (None, self.count, self.columns), lambda step: (step // each, step % each, 0)
+                )
+            ],
+        )(self.source(), results[0])
+
+
+class HeadsBehind(Task):
+    def __init__(self, source, marks, arrays, scale, tile=256):
+        self.source, self.scale, self.tile, self.calls = source, scale, tile, 0
+        place, segment = marks
+        query, keyed = arrays[:2]
+        self.seqs, self.length, columns = query.shape
+        self.width = keyed.shape[2]
+        self.heads = columns // self.width
+        self.operands = [place[:, :, None], segment[:, :, None], place[:, None], segment[:, None]]
+        self.operands += list(arrays)
+        self.results = [
+            jax.ShapeDtypeStruct(query.shape, low),
+            jax.ShapeDtypeStruct(keyed.shape, wide),
+            jax.ShapeDtypeStruct(keyed.shape, wide),
+        ]
+        total = pltpu.VMEM((self.length, self.width), wide)
+        self.scratch = [pltpu.VMEM((self.length, tile), wide), total, total]
+
+    def run(self, operands, results, scratch):
+        bias, d_k_total, d_v_total = scratch
+        seq = self.calls
+        self.calls = (self.calls + 1) % self.seqs
+        tiles = self.length // self.tile
+        d_k_total[...] = jnp.zeros_like(d_k_total)
+        d_v_total[...] = jnp.zeros_like(d_v_total)
+
+        def body(
+            k_place,
+            k_segment,
+            q_place,
+            q_segment,
+            q_ref,
+            k_ref,
+            v_ref,
+            kt_ref,
+            total_ref,
+            d_mixed_ref,
+            d_q_ref,
+            d_k_ref,
+            d_v_ref,
+        ):
+            at, head = pl.program_id(0), pl.program_id(1)
+
+            @pl.when(head == 0)
+            def _():
+                allowed = (k_segment[...] == q_segment[...]) & (k_place[...] <= q_place[...])
+                bias[...] = jnp.where(allowed, 0.0, -1e30)
+
+            query, d_mixed = q_ref[...], d_mixed_ref[...]
+            probs = jnp.exp(dot_nt(k_ref[...], query) * self.scale + bias[...] - total_ref[...])
+            d_probs = dot_nt(v_ref[...], d_mixed)
+            row_dot = jnp.sum(probs * d_probs, axis=0, keepdims=True)
+            d_scores = (probs * (d_probs - row_dot)).astype(low)
+            d_v_total[...] += dot(probs.astype(low), d_mixed)
+            d_k_total[...] += dot(d_scores, query)
+            d_q_ref[...] = (dot(kt_ref[...], d_scores) * self.scale).T.astype(low)
+
+            @pl.when((at == tiles - 1) & (head == self.heads - 1))
+            def _():
+                d_k_ref[...] = d_k_total[...]
+                d_v_ref[...] = d_v_total[...]
+
+        column = pl.BlockSpec((None, self.length, 1), lambda i, h: (seq, 0, 0))
+        row = pl.BlockSpec((None, 1, self.tile), lambda i, h: (seq, 0, i))
+        query = pl.BlockSpec((None, self.tile, self.width), lambda i, h: (seq, i, h))
+        keys = pl.BlockSpec((None, self.length, self.width), lambda i, h: (seq, 0, 0))
+        flat = pl.BlockSpec((None, self.width, self.length), lambda i, h: (seq, 0, 0))
+        total = pl.BlockSpec((None, None, 1, self.tile), lambda i, h: (seq, h, 0, i))
+        pltpu.emit_pipeline(
+            body,
+            grid=(tiles, self.heads),
+            in_specs=[column, column, row, row, query, keys, keys, flat, total, query],
+            out_specs=[query, keys, keys],
+        )(*operands, self.source(), *results)
+
+
 class WeightGrad(Task):
     def __init__(self, lefts, rights, turns=1, pieces=1, source=None, out=None, room=None):
         self.amount, self.turns, self.pieces, self.calls = len(lefts), turns, pieces, 0
@@ -515,7 +643,7 @@
         self.out = out or ((self.columns, self.width), (TILE, self.width), self.place)
         self.results = [jax.ShapeDtypeStruct(self.out[0], low)]
         shape = (self.amount, self.blocks, self.rows, self.width)
-        self.scratch = [sems(self.amount)] + ([] if room else [pltpu.VMEM(shape, low)])
+        self.scratch = [sems(max(self.amount, self.blocks))] + ([] if room else [pltpu.VMEM(shape, low)])
 
     def run(self, operands, results, scratch):
         done = scratch[0]
@@ -528,7 +656,13 @@
                     right, held.at[number, :, :, pl.ds(0, self.width)], done.at[number]
                 )
                 for number, right in enumerate(rights)
+                if len(right.shape) == 3
             ]
+            if not copies:
+                copies = [
+                    pltpu.make_async_copy(rights[0].at[bits], held.at[0, number], done.at[number])
+                    for number, bits in enumerate(bit_spots(self.blocks))
+                ]
             for copy in copies:
                 copy.start()
             for copy in copies:
@@ -1309,29 +1443,30 @@
     made_shape = (2,) * len(made_axes) + (parts_near * count, model_width)
     made = (made_parts[0].reshape(made_shape), far_made.reshape(made_shape))
     made_spans = [(lo * parts_near, hi * parts_near, order) for lo, hi, order in plane_parts]
-    d_branch, made = transfer(
+    branch_flow = Gather(plane_axes, d_resid_one.astype(low), core_last(plane_parts))
+    planes = 1 << len(plane_axes)
+    branch_task = Branch(lambda: branch_flow.refs[1][0], w_mix, groups, planes, count)
+    behind_task = HeadsBehind(
+        lambda: branch_task.refs[1][0],
+        (place, segment),
+        (query_low, keyed_low, value_low, keyed_low.transpose(0, 2, 1), log_total),
+        scale,
+    )
+    out_task = WeightGrad(
+        [mixed_rows.reshape(planes, count, q_cols)],
+        [jax.ShapeDtypeStruct((planes, count, model_width), low)],
+        source=lambda: branch_flow.refs[1][0],
+    )
+    _, made, _, d_query, d_keyed, d_value, part_out = transfer(
         5,
         [
-            Gather(plane_axes, d_resid_one.astype(low), core_last(plane_parts)),
-            ReduceBoth(made_axes, *made, made_spans),
+            branch_flow,
+            ReduceBoth(made_axes, *made, made_spans, hold=True),
+            branch_task,
+            behind_task,
+            out_task,
         ],
-    )
-    d_branch = d_branch.reshape(-1, model_width)
-    d_mixed = dot_nt(d_branch, w_mix).astype(low).reshape(query_low.shape)
-    shapes = [
-        jax.ShapeDtypeStruct(query_low.shape, low),
-        jax.ShapeDtypeStruct(keyed_low.shape, wide),
-        jax.ShapeDtypeStruct(keyed_low.shape, wide),
-    ]
-    d_query, d_keyed, d_value = attention_call(
-        behind_kernel,
-        (place, segment),
-        (query_low, d_mixed, keyed_low, value_low, keyed_low.transpose(0, 2, 1), log_total),
-        ("query", "query", "keys", "keys", "flat", "total"),
-        list(zip(("query", "keys", "keys"), shapes)),
-        width,
-        scale,
-        10,
+        (0,) * (len(plane_axes) - 1) + (1, 0, -1) + (-2,) * groups + (1, -3, 1),
     )
     heads_back = HeadsBack(
         heads,
@@ -1350,7 +1485,6 @@
         d_gain_ffn.reshape(-1, width),
         plane_axes,
     )
-    part_out = weight_grad([mixed_rows], [d_branch]).reshape(q_cols, model_width)
     pieces_tile = TILE // rows_d
     runs = parts_f // pieces_tile
     spare = len(f_axes) - (pieces_tile.bit_length() - 1)

time: 1110 us -> 1070 us (0.964)
  Pallas kernels: 1010 us -> 978 us
    pallas_call x2 -> x1, Pallas kernels: 71.4 us -> 31.7 us  [attention_call(): pl.pallas_call(functools.partial(kernel, scale), grid=(seqs, length // ti...]
    pallas_call x6, Pallas kernels: 789 us -> 810 us  [transfer(): pl.pallas_call(functools.partial(flow_kernel, flows, plan), out_shape=sha...]
  transfers between devices with their start and end apart: 6 -> 6, of which waited for: 1 -> 1; matrix products, arithmetic and copies ran while one was open for 4% -> 3% of each run, Pallas kernels for 36% -> 35%
where the time goes in v6:
time: 1070 us; the launch traced here: 1060 us
  Pallas kernels  978 us (91%)
  local copies, waits for them, and re-layouts  24.4 us (2%)
  other arithmetic  23.2 us (2%)
  between operations  15.7 us (1%)
  matrix products  12.5 us (1%)
    pallas_call x6, Pallas kernels, transfer(): pl.pallas_call(functools.partial(flow_kernel, flows, plan), out_shape=sha...  810 us
    pallas_call x2, Pallas kernels, expert_rows(): pl.pallas_call(functools.partial(expert_kernel, near), grid_spec=pltpu.Pr...  104 us
    pallas_call x1, Pallas kernels, attention_call(): pl.pallas_call(functools.partial(kernel, scale), grid=(seqs, length // ti...  31.7 us
  transfers between devices with their start and end apart: 6, of which 1 were waited for; matrix products, arithmetic and copies ran while one was open for 3% of the time, Pallas kernels for 35%

profile of v6, /device:TPU:0, one launch (start us, length us, event | category | flops | bytes accessed | tf_op | source)
XLA Modules:
  0.0 1058.5 jit_solution(8869623013441146794)
XLA Ops:
  7.2 1.9 reshape.218
  17.1 214.9 %shard_map.272 = (bf16[2,2,2,256,2048]{4,3,2,1,0:T(8,128)(2,1)}, bf16[4,2,2,128,768]{4,3,2,1,0:T(8,128)(2,1)}, bf16[2,2,2,256,2048]{4,3,2,1,0:T(8,128)(2,1)}, bf...) custom-call(bf16[256,2048]{1,0:T(8,128)(2,1)} %fusion.5.refs_0_, ...), custom_call_target="tpu_custom_call" | custom-call | tf_op jit(solution)/shard_map/pallas_call | solution.py:829
  233.4 15.5 %shard_map.273 = (f32[2048,640]{1,0:T(8,128)}, bf16[2048,512]{1,0:T(8,128)(2,1)}, bf16[2048,128]{1,0:T(8,128)(2,1)S(1)}, bf16[2048,128]{1,0:T(8,128)(2,1)S(1)}, ...) custom-call(bf16[2048,2048]{1,0:T(8,128)(2,1)} %bitcast.137, bf16[2048,768]{1,0:T(8,128)(2,1)} %bitcast.140, ...), custom_call_target="tpu_custom_call" | custom-call | tf_op jit(solution)/shard_map/pallas_call | solution.py:1095
  252.1 31.7 %shard_map.274 = (bf16[2,1024,512]{2,1,0:T(8,128)(2,1)S(1)}, f32[2,4,1,1024]{3,2,1,0:T(1,128)S(1)}) custom-call(s32[2,1024,1]{2,1,0:T(8,128)S(1)} %copy.91.k_place.refs_4_, s32[2,1024,1]{2,1,0:T(8,128)S(1)} %copy.92.k_segment.refs_5_, s32[2,1,1024]{2,1,0:T(1,128)S(1)} %get-tuple-element.159.q_place.refs_6_, ...), custom_call_target="tpu_custom_call" | custom-call | tf_op jit(solution)/shard_map/pallas_call | solution.py:1181
  283.9 6.8 convolution_convert_fusion
  290.7 48.4 %shard_map.275 = f32[256,2048]{1,0:T(8,128)} custom-call(bf16[2,2,2,256,2048]{4,3,2,1,0:T(8,128)(2,1)} %bitcast.151), custom_call_target="tpu_custom_call" | custom-call | tf_op jit(solution)/shard_map/pallas_call | solution.py:829
  339.2 2.0 multiply_reduce_fusion.2
  344.3 96.4 %shard_map.276 = (bf16[2,2,2,256,2048]{4,3,2,1,0:T(8,128)(2,1)}, f32[2,2,2,2,16,256]{5,4,3,2,1,0:T(8,128)}) custom-call(bf16[256,2048]{1,0:T(8,128)(2,1)} %copy-done.20, f32[16,256]{1,0:T(8,128)} %fusion.19.refs_1_), custom_call_target="tpu_custom_call" | custom-call | tf_op jit(solution)/shard_map/pallas_call | solution.py:829
  443.5 4.0 copy.106
  448.8 51.9 %shard_map.277 = (bf16[2048,768]{1,0:T(8,128)(2,1)}, bf16[2048,1536]{1,0:T(8,128)(2,1)}, f32[2048,1]{1,0:T(8,128)S(1)}, bf16[2048,2048]{1,0:T(8,128)(2,1)}, bf16[2048,2048]{1,0:T(8,128)(2,1)}) custom-call(s32[8]{0:T(128)S(1)} %iota_xor_fusion.ids_ref, bf16[8,256,2048]{2,1,0:T(8,128)(2,1)} %bitcast.146, bf16[8,256,2048]{2,1,0:T(8,128)(2,1)} %bitcast.143, ...), custom_call_target="tpu_custom_call" | custom-call | flops 927712935936 | bytes 58720256 | tf_op jit(solution)/shard_map/pallas_call | solution.py:934
  502.8 51.7 %shard_map.278 = (bf16[2048,768]{1,0:T(8,128)(2,1)}, bf16[2048,1536]{1,0:T(8,128)(2,1)}, f32[2048,1]{1,0:T(8,128)S(1)}, bf16[2048,2048]{1,0:T(8,128)(2,1)}, bf16[2048,2048]{1,0:T(8,128)(2,1)}) custom-call(s32[8]{0:T(128)S(1)} %broadcast_add_fusion.ids_ref, bf16[8,256,2048]{2,1,0:T(8,128)(2,1)} %collective-permute-done.rows_ref.refs_8_, ...), custom_call_target="tpu_custom_call" | custom-call | flops 927712935936 | bytes 58720256 | tf_op jit(solution)/shard_map/pallas_call | solution.py:934
  555.5 125.1 %shard_map.279 = (f32[256,2048]{1,0:T(8,128)}, f32[16,1,256]{2,1,0:T(1,128)}, bf16[768,2048]{1,0:T(8,128)(2,1)}, bf16[2048,1536]{1,0:T(8,128)(2,1)}, bf16[4,96,2048]{2,1,0:T(8,128)(2,1)}) custom-call(bf16[2,2,2,256,2048]{4,3,2,1,0:T(8,128)(2,1)} %bitcast.148, bf16[2,2,2,256,2048]{4,3,2,1,0:T(8,128)(2,1)} %bitcast.149, f32[16,1,256]{2,1,0:T(1,128)} %bitcast.181, ...), custom_call_target="tpu_custom_call" | custom-call | tf_op jit(solution)/shard_map/pallas_call | solution.py:829
  682.0 1.5 convolution_convert_fusion.1
  684.7 3.7 multiply_reduce_fusion
  688.5 2.4 fusion.25
  690.9 3.4 collective-permute-done.2
  694.3 130.2 %shard_map.280 = (bf16[2,2,2,256,2048]{4,3,2,1,0:T(8,128)(2,1)}, f32[512,2048]{1,0:T(8,128)}, bf16[2,1024,512]{2,1,0:T(8,128)(2,1)}, bf16[2,1024,512]{2,1,0:T(8,...) custom-call(bf16[256,2048]{1,0:T(8,128)(2,1)} %get-tuple-element.146.refs_0_, ...), custom_call_target="tpu_custom_call" | custom-call | tf_op jit(solution)/shard_map/pallas_call | solution.py:829
  824.4 3.8 convert_element_type.64
  828.3 195.4 %shard_map.281 = (bf16[8,2,48,2048]{3,2,1,0:T(8,128)(2,1)}, bf16[8,2,128,1536]{3,2,1,0:T(8,128)(2,1)}, f32[256,2048]{1,0:T(8,128)}, bf16[4,2,128,768]{3,2,1,0:T(...) custom-call(bf16[8,48,2048]{2,1,0:T(8,128)(2,1)} %bitcast.173, ...), custom_call_target="tpu_custom_call" | custom-call | tf_op jit(solution)/shard_map/pallas_call | solution.py:829
  1026.0 7.7 shard_map.283
  1033.7 5.2 shard_map.284
  1039.6 3.9 shard_map.282
  1043.5 1.6 bitcast_convert_fusion
  1045.8 5.7 fusion.2
  (185 shorter events, 28.1 us)
Async XLA Ops:
  7.2 441.6 %all-gather.5.cloned.1.call-start = ((), (), s32[]{:S(2)}) async-start(), calls=%async_computation.2 | async-start | bytes 4718592 | tf_op jit(solution)/shard_map/all_gather | solution.py:1317
  13.5 218.5 %copy-start.50 = (f32[256]{0:T(256)}, f32[256]{0:T(256)S(1)}, u32[]{:S(2)}) copy-start(f32[256]{0:T(256)S(1)} %fusion.3) | copy-start | bytes 3076
  13.5 218.5 %copy-start.48 = (f32[256]{0:T(256)}, f32[256]{0:T(256)S(1)}, u32[]{:S(2)}) copy-start(f32[256]{0:T(256)S(1)} %fusion.23) | copy-start | bytes 3076
  232.1 216.7 %all-gather.7.cloned.1.call-start = ((), (), s32[]{:S(2)}) async-start(), calls=%async_computation.3 | async-start | bytes 4718592 | tf_op jit(solution)/shard_map/all_gather | solution.py:1317
  232.9 595.4 %reduce-scatter.2.cloned.1.call-start = ((), (), s32[]{:S(2)}) async-start(), calls=%async_computation.1 | async-start | bytes 9437184 | tf_op jit(solution)/shard_map/reduce_scatter | solution.py:1427
  232.9 19.1 %copy-start.9 = (s32[2,1,1024]{2,1,0:T(1,128)}, s32[2,1,1024]{2,1,0:T(1,128)S(1)}, u32[]{:S(2)}) copy-start(s32[2,1,1024]{2,1,0:T(1,128)S(1)} %get-tuple-element.159.q_place.refs_6_) | copy-start | bytes 24580
  233.0 19.1 %copy-start.10 = (s32[2,1,1024]{2,1,0:T(1,128)}, s32[2,1,1024]{2,1,0:T(1,128)S(1)}, u32[]{:S(2)}) copy-start(s32[2,1,1024]{2,1,0:T(1,128)S(1)} %get-tuple-element.156.q_segment.refs_7_) | copy-start | bytes 24580
  250.8 430.0 %copy-start.4 = (bf16[2048,128]{1,0:T(8,128)(2,1)}, bf16[2048,128]{1,0:T(8,128)(2,1)S(1)}, u32[]{:S(2)}) copy-start(bf16[2048,128]{1,0:T(8,128)(2,1)S(1)} %get-tuple-element.69) | copy-start | bytes 1572868
  251.7 32.1 %copy-start.2 = (s32[2,1024,1]{2,1,0:T(8,128)}, s32[2,1024,1]{2,1,0:T(8,128)S(1)}, u32[]{:S(2)}) copy-start(s32[2,1024,1]{2,1,0:T(8,128)S(1)} %copy.91.k_place.refs_4_) | copy-start | bytes 24580
  252.0 31.8 %copy-start.3 = (s32[2,1024,1]{2,1,0:T(8,128)}, s32[2,1024,1]{2,1,0:T(8,128)S(1)}, u32[]{:S(2)}) copy-start(s32[2,1024,1]{2,1,0:T(8,128)S(1)} %copy.92.k_segment.refs_5_) | copy-start | bytes 24580
  252.1 31.8 %copy-start.24 = (bf16[2,2,128,2048]{3,2,1,0:T(8,128)(2,1)S(1)}, bf16[2,2,128,2048]{3,2,1,0:T(8,128)(2,1)}, u32[]{:S(2)}) copy-start(bf16[2,2,128,2048]{3,2,1,0:T(8,128)(2,1)} %get-tuple-element.72) | copy-start | bytes 6291460
  283.8 6.9 copy-start.5
  283.8 6.9 copy-start.11
  290.7 48.4 %copy-start.54 = (s32[1,256,8]{1,2,0:T(8,128)S(1)}, s32[1,256,8]{1,2,0:T(8,128)}, u32[]{:S(2)}) copy-start(s32[1,256,8]{1,2,0:T(8,128)} %param.20) | copy-start | bytes 24580
  290.7 48.5 %copy-start.18 = (bf16[1,256,2048]{2,1,0:T(8,128)(2,1)S(1)}, bf16[1,256,2048]{2,1,0:T(8,128)(2,1)}, u32[]{:S(2)}) copy-start(bf16[1,256,2048]{2,1,0:T(8,128)(2,1)} %param.17) | copy-start | bytes 3145732
  343.7 103.8 %copy-start.45 = (f32[256]{0:T(256)}, f32[256]{0:T(256)S(1)}, u32[]{:S(2)}) copy-start(f32[256]{0:T(256)S(1)} %fusion.21) | copy-start | bytes 3076
  440.7 62.1 %collective-permute-start = (bf16[8,256,2048]{2,1,0:T(8,128)(2,1)}, bf16[8,256,2048]{2,1,0:T(8,128)(2,1)}, u32[]{:S(2)}, u32[]{:S(2)}) collective-permute-start(bf16[8,256,2048]{2,1,0:T(8,128)(2,1)} %bitcast.145), channel_id=1, source_target_pairs={{0,4},{4,0},{1,5},{5,1},{2,6},{6,2},{3,7},{7,3},{8,12},{12,8},{9,1... | collective-permute-start | bytes 25165832 | tf_op jit(solution)/shard_map/ppermute | solution.py:1377
  441.1 61.7 %collective-permute-start.1 = (bf16[8,256,2048]{2,1,0:T(8,128)(2,1)}, bf16[8,256,2048]{2,1,0:T(8,128)(2,1)}, u32[]{:S(2)}, u32[]{:S(2)}) collective-permute-start(bf16[8,256,2048]{2,1,0:T(8,128)(2,1)} %bitcast.142), channel_id=1, source_target_pairs={{0,4},{4,0},{1,5},{5,1},{2,6},{6,2},{3,7},{7,3},{8,12},{12,8},{9,1... | collective-permute-start | bytes 25165832 | tf_op jit(solution)/shard_map/ppermute | solution.py:1307
  502.8 52.0 %copy-start.39 = (f32[2048]{0:T(1024)S(1)}, f32[2048]{0:T(1024)}, u32[]{:S(2)}) copy-start(f32[2048]{0:T(1024)} %reduce.1) | copy-start | bytes 24580
  680.7 13.6 %collective-permute-start.2 = (bf16[2048,2048]{1,0:T(8,128)(2,1)}, bf16[2048,2048]{1,0:T(8,128)(2,1)}, u32[]{:S(2)}, u32[]{:S(2)}) collective-permute-start(bf16[2048,2048]{1,0:T(8,128)(2,1)} %get-tuple-element.93), channel_id=1, source_target_pairs={{0,4},{4,0},{1,5},{5,1},{2,6},{6,2},{3,7},{7,3},{8,12},{12,8},{9,1... | collective-permute-start | bytes 25165832 | tf_op jit(solution)/shard_map/ppermute | solution.py:1392
  1039.5 5.6 copy-start.38
  1039.5 6.3 copy-start.16
  1039.6 6.3 copy-start.49
  1045.8 5.7 copy-start.1
  (40 other events, 103.4 us)
Sparse Core Ops, SparseCore 0:
  232.2 77.8 all-gather.4
  311.7 78.6 all-gather.6
  680.8 143.8 reduce-scatter.1

commit v7 on v6

--- a/solution.py
+++ b/solution.py
@@ -1389,7 +1389,6 @@
         ids = ids + zero_of(sides[0][2]).astype(jnp.int32)
     hiddens, d_ins, d_gate_parts, made_parts, back_parts = zip(*sides)
     half_shape = (2,) * len(turn) + (count, model_width)
-    far_made = lax.ppermute(made_parts[1], core[0], SWAP)
     far_parts = 1 << len(far_axes)
     straight = parts_near * rows_d == TILE
     d_gates = jnp.stack(d_gate_parts).reshape(experts, 1, count)
@@ -1441,7 +1440,7 @@
 
     made_axes = turn[: len(turn) - len(near_axes)]
     made_shape = (2,) * len(made_axes) + (parts_near * count, model_width)
-    made = (made_parts[0].reshape(made_shape), far_made.reshape(made_shape))
+    made = [part.reshape(made_shape) for part in made_parts]
     made_spans = [(lo * parts_near, hi * parts_near, order) for lo, hi, order in plane_parts]
     branch_flow = Gather(plane_axes, d_resid_one.astype(low), core_last(plane_parts))
     planes = 1 << len(plane_axes)
@@ -1461,12 +1460,12 @@
         5,
         [
             branch_flow,
-            ReduceBoth(made_axes, *made, made_spans, hold=True),
+            ReduceBoth(made_axes, *made, made_spans, core, True),
             branch_task,
             behind_task,
             out_task,
         ],
-        (0,) * (len(plane_axes) - 1) + (1, 0, -1) + (-2,) * groups + (1, -3, 1),
+        (0, 1) + (0,) * (len(plane_axes) - 2) + (1, 0, -1) + (-2,) * groups + (1, -3, 1),
     )
     heads_back = HeadsBack(
         heads,

time: 1070 us -> 1070 us (level)
  transfers between devices with their start and end apart: 6 -> 5, of which waited for: 1 -> 1; matrix products, arithmetic and copies ran while one was open for 3% -> 3% of each run, Pallas kernels for 35% -> 35%
where the time goes in v7:
time: 1070 us; the launch traced here: 1060 us
  Pallas kernels  979 us (91%)
  local copies, waits for them, and re-layouts  25 us (2%)
  other arithmetic  23.3 us (2%)
  between operations  15.6 us (1%)
    pallas_call x6, Pallas kernels, transfer(): pl.pallas_call(functools.partial(flow_kernel, flows, plan), out_shape=sha...  812 us
    pallas_call x2, Pallas kernels, expert_rows(): pl.pallas_call(functools.partial(expert_kernel, near), grid_spec=pltpu.Pr...  104 us
    pallas_call x1, Pallas kernels, attention_call(): pl.pallas_call(functools.partial(kernel, scale), grid=(seqs, length // ti...  31.7 us
  transfers between devices with their start and end apart: 5, of which 1 were waited for; matrix products, arithmetic and copies ran while one was open for 3% of the time, Pallas kernels for 35%

profile of v7, /device:TPU:0, one launch (start us, length us, event | category | flops | bytes accessed | tf_op | source)
XLA Modules:
  0.0 1055.8 jit_solution(8052227050813194895)
XLA Ops:
  7.2 1.9 reshape.218
  17.1 214.9 %shard_map.272 = (bf16[2,2,2,256,2048]{4,3,2,1,0:T(8,128)(2,1)}, bf16[4,2,2,128,768]{4,3,2,1,0:T(8,128)(2,1)}, bf16[2,2,2,256,2048]{4,3,2,1,0:T(8,128)(2,1)}, bf...) custom-call(bf16[256,2048]{1,0:T(8,128)(2,1)} %fusion.5.refs_0_, ...), custom_call_target="tpu_custom_call" | custom-call | tf_op jit(solution)/shard_map/pallas_call | solution.py:829
  233.4 15.5 %shard_map.273 = (f32[2048,640]{1,0:T(8,128)}, bf16[2048,512]{1,0:T(8,128)(2,1)}, bf16[2048,128]{1,0:T(8,128)(2,1)S(1)}, bf16[2048,128]{1,0:T(8,128)(2,1)S(1)}, ...) custom-call(bf16[2048,2048]{1,0:T(8,128)(2,1)} %bitcast.137, bf16[2048,768]{1,0:T(8,128)(2,1)} %bitcast.140, ...), custom_call_target="tpu_custom_call" | custom-call | tf_op jit(solution)/shard_map/pallas_call | solution.py:1095
  252.1 31.7 %shard_map.274 = (bf16[2,1024,512]{2,1,0:T(8,128)(2,1)S(1)}, f32[2,4,1,1024]{3,2,1,0:T(1,128)S(1)}) custom-call(s32[2,1024,1]{2,1,0:T(8,128)S(1)} %copy.91.k_place.refs_4_, s32[2,1024,1]{2,1,0:T(8,128)S(1)} %copy.92.k_segment.refs_5_, s32[2,1,1024]{2,1,0:T(1,128)S(1)} %get-tuple-element.159.q_place.refs_6_, ...), custom_call_target="tpu_custom_call" | custom-call | tf_op jit(solution)/shard_map/pallas_call | solution.py:1181
  283.9 6.8 convolution_convert_fusion
  290.7 48.4 %shard_map.275 = f32[256,2048]{1,0:T(8,128)} custom-call(bf16[2,2,2,256,2048]{4,3,2,1,0:T(8,128)(2,1)} %bitcast.151), custom_call_target="tpu_custom_call" | custom-call | tf_op jit(solution)/shard_map/pallas_call | solution.py:829
  339.2 2.0 multiply_reduce_fusion.2
  344.3 96.4 %shard_map.276 = (bf16[2,2,2,256,2048]{4,3,2,1,0:T(8,128)(2,1)}, f32[2,2,2,2,16,256]{5,4,3,2,1,0:T(8,128)}) custom-call(bf16[256,2048]{1,0:T(8,128)(2,1)} %copy-done.20, f32[16,256]{1,0:T(8,128)} %fusion.19.refs_1_), custom_call_target="tpu_custom_call" | custom-call | tf_op jit(solution)/shard_map/pallas_call | solution.py:829
  442.1 1.3 copy.95.gate_ref
  443.5 4.0 copy.106
  447.4 1.4 copy.96.gate_ref
  448.8 51.9 %shard_map.277 = (bf16[2048,768]{1,0:T(8,128)(2,1)}, bf16[2048,1536]{1,0:T(8,128)(2,1)}, f32[2048,1]{1,0:T(8,128)S(1)}, bf16[2048,2048]{1,0:T(8,128)(2,1)}, bf16[2048,2048]{1,0:T(8,128)(2,1)}) custom-call(s32[8]{0:T(128)S(1)} %iota_xor_fusion.ids_ref, bf16[8,256,2048]{2,1,0:T(8,128)(2,1)} %bitcast.146, bf16[8,256,2048]{2,1,0:T(8,128)(2,1)} %bitcast.143, ...), custom_call_target="tpu_custom_call" | custom-call | flops 927712935936 | bytes 58720256 | tf_op jit(solution)/shard_map/pallas_call | solution.py:934
  502.8 51.7 %shard_map.278 = (bf16[2048,768]{1,0:T(8,128)(2,1)}, bf16[2048,1536]{1,0:T(8,128)(2,1)}, f32[2048,1]{1,0:T(8,128)S(1)}, bf16[2048,2048]{1,0:T(8,128)(2,1)}, bf16[2048,2048]{1,0:T(8,128)(2,1)}) custom-call(s32[8]{0:T(128)S(1)} %broadcast_add_fusion.ids_ref, bf16[8,256,2048]{2,1,0:T(8,128)(2,1)} %collective-permute-done.rows_ref.refs_8_, ...), custom_call_target="tpu_custom_call" | custom-call | flops 927712935936 | bytes 58720256 | tf_op jit(solution)/shard_map/pallas_call | solution.py:934
  555.5 125.1 %shard_map.279 = (f32[256,2048]{1,0:T(8,128)}, f32[16,1,256]{2,1,0:T(1,128)}, bf16[768,2048]{1,0:T(8,128)(2,1)}, bf16[2048,1536]{1,0:T(8,128)(2,1)}, bf16[4,96,2048]{2,1,0:T(8,128)(2,1)}) custom-call(bf16[2,2,2,256,2048]{4,3,2,1,0:T(8,128)(2,1)} %bitcast.148, bf16[2,2,2,256,2048]{4,3,2,1,0:T(8,128)(2,1)} %bitcast.149, f32[16,1,256]{2,1,0:T(1,128)} %bitcast.182, ...), custom_call_target="tpu_custom_call" | custom-call | tf_op jit(solution)/shard_map/pallas_call | solution.py:829
  682.5 3.2 multiply_reduce_fusion
  685.8 2.4 fusion.25
  688.2 130.6 %shard_map.280 = (bf16[2,2,2,256,2048]{4,3,2,1,0:T(8,128)(2,1)}, f32[512,2048]{1,0:T(8,128)}, bf16[2,1024,512]{2,1,0:T(8,128)(2,1)}, bf16[2,1024,512]{2,1,0:T(8,...) custom-call(bf16[256,2048]{1,0:T(8,128)(2,1)} %get-tuple-element.146.refs_0_, ...), custom_call_target="tpu_custom_call" | custom-call | tf_op jit(solution)/shard_map/pallas_call | solution.py:829
  818.8 3.9 convert_element_type.64
  824.7 196.3 %shard_map.281 = (bf16[8,2,48,2048]{3,2,1,0:T(8,128)(2,1)}, bf16[8,2,128,1536]{3,2,1,0:T(8,128)(2,1)}, f32[256,2048]{1,0:T(8,128)}, bf16[4,2,128,768]{3,2,1,0:T(...) custom-call(bf16[8,48,2048]{2,1,0:T(8,128)(2,1)} %bitcast.174, ...), custom_call_target="tpu_custom_call" | custom-call | tf_op jit(solution)/shard_map/pallas_call | solution.py:829
  1023.3 7.7 shard_map.283
  1031.0 5.2 shard_map.284
  1036.9 3.9 shard_map.282
  1040.8 1.6 bitcast_convert_fusion
  1043.1 5.7 fusion.2
  (185 shorter events, 26.8 us)
Async XLA Ops:
  7.2 441.6 %all-gather.5.cloned.1.call-start = ((), (), s32[]{:S(2)}) async-start(), calls=%async_computation.2 | async-start | bytes 4718592 | tf_op jit(solution)/shard_map/all_gather | solution.py:1317
  13.5 218.5 %copy-start.51 = (f32[256]{0:T(256)}, f32[256]{0:T(256)S(1)}, u32[]{:S(2)}) copy-start(f32[256]{0:T(256)S(1)} %fusion.3) | copy-start | bytes 3076
  13.5 218.5 %copy-start.49 = (f32[256]{0:T(256)}, f32[256]{0:T(256)S(1)}, u32[]{:S(2)}) copy-start(f32[256]{0:T(256)S(1)} %fusion.23) | copy-start | bytes 3076
  232.1 216.7 %all-gather.7.cloned.1.call-start = ((), (), s32[]{:S(2)}) async-start(), calls=%async_computation.3 | async-start | bytes 4718592 | tf_op jit(solution)/shard_map/all_gather | solution.py:1317
  232.9 591.9 %reduce-scatter.2.cloned.1.call-start = ((), (), s32[]{:S(2)}) async-start(), calls=%async_computation.1 | async-start | bytes 9437184 | tf_op jit(solution)/shard_map/reduce_scatter | solution.py:1426
  232.9 19.1 %copy-start.9 = (s32[2,1,1024]{2,1,0:T(1,128)}, s32[2,1,1024]{2,1,0:T(1,128)S(1)}, u32[]{:S(2)}) copy-start(s32[2,1,1024]{2,1,0:T(1,128)S(1)} %get-tuple-element.159.q_place.refs_6_) | copy-start | bytes 24580
  233.0 19.1 %copy-start.10 = (s32[2,1,1024]{2,1,0:T(1,128)}, s32[2,1,1024]{2,1,0:T(1,128)S(1)}, u32[]{:S(2)}) copy-start(s32[2,1,1024]{2,1,0:T(1,128)S(1)} %get-tuple-element.156.q_segment.refs_7_) | copy-start | bytes 24580
  250.8 429.9 %copy-start.4 = (bf16[2048,128]{1,0:T(8,128)(2,1)}, bf16[2048,128]{1,0:T(8,128)(2,1)S(1)}, u32[]{:S(2)}) copy-start(bf16[2048,128]{1,0:T(8,128)(2,1)S(1)} %get-tuple-element.69) | copy-start | bytes 1572868
  251.7 32.1 %copy-start.2 = (s32[2,1024,1]{2,1,0:T(8,128)}, s32[2,1024,1]{2,1,0:T(8,128)S(1)}, u32[]{:S(2)}) copy-start(s32[2,1024,1]{2,1,0:T(8,128)S(1)} %copy.91.k_place.refs_4_) | copy-start | bytes 24580
  252.0 31.8 %copy-start.3 = (s32[2,1024,1]{2,1,0:T(8,128)}, s32[2,1024,1]{2,1,0:T(8,128)S(1)}, u32[]{:S(2)}) copy-start(s32[2,1024,1]{2,1,0:T(8,128)S(1)} %copy.92.k_segment.refs_5_) | copy-start | bytes 24580
  252.1 31.8 %copy-start.25 = (bf16[2,2,128,2048]{3,2,1,0:T(8,128)(2,1)S(1)}, bf16[2,2,128,2048]{3,2,1,0:T(8,128)(2,1)}, u32[]{:S(2)}) copy-start(bf16[2,2,128,2048]{3,2,1,0:T(8,128)(2,1)} %get-tuple-element.72) | copy-start | bytes 6291460
  283.8 6.9 copy-start.5
  283.8 6.9 copy-start.11
  290.7 48.4 %copy-start.55 = (s32[1,256,8]{1,2,0:T(8,128)S(1)}, s32[1,256,8]{1,2,0:T(8,128)}, u32[]{:S(2)}) copy-start(s32[1,256,8]{1,2,0:T(8,128)} %param.20) | copy-start | bytes 24580
  290.7 48.5 %copy-start.18 = (bf16[1,256,2048]{2,1,0:T(8,128)(2,1)S(1)}, bf16[1,256,2048]{2,1,0:T(8,128)(2,1)}, u32[]{:S(2)}) copy-start(bf16[1,256,2048]{2,1,0:T(8,128)(2,1)} %param.17) | copy-start | bytes 3145732
  343.7 103.8 %copy-start.46 = (f32[256]{0:T(256)}, f32[256]{0:T(256)S(1)}, u32[]{:S(2)}) copy-start(f32[256]{0:T(256)S(1)} %fusion.21) | copy-start | bytes 3076
  440.7 62.1 %collective-permute-start = (bf16[8,256,2048]{2,1,0:T(8,128)(2,1)}, bf16[8,256,2048]{2,1,0:T(8,128)(2,1)}, u32[]{:S(2)}, u32[]{:S(2)}) collective-permute-start(bf16[8,256,2048]{2,1,0:T(8,128)(2,1)} %bitcast.145), channel_id=1, source_target_pairs={{0,4},{4,0},{1,5},{5,1},{2,6},{6,2},{3,7},{7,3},{8,12},{12,8},{9,1... | collective-permute-start | bytes 25165832 | tf_op jit(solution)/shard_map/ppermute | solution.py:1377
  441.1 61.7 %collective-permute-start.1 = (bf16[8,256,2048]{2,1,0:T(8,128)(2,1)}, bf16[8,256,2048]{2,1,0:T(8,128)(2,1)}, u32[]{:S(2)}, u32[]{:S(2)}) collective-permute-start(bf16[8,256,2048]{2,1,0:T(8,128)(2,1)} %bitcast.142), channel_id=1, source_target_pairs={{0,4},{4,0},{1,5},{5,1},{2,6},{6,2},{3,7},{7,3},{8,12},{12,8},{9,1... | collective-permute-start | bytes 25165832 | tf_op jit(solution)/shard_map/ppermute | solution.py:1307
  502.8 52.0 %copy-start.40 = (f32[2048]{0:T(1024)S(1)}, f32[2048]{0:T(1024)}, u32[]{:S(2)}) copy-start(f32[2048]{0:T(1024)} %reduce.1) | copy-start | bytes 24580
  1031.0 5.2 copy-start.36
  1036.9 5.6 copy-start.39
  1036.9 6.3 copy-start.16
  1036.9 6.3 copy-start.50
  1043.1 5.7 copy-start.1
  (40 other events, 91.4 us)
Sparse Core Ops, SparseCore 0:
  232.2 77.8 all-gather.4
  311.7 78.6 all-gather.6
  680.8 143.8 reduce-scatter.1
